TPU v7x, 32 devices: a whole 2x2x4 slice. The times are simulated.
32 devices in a mesh: grp: 2 (over y), wide: 4 (over z), freq: 2 (over x), pol: 2 (over core).
Axes of the slice: x: 2, y: 2, z: 4, core: 2. Of those that a mesh axis runs over, the one named last changes fastest.
Arguments:
- visibilities: float32 [2, 4096, 8, 384], P(None, ('grp', 'wide'), 'freq', 'pol'), parts along dimension 1, may hold values from -6 to 6
- beams: bfloat16 [8, 8, 2, 384, 768], P('wide', 'freq', None, 'pol'), may hold values from -0.21875 to 0.21875
- spectra: float32 [8, 5, 768], P('freq'), may hold values from 0.1 to 1
- m_orders: int32 [8], replicated, may hold values from 0 to 1023, as said below
Outputs:
- msdata: float32 [16, 8, 2, 384], P(('grp', 'wide'), 'freq', None, 'pol'), parts along dimension 0
- weighted: float32 [16, 8, 2, 384], P(('grp', 'wide'), 'freq', None, 'pol'), parts along dimension 0
There are 2 independent parts, one for each index of `grp`. A program takes and returns all parts, laid end to end along the dimension named above; an argument that names none is the same for every part. Nothing has to cross between parts.
Inputs may be any that keep to these rules, and one draw needn't show every extreme that they name: `m_orders`: the m-orders are distinct, and 0 and 1023 are always among them.
All inputs are finite; a program needn't handle non-finite values.
Results may differ from a plain program's by a relative error of at most 0.0039.
Values sent between devices are 32-bit elements; how exact they have to be, the bound alone decides.
No kernel may reach another device: no remote copies, remote signals or barrier semaphores. Data moves between devices by JAX's collectives and lax.ppermute only.
A program may use at most 64 MiB of HBM per device.

v0:
```python
import math

import jax
import jax.numpy as jnp
from jax import lax
from jax.sharding import PartitionSpec as P

TIME = 2048
BAND = 4


def shifted(array, axis, by):
    size = lax.axis_size(axis)
    return lax.ppermute(array, axis, [(i, (i + by) % size) for i in range(size)])


def fourier_tables(orders, times):
    product = orders[:, None] * times[None, :] % TIME
    angle = product.astype(jnp.float32) * (2.0 * math.pi / TIME)
    factor = 1.0 / math.sqrt(TIME)
    return (jnp.cos(angle) * factor, jnp.sin(angle) * factor)


def transform(orders, times, block):
    cosine, sine_tab = fourier_tables(orders, times)
    count = times.shape[0]
    data_real = block[0].reshape(count, -1)
    data_imag = block[1].reshape(count, -1)
    exact_mode = lax.Precision.HIGHEST
    part_real = jnp.dot(
        cosine, data_real, precision=exact_mode, preferred_element_type=jnp.float32
    ) + jnp.dot(sine_tab, data_imag, precision=exact_mode, preferred_element_type=jnp.float32)
    part_imag = jnp.dot(
        cosine, data_imag, precision=exact_mode, preferred_element_type=jnp.float32
    ) - jnp.dot(sine_tab, data_real, precision=exact_mode, preferred_element_type=jnp.float32)
    shape_out = (orders.shape[0], block.shape[2], block.shape[3])
    return jnp.stack([part_real.reshape(shape_out), part_imag.reshape(shape_out)], axis=2)


def shards(visibilities, beams, spectra, m_orders):
    local_blocks = beams.shape[1]
    local_times = visibilities.shape[1]
    first_time = lax.axis_index("wide") * local_times
    times = first_time + jnp.arange(local_times, dtype=jnp.int32)
    msdata = lax.psum_scatter(
        transform(m_orders, times, visibilities), "wide", scatter_dimension=0, tiled=True
    )
    rounded = msdata.astype(jnp.bfloat16)
    round_real = rounded[:, :, 0]
    round_imag = rounded[:, :, 1]
    stacked = jnp.stack(
        [jnp.stack([round_real, round_imag], 2), jnp.stack([round_imag, -round_real], 2)], 2
    )
    partial_proj = lax.dot_general(
        stacked, beams, (((3, 4), (2, 3)), ((0, 1), (0, 1))), preferred_element_type=jnp.float32
    )
    projected = lax.psum(partial_proj, "pol")
    following = shifted(projected, "freq", -1)
    extended = jnp.concatenate([projected, following], axis=1)
    mixed = spectra[None, :, 0, None, :] * projected
    for offset in range(1, BAND + 1):
        mixed = (
            mixed + spectra[None, :, offset, None, :] * extended[:, offset : offset + local_blocks]
        )
    coupled = mixed.astype(jnp.bfloat16)
    cop_real = coupled[:, :, 0]
    cop_imag = coupled[:, :, 1]
    paired = jnp.stack([jnp.stack([cop_real, -cop_imag], 2), jnp.stack([cop_imag, cop_real], 2)], 2)
    weighted = lax.dot_general(
        paired, beams, (((3, 4), (2, 4)), ((0, 1), (0, 1))), preferred_element_type=jnp.float32
    )
    return (msdata, weighted)


def solution(mesh):
    return jax.shard_map(
        shards,
        mesh=mesh,
        in_specs=(
            P(None, ("grp", "wide"), "freq", "pol"),
            P("wide", "freq", None, "pol", None),
            P("freq", None, None),
            P(),
        ),
        out_specs=(
            P(("grp", "wide"), "freq", None, "pol"),
            P(("grp", "wide"), "freq", None, "pol"),
        ),
        check_vma=False,
    )
```

profile of v0, /device:TPU:0, one launch (start us, length us, event | category | flops | bytes accessed | tf_op | source)
XLA Modules:
  0.0 47.3 jit_solution(1263961565827750037)
XLA Ops:
  0.6 0.0 copy-start.1
  0.7 2.2 %fusion.44 = (f32[1,512,4,192]{1,3,2,0:T(8,128)S(1)}, f32[1,512,4,192]{1,3,2,0:T(8,128)S(1)}) fusion(f32[2,512,4,192]{1,3,2,0:T(8,128)} %param.4), kind=kLoop, calls=%fused_computation.70 | loop fusion | bytes 6291456 | tf_op jit(solution)/shard_map/slice | solution.py:27
  2.9 0.0 copy-done.1
  2.9 1.4 %fusion.13 = f32[8,768]{1,0:T(8,128)S(1)} fusion(f32[512,768]{0,1:T(8,128)S(1)} %bitcast.34, s32[512]{0:T(512)S(1)} %iota_add_fusion, s32[8]{0:T(128)S(1)} %copy-done.1), kind=kOutput, calls=%fused_computation.31 | convolution fusion | flops 37810176 | bytes 1599520 | tf_op jit(solution)/shard_map/dot_general | solution.py:30
  4.3 1.5 %fusion.12 = f32[8,768]{1,0:T(8,128)S(1)} fusion(f32[512,768]{0,1:T(8,128)S(1)} %bitcast.36, s32[512]{0:T(512)S(1)} %iota_add_fusion, s32[8]{0:T(128)S(1)} %copy-done.1), kind=kOutput, calls=%fused_computation.30 | convolution fusion | flops 37810176 | bytes 1599520 | tf_op jit(solution)/shard_map/dot_general | solution.py:33
  5.8 0.0 copy-start.2
  5.8 1.5 %convolution_add_fusion = f32[8,768]{1,0:T(8,128)S(1)} fusion(f32[8,768]{1,0:T(8,128)S(1)} %fusion.13, f32[512,768]{0,1:T(8,128)S(1)} %bitcast.37, s32[512]{0:T(512)S(1)} %iota_add_fusion, s32[8]{0:T(128)S(1)} %copy-done.1), kind=kOutput, calls=%fused_computation.2 | convolution fusion | flops 37816320 | bytes 1624096 | tf_op jit(solution)/shard_map/dot_general | solution.py:32
  7.3 0.1 stack_reshape.6
  7.4 1.4 %convolution_subtract_fusion = f32[8,768]{1,0:T(8,128)S(1)} fusion(f32[8,768]{1,0:T(8,128)S(1)} %fusion.12, f32[512,768]{0,1:T(8,128)S(1)} %bitcast.35, s32[512]{0:T(512)S(1)} %iota_add_fusion, s32[8]{0:T(128)S(1)} %copy-done.1), kind=kOutput, calls=%fused_computation.1 | convolution fusion | flops 37816320 | bytes 1624096 | tf_op jit(solution)/shard_map/dot_general | solution.py:35
  8.8 0.1 stack_reshape.7
  9.0 21.5 %all-reduce = f32[8,4,2,192]{3,1,2,0:T(4,128)S(1)} all-reduce(f32[8,4,2,192]{3,1,2,0:T(4,128)S(1)} %pad_maximum_fusion), channel_id=2, replica_groups=mesh['grp'=2,'wide'=4,'freq'=2,'pol'=2] {'wide'}, use_global_device_ids=true, to_apply=%region_0.1.clone | all-reduce | flops 12288 | bytes 98304
  30.5 0.0 copy-done.2
  30.5 0.6 %dynamic-slice = u32[1]{0:T(128)} dynamic-slice(u32[32]{0:T(128)S(1)} %copy-done.2, u32[]{:T(128)S(6)} %add.44), dynamic_slice_sizes={1} | dynamic-slice | bytes 12
  31.9 0.0 copy-start
  31.9 3.1 %convolution_bitcast_fusion = f32[2,4,2,768]{3,2,1,0:T(2,128)S(1)} fusion(bf16[2,4,2,192,768]{4,3,2,1,0:T(8,128)(2,1)} %param.5, bf16[2,4,1,2,192]{4,2,3,1,0:T(2,128)(2,1)S(1)} %copy.24, bf16[2,4,1,2,192]{4,2,3,1,0:T(2,128)(2,1)S(1)} %copy.23), kind=kOutput, calls=%fused_computation | convolution fusion | flops 9461760 | bytes 4780032 | tf_op jit(solution)/shard_map/dot_general | solution.py:54
  35.0 3.5 %psum.7 = f32[2,4,2,768]{3,2,1,0:T(2,128)S(1)} all-reduce(f32[2,4,2,768]{3,2,1,0:T(2,128)S(1)} %convolution_bitcast_fusion), channel_id=1, replica_groups=mesh['grp'=2,'wide'=4,'freq'=2,'pol'=2] {'pol'}, use_global_device_ids=true, to_apply=%region_1.2 | all-reduce | flops 12288 | bytes 98304 | tf_op jit(solution)/shard_map/psum | solution.py:57
  38.5 1.6 %collective-permute-start = (f32[2,4,2,768]{3,2,1,0:T(2,128)S(1)}, f32[2,4,2,768]{3,2,1,0:T(2,128)S(1)}, u32[]{:S(2)}, u32[]{:S(2)}) collective-permute-start(f32[2,4,2,768]{3,2,1,0:T(2,128)S(1)} %psum.7), channel_id=1, source_target_pairs={{0,2},{2,0},{1,3},{3,1},{4,6},{6,4},{5,7},{7,5},{8,10},{10,8},{9,1... | collective-permute-start | bytes 147464 | tf_op jit(solution)/shard_map/ppermute | solution.py:14
  40.1 0.0 copy-done
  40.1 0.6 %copy.26 = f32[2,4,2,192]{3,2,1,0:T(2,128)} copy(f32[2,4,2,192]{3,1,2,0:T(4,128)S(1)} %get-tuple-element.5) | data formatting | bytes 24576
  40.7 2.0 %collective-permute-done = f32[2,4,2,768]{3,2,1,0:T(2,128)S(1)} collective-permute-done((f32[2,4,2,768]{3,2,1,0:T(2,128)S(1)}, f32[2,4,2,768]{3,2,1,0:T(2,128)S(1)}, u32[]{:S(2)}, u32[]{:S(2)}) %collective-permute-start) | collective-permute-done | bytes 49184 | tf_op jit(solution)/shard_map/ppermute | solution.py:14
  42.7 0.1 fusion.5
  42.8 0.1 slice_negate_fusion.1
  42.9 0.1 maximum_bitcast_fusion
  43.0 0.1 pad_maximum_fusion.1
  43.1 4.3 %convolution_bitcast_fusion.1 = f32[2,4,2,192]{3,2,1,0:T(2,128)} fusion(bf16[2,4,2,192,768]{4,3,2,1,0:T(8,128)(2,1)} %param.5, bf16[2,4,2,2,768]{4,3,1,0,2:T(2,128)(2,1)S(1)} %pad_maximum_fusion.1), kind=kOutput, calls=%fused_computation.3 | convolution fusion | flops 9437184 | bytes 4780032 | tf_op jit(solution)/shard_map/dot_general | solution.py:69
  (10 shorter events, 0.1 us)
Async XLA Ops:
  0.6 2.2 %copy-start.1 = (s32[8]{0:T(128)S(1)}, s32[8]{0:T(128)}, u32[]{:S(2)}) copy-start(s32[8]{0:T(128)} %param.7) | copy-start | bytes 100
  5.8 24.7 %copy-start.2 = (u32[32]{0:T(128)S(1)}, u32[32]{0:T(128)}, u32[]{:S(2)}) copy-start(u32[32]{0:T(128)} %constant.29) | copy-start | bytes 388
  31.9 8.2 %copy-start = (f32[4,5,768]{2,0,1:T(4,128)S(1)}, f32[4,5,768]{2,0,1:T(4,128)}, u32[]{:S(2)}) copy-start(f32[4,5,768]{2,0,1:T(4,128)} %param.6) | copy-start | bytes 184324
  38.5 4.2 %collective-permute-start = (f32[2,4,2,768]{3,2,1,0:T(2,128)S(1)}, f32[2,4,2,768]{3,2,1,0:T(2,128)S(1)}, u32[]{:S(2)}, u32[]{:S(2)}) collective-permute-start(f32[2,4,2,768]{3,2,1,0:T(2,128)S(1)} %psum.7), channel_id=1, source_target_pairs={{0,2},{2,0},{1,3},{3,1},{4,6},{6,4},{5,7},{7,5},{8,10},{10,8},{9,1... | collective-permute-start | bytes 147464 | tf_op jit(solution)/shard_map/ppermute | solution.py:14
where the time goes:
time: 47.6 us; the launch traced here: 47.3 us
  blocking collectives  25 us (53%)
  matrix products  13.3 us (28%)
  local copies, waits for them, and re-layouts  3.68 us (8%)
  waiting for transfers between devices  1.96 us (4%)
  starting transfers between devices  1.56 us (3%)
  between operations  1.46 us (3%)
    unnamed x1, blocking collectives  21.5 us
    dot_general x1, matrix products, shards(): lax.dot_general(paired, beams, (((3, 4), (2, 4)), ((0, 1), (0, 1))), pref...  4.27 us
    psum x1, blocking collectives, shards(): projected = lax.psum(partial_proj, 'pol')  3.52 us
    dot_general x1, matrix products, shards(): lax.dot_general(stacked, beams, (((3, 4), (2, 3)), ((0, 1), (0, 1))), pre...  3.14 us
    slice x1, local copies, waits for them, and re-layouts, transform(): data_real = block[0].reshape(count, -1)  2.19 us
    ppermute x1, waiting for transfers between devices, shifted(): lax.ppermute(array, axis, [(i, (i + by) % size) for i in range(size)])  1.96 us
    ppermute x1, starting transfers between devices, shifted(): lax.ppermute(array, axis, [(i, (i + by) % size) for i in range(size)])  1.56 us
    dot_general x1, matrix products, transform(): jnp.dot(cosine, data_imag, precision=exact_mode, preferred_element_type=j...  1.48 us
  transfers between devices with their start and end apart: 1, of which 1 were waited for; matrix products, arithmetic and copies ran while one was open for 1% of the time, Pallas kernels for 0%

commit v1 on v0

v1 whole, which is shorter than its diff:
```python
import math

import jax
import jax.numpy as jnp
from jax import lax
from jax.experimental import pallas as pl
from jax.experimental.pallas import tpu as pltpu
from jax.sharding import PartitionSpec as P

TIME = 2048
BAND = 4
MIB = 1024 * 1024


def tables(order, time):
    step = (order * time) & (TIME - 1)
    quarter = (step + TIME // 8) >> 9
    x = (step - (quarter << 9)).astype(jnp.float32) * (2.0 * math.pi / TIME)
    y = x * x
    sine = x * (1.0 + y * (-1.0 / 6 + y * (1.0 / 120 + y * (-1.0 / 5040 + y * (1.0 / 362880)))))
    cosine = 1.0 + y * (
        -0.5 + y * (1.0 / 24 + y * (-1.0 / 720 + y * (1.0 / 40320 + y * (-1.0 / 3628800))))
    )
    factor = 1.0 / math.sqrt(TIME)
    odd = (quarter & 1) == 1
    cos_sign = jnp.where(((quarter + 1) & 2) == 2, -factor, factor)
    sin_sign = jnp.where((quarter & 2) == 2, -factor, factor)
    return jnp.where(odd, sine, cosine) * cos_sign, jnp.where(odd, cosine, sine) * sin_sign


def split(value):
    high = value.astype(jnp.bfloat16)
    return high, (value - high.astype(jnp.float32)).astype(jnp.bfloat16)


def dot_last(left, right):
    return lax.dot_general(left, right, (((1,), (1,)), ((), ())), preferred_element_type=jnp.float32)


def transform(visibilities, m_orders, size):
    _, blocks, modes, times = visibilities.shape
    total = m_orders.shape[0]
    per = total // size

    def kernel(orders, vis, *rest):
        outs, (held, sems) = rest[:size], rest[size:]
        copies = [
            [pltpu.make_async_copy(vis.at[c, f], held.at[c, f], sems.at[c, f]) for c in range(2)]
            for f in range(blocks)
        ]
        for pair in copies:
            for copy in pair:
                copy.start()
        me = lax.axis_index("wide")
        row = lax.broadcasted_iota(jnp.int32, (total, times), 0)
        order = jnp.zeros((total, times), jnp.int32)
        for s in range(size):
            for i in range(per):
                order = jnp.where(row == s * per + i, orders[partner(me, s, size) * per + i], order)
        time = lax.broadcasted_iota(jnp.int32, (total, times), 1) + me * times
        cosine, sine = tables(order, time)
        lefts = []
        for c in range(2):
            table = jnp.concatenate([cosine, -sine] if c == 0 else [sine, cosine], 0)
            high, low = split(table)
            lefts.append((jnp.concatenate([high, low], 0), high))
        for f in range(blocks):
            acc = None
            for c in range(2):
                copies[f][c].wait()
                high, low = split(held[c, f])
                both = dot_last(lefts[c][0], high)
                term = both[: 2 * total] + both[2 * total :] + dot_last(lefts[c][1], low)
                acc = term if acc is None else acc + term
            for s in range(size):
                for c in range(2):
                    first = c * total + s * per
                    outs[s][f, c * per : (c + 1) * per, :] = acc[first : first + per]

    return pl.pallas_call(
        kernel,
        out_shape=[jax.ShapeDtypeStruct((blocks, 2 * per, modes), jnp.float32)] * size,
        in_specs=[
            pl.BlockSpec(memory_space=pltpu.SMEM),
            pl.BlockSpec(memory_space=pltpu.HBM),
        ],
        out_specs=[pl.BlockSpec(memory_space=pltpu.VMEM)] * size,
        scratch_shapes=[
            pltpu.VMEM((2, blocks, modes, times), jnp.float32),
            pltpu.SemaphoreType.DMA((2, blocks)),
        ],
        compiler_params=pltpu.CompilerParams(vmem_limit_bytes=12 * MIB),
        name="transform",
    )(m_orders, visibilities)


def project(parts, beams):
    per, blocks, _, modes, degrees = beams.shape
    count = len(parts)

    def kernel(*refs):
        pieces, beam, ms_out, proj_out = refs[:count], refs[count], refs[count + 1], refs[count + 2]
        row = lax.broadcasted_iota(jnp.int32, (2 * per, degrees), 0)
        for f in range(blocks):
            total = pieces[0][f]
            for piece in pieces[1:]:
                total = total + piece[f]
            for r in range(per):
                for c in range(2):
                    ms_out[r, f, c : c + 1, :] = total[c * per + r : c * per + r + 1]
            turned = jnp.concatenate([total[per:], -total[:per]], 0).astype(jnp.bfloat16)
            plain = total.astype(jnp.bfloat16)
            acc = None
            for r in range(per):
                term = jnp.dot(plain, beam[r, f, 0], preferred_element_type=jnp.float32)
                term = term + jnp.dot(turned, beam[r, f, 1], preferred_element_type=jnp.float32)
                acc = term if acc is None else jnp.where(row % per == r, term, acc)
            proj_out[f] = acc

    return pl.pallas_call(
        kernel,
        out_shape=[
            jax.ShapeDtypeStruct((per, blocks, 2, modes), jnp.float32),
            jax.ShapeDtypeStruct((blocks, 2 * per, degrees), jnp.float32),
        ],
        in_specs=[pl.BlockSpec(memory_space=pltpu.VMEM)] * (count + 1),
        out_specs=[pl.BlockSpec(memory_space=pltpu.VMEM)] * 2,
        compiler_params=pltpu.CompilerParams(vmem_limit_bytes=12 * MIB),
        name="project",
    )(*parts, beams)


def couple(own, others, spectra, beams):
    per, blocks, _, modes, degrees = beams.shape

    def kernel(own_ref, pol_ref, next_ref, cross_ref, spec, beam, out):
        row = lax.broadcasted_iota(jnp.int32, (2 * per, modes), 0)
        summed = [own_ref[f] + pol_ref[f] for f in range(blocks)]
        summed += [next_ref[f] + cross_ref[f] for f in range(blocks)]
        for f in range(blocks):
            mixed = None
            for d in range(BAND + 1):
                term = spec[f, d : d + 1, :] * summed[f + d]
                mixed = term if mixed is None else mixed + term
            turned = jnp.concatenate([-mixed[per:], mixed[:per]], 0).astype(jnp.bfloat16)
            plain = mixed.astype(jnp.bfloat16)
            acc = None
            for r in range(per):
                term = dot_last(plain, beam[r, f, 0]) + dot_last(turned, beam[r, f, 1])
                acc = term if acc is None else jnp.where(row % per == r, term, acc)
            for r in range(per):
                for c in range(2):
                    out[r, f, c : c + 1, :] = acc[c * per + r : c * per + r + 1]

    return pl.pallas_call(
        kernel,
        out_shape=jax.ShapeDtypeStruct((per, blocks, 2, modes), jnp.float32),
        in_specs=[pl.BlockSpec(memory_space=pltpu.VMEM)] * 6,
        out_specs=pl.BlockSpec(memory_space=pltpu.VMEM),
        compiler_params=pltpu.CompilerParams(vmem_limit_bytes=12 * MIB),
        name="couple",
    )(own, *others, spectra, beams)


def partner(me, step, size):
    return lax.rem(me + step, size)


def shards(visibilities, beams, spectra, m_orders):
    size = lax.axis_size("wide")
    freqs = lax.axis_size("freq")
    pols = lax.axis_size("pol")
    parts = transform(visibilities.transpose(0, 2, 3, 1), m_orders, size)
    arrived = [parts[0]]
    for s in range(1, size):
        arrived.append(lax.ppermute(parts[s], "wide", [(i, (i + s) % size) for i in range(size)]))
    msdata, partial = project(arrived, beams)

    def fetch(freq_step, pol_step):
        pairs = [
            (((f + freq_step) % freqs) * pols + (p + pol_step) % pols, f * pols + p)
            for f in range(freqs)
            for p in range(pols)
        ]
        return lax.ppermute(partial, ("freq", "pol"), pairs)

    others = [fetch(0, 1), fetch(1, 0), fetch(1, 1)]
    return msdata, couple(partial, others, spectra, beams)


def solution(mesh):
    return jax.shard_map(
        shards,
        mesh=mesh,
        in_specs=(
            P(None, ("grp", "wide"), "freq", "pol"),
            P("wide", "freq", None, "pol", None),
            P("freq", None, None),
            P(),
        ),
        out_specs=(
            P(("grp", "wide"), "freq", None, "pol"),
            P(("grp", "wide"), "freq", None, "pol"),
        ),
        check_vma=False,
    )
```

time: 47.6 us -> 27.5 us (0.58)
  blocking collectives: 25 us -> 0 us
  matrix products: 13.3 us -> 0 us
  Pallas kernels: 0 us -> 7.42 us
  starting transfers between devices: 1.56 us -> 8.87 us
  waiting for transfers between devices: 1.96 us -> 5.42 us
  local copies, waits for them, and re-layouts: 3.68 us -> 4.9 us
  between operations: 1.46 us -> 0.66 us
    unnamed x1 -> x0, blocking collectives: 21.5 us -> none
    dot_general x6 -> x0, matrix products: 13.3 us -> none  [the longest x1 4.27 us: shards(): lax.dot_general(paired, beams, (((3, 4), (2, 4)), ((0, 1), (0, 1))), pref...]
    pallas_call x0 -> x3, Pallas kernels: none -> 7.42 us  [the longest x1 4.28 us: transform(): pl.pallas_call(kernel, out_shape=[jax.ShapeDtypeStruct((blocks, 2 * per,...]
    ppermute x1 -> x6, starting transfers between devices: 1.56 us -> 8.87 us  [the longest x3 7.01 us: shards(): lax.ppermute(parts[s], 'wide', [(i, (i + s) % size) for i in range(size)])]
    unnamed x9 -> x11, local copies, waits for them, and re-layouts: 1.22 us -> 4.9 us
    psum x1 -> x0, blocking collectives: 3.52 us -> none  [shards(): projected = lax.psum(partial_proj, 'pol')]
    ppermute x1 -> x6, waiting for transfers between devices: 1.96 us -> 5.42 us  [the longest x3 3.03 us: fetch(): return lax.ppermute(partial, ('freq', 'pol'), pairs)]
    slice x1 -> x0, local copies, waits for them, and re-layouts: 2.19 us -> none  [transform(): data_real = block[0].reshape(count, -1)]
  transfers between devices with their start and end apart: 1 -> 6, of which waited for: 1 -> 4; matrix products, arithmetic and copies ran while one was open for 1% -> 0% of each run, Pallas kernels for 0% -> 0%
where the time goes in v1:
time: 27.5 us; the launch traced here: 27.3 us
  starting transfers between devices  8.87 us (32%)
  Pallas kernels  7.42 us (27%)
  waiting for transfers between devices  5.42 us (20%)
  local copies, waits for them, and re-layouts  4.9 us (18%)
  between operations  0.66 us (2%)
    ppermute x3, starting transfers between devices, shards(): lax.ppermute(parts[s], 'wide', [(i, (i + s) % size) for i in range(size)])  7.01 us
    unnamed x11, local copies, waits for them, and re-layouts  4.9 us
    pallas_call x1, Pallas kernels, transform(): pl.pallas_call(kernel, out_shape=[jax.ShapeDtypeStruct((blocks, 2 * per,...  4.28 us
    ppermute x3, waiting for transfers between devices, fetch(): return lax.ppermute(partial, ('freq', 'pol'), pairs)  3.03 us
    ppermute x3, waiting for transfers between devices, shards(): lax.ppermute(parts[s], 'wide', [(i, (i + s) % size) for i in range(size)])  2.39 us
    pallas_call x1, Pallas kernels, couple(): pl.pallas_call(kernel, out_shape=jax.ShapeDtypeStruct((per, blocks, 2, mo...  1.95 us
    ppermute x3, starting transfers between devices, fetch(): return lax.ppermute(partial, ('freq', 'pol'), pairs)  1.86 us
    pallas_call x1, Pallas kernels, project(): pl.pallas_call(kernel, out_shape=[jax.ShapeDtypeStruct((per, blocks, 2, m...  1.19 us
  transfers between devices with their start and end apart: 6, of which 4 were waited for; matrix products, arithmetic and copies ran while one was open for 0% of the time, Pallas kernels for 0%

profile of v1, /device:TPU:0, one launch (start us, length us, event | category | flops | bytes accessed | tf_op | source)
XLA Modules:
  0.0 27.3 jit_solution(1964154606781490228)
XLA Ops:
  0.6 0.0 copy-start.2
  0.6 1.9 %copy-done.2 = f32[2,512,4,192]{1,3,2,0:T(8,128)S(1)} copy-done((f32[2,512,4,192]{1,3,2,0:T(8,128)S(1)}, f32[2,512,4,192]{1,3,2,0:T(8,128)}, u32[]{:S(2)}) %copy-start.2) | copy-done | bytes 3145752
  2.5 0.0 copy-start.3
  2.5 0.7 %copy-done.3 = s32[8]{0:T(128)S(1)} copy-done((s32[8]{0:T(128)S(1)}, s32[8]{0:T(128)}, u32[]{:S(2)}) %copy-start.3) | copy-done | bytes 56
  3.2 0.0 copy-start.4
  3.2 4.3 %transform.1 = (f32[4,4,192]{2,1,0:T(4,128)S(1)}, f32[4,4,192]{2,1,0:T(4,128)S(1)}, f32[4,4,192]{2,1,0:T(4,128)S(1)}, f32[4,4,192]{2,1,0:T(4,128)S(1)}) custom-call(s32[8]{0:T(128)S(1)} %copy-done.3, f32[2,4,192,512]{3,2,1,0:T(8,128)S(1)} %bitcast.1), custom_call_target="tpu_custom_call" | custom-call | tf_op jit(solution)/shard_map/transform/pallas_call | solution.py:80
  7.5 3.1 %collective-permute-start = (f32[4,4,192]{2,1,0:T(4,128)S(1)}, f32[4,4,192]{2,1,0:T(4,128)S(1)}, u32[]{:S(2)}, u32[]{:S(2)}) collective-permute-start(f32[4,4,192]{2,1,0:T(4,128)S(1)} %get-tuple-element.9), channel_id=1, source_target_pairs={{0,4},{4,8},{8,12},{12,0},{1,5},{5,9},{9,13},{13,1},{2,6},{6,10},{... | collective-permute-start | bytes 36872 | tf_op jit(solution)/shard_map/ppermute | solution.py:176
  10.5 2.6 %collective-permute-start.1 = (f32[4,4,192]{2,1,0:T(4,128)S(1)}, f32[4,4,192]{2,1,0:T(4,128)S(1)}, u32[]{:S(2)}, u32[]{:S(2)}) collective-permute-start(f32[4,4,192]{2,1,0:T(4,128)S(1)} %get-tuple-element.10), channel_id=1, source_target_pairs={{0,8},{4,12},{8,0},{12,4},{1,9},{5,13},{9,1},{13,5},{2,10},{6,14},... | collective-permute-start | bytes 36872 | tf_op jit(solution)/shard_map/ppermute | solution.py:176
  13.1 1.3 %collective-permute-start.2 = (f32[4,4,192]{2,1,0:T(4,128)S(1)}, f32[4,4,192]{2,1,0:T(4,128)S(1)}, u32[]{:S(2)}, u32[]{:S(2)}) collective-permute-start(f32[4,4,192]{2,1,0:T(4,128)S(1)} %get-tuple-element.11), channel_id=1, source_target_pairs={{0,12},{4,0},{8,4},{12,8},{1,13},{5,1},{9,5},{13,9},{2,14},{6,2},{... | collective-permute-start | bytes 36872 | tf_op jit(solution)/shard_map/ppermute | solution.py:176
  14.5 0.0 collective-permute-done.refs_1_
  14.5 0.8 %collective-permute-done.1.refs_2_ = f32[4,4,192]{2,1,0:T(4,128)S(1)} collective-permute-done((f32[4,4,192]{2,1,0:T(4,128)S(1)}, f32[4,4,192]{2,1,0:T(4,128)S(1)}, u32[]{:S(2)}, u32[]{:S(2)}) %collective-permute-start.1) | collective-permute-done | bytes 12320 | tf_op jit(solution)/shard_map/ppermute | solution.py:176
  15.3 1.6 %collective-permute-done.2.refs_3_ = f32[4,4,192]{2,1,0:T(4,128)S(1)} collective-permute-done((f32[4,4,192]{2,1,0:T(4,128)S(1)}, f32[4,4,192]{2,1,0:T(4,128)S(1)}, u32[]{:S(2)}, u32[]{:S(2)}) %collective-permute-start.2) | collective-permute-done | bytes 12320 | tf_op jit(solution)/shard_map/ppermute | solution.py:176
  16.9 0.0 copy-start
  16.9 2.3 %copy-done = bf16[2,4,2,192,768]{4,3,2,1,0:T(8,128)(2,1)S(1)} copy-done((bf16[2,4,2,192,768]{4,3,2,1,0:T(8,128)(2,1)S(1)}, bf16[2,4,2,192,768]{4,3,2,1,0:T(8,128)(2,1)}, u32[]{:S(2)}) %copy-start) | copy-done | bytes 4718616
  19.2 0.0 copy-start.1
  19.2 1.2 %project.1 = (f32[2,4,2,192]{3,2,1,0:T(2,128)}, f32[4,4,768]{2,1,0:T(4,128)S(1)}) custom-call(f32[4,4,192]{2,1,0:T(4,128)S(1)} %get-tuple-element.8.refs_0_, f32[4,4,192]{2,1,0:T(4,128)S(1)} %collective-permute-done.refs_1_, f32[4,4,192]{2,1,0:T(4,128)S(1)} %collective-permute-done.1.refs_2_, f32[4,4,192]{2,1,0:T(4,128)S(1)} %collective-permute-done.2.refs_3_, ...), custom_call_target="tpu_custom_call" | custom-call | tf_op jit(solution)/shard_map/project/pallas_call | solution.py:120
  20.4 0.0 collective-permute-start.5
  20.4 1.5 %collective-permute-start.4 = (f32[4,4,768]{2,1,0:T(4,128)S(1)}, f32[4,4,768]{2,1,0:T(4,128)S(1)}, u32[]{:S(2)}, u32[]{:S(2)}) collective-permute-start(f32[4,4,768]{2,1,0:T(4,128)S(1)} %get-tuple-element.13.own_ref), channel_id=1, source_target_pairs={{2,0},{3,1},{0,2},{1,3},{6,4},{7,5},{4,6},{5,7},{10,8},{11,9},{8,1... | collective-permute-start | bytes 147464 | tf_op jit(solution)/shard_map/ppermute | solution.py:185
  21.9 0.3 %collective-permute-start.3 = (f32[4,4,768]{2,1,0:T(4,128)S(1)}, f32[4,4,768]{2,1,0:T(4,128)S(1)}, u32[]{:S(2)}, u32[]{:S(2)}) collective-permute-start(f32[4,4,768]{2,1,0:T(4,128)S(1)} %get-tuple-element.13.own_ref), channel_id=1, source_target_pairs={{1,0},{0,1},{3,2},{2,3},{5,4},{4,5},{7,6},{6,7},{9,8},{8,9},{11,10... | collective-permute-start | bytes 147464 | tf_op jit(solution)/shard_map/ppermute | solution.py:185
  22.3 0.0 copy-done.4
  22.3 2.1 %collective-permute-done.5.cross_ref = f32[4,4,768]{2,1,0:T(4,128)S(1)} collective-permute-done((f32[4,4,768]{2,1,0:T(4,128)S(1)}, f32[4,4,768]{2,1,0:T(4,128)S(1)}, u32[]{:S(2)}, u32[]{:S(2)}) %collective-permute-start.5) | collective-permute-done | bytes 49184 | tf_op jit(solution)/shard_map/ppermute | solution.py:185
  24.4 0.9 %collective-permute-done.4.next_ref = f32[4,4,768]{2,1,0:T(4,128)S(1)} collective-permute-done((f32[4,4,768]{2,1,0:T(4,128)S(1)}, f32[4,4,768]{2,1,0:T(4,128)S(1)}, u32[]{:S(2)}, u32[]{:S(2)}) %collective-permute-start.4) | collective-permute-done | bytes 49184 | tf_op jit(solution)/shard_map/ppermute | solution.py:185
  25.3 0.0 collective-permute-done.3.pol_ref
  25.3 0.0 copy-done.1
  25.3 1.9 %couple.1 = f32[2,4,2,192]{3,2,1,0:T(2,128)} custom-call(f32[4,4,768]{2,1,0:T(4,128)S(1)} %get-tuple-element.13.own_ref, f32[4,4,768]{2,1,0:T(4,128)S(1)} %collective-permute-done.3.pol_ref, f32[4,4,768]{2,1,0:T(4,128)S(1)} %collective-permute-done.4.next_ref, f32[4,4,768]{2,1,0:T(4,128)S(1)} %collective-permute-done.5.cross_ref, ...), custom_call_target="tpu_custom_call" | custom-call | tf_op jit(solution)/shard_map/couple/pallas_call | solution.py:155
  (1 shorter events, 0.0 us)
Async XLA Ops:
  0.6 1.9 %copy-start.2 = (f32[2,512,4,192]{1,3,2,0:T(8,128)S(1)}, f32[2,512,4,192]{1,3,2,0:T(8,128)}, u32[]{:S(2)}) copy-start(f32[2,512,4,192]{1,3,2,0:T(8,128)} %param.4) | copy-start | bytes 9437188
  2.5 0.7 %copy-start.3 = (s32[8]{0:T(128)S(1)}, s32[8]{0:T(128)}, u32[]{:S(2)}) copy-start(s32[8]{0:T(128)} %orders.1) | copy-start | bytes 100
  3.2 19.1 %copy-start.4 = (f32[4,5,768]{2,0,1:T(4,128)S(1)}, f32[4,5,768]{2,0,1:T(4,128)}, u32[]{:S(2)}) copy-start(f32[4,5,768]{2,0,1:T(4,128)} %param.6) | copy-start | bytes 184324
  7.5 7.0 %collective-permute-start = (f32[4,4,192]{2,1,0:T(4,128)S(1)}, f32[4,4,192]{2,1,0:T(4,128)S(1)}, u32[]{:S(2)}, u32[]{:S(2)}) collective-permute-start(f32[4,4,192]{2,1,0:T(4,128)S(1)} %get-tuple-element.9), channel_id=1, source_target_pairs={{0,4},{4,8},{8,12},{12,0},{1,5},{5,9},{9,13},{13,1},{2,6},{6,10},{... | collective-permute-start | bytes 36872 | tf_op jit(solution)/shard_map/ppermute | solution.py:176
  10.5 4.7 %collective-permute-start.1 = (f32[4,4,192]{2,1,0:T(4,128)S(1)}, f32[4,4,192]{2,1,0:T(4,128)S(1)}, u32[]{:S(2)}, u32[]{:S(2)}) collective-permute-start(f32[4,4,192]{2,1,0:T(4,128)S(1)} %get-tuple-element.10), channel_id=1, source_target_pairs={{0,8},{4,12},{8,0},{12,4},{1,9},{5,13},{9,1},{13,5},{2,10},{6,14},... | collective-permute-start | bytes 36872 | tf_op jit(solution)/shard_map/ppermute | solution.py:176
  13.1 3.7 %collective-permute-start.2 = (f32[4,4,192]{2,1,0:T(4,128)S(1)}, f32[4,4,192]{2,1,0:T(4,128)S(1)}, u32[]{:S(2)}, u32[]{:S(2)}) collective-permute-start(f32[4,4,192]{2,1,0:T(4,128)S(1)} %get-tuple-element.11), channel_id=1, source_target_pairs={{0,12},{4,0},{8,4},{12,8},{1,13},{5,1},{9,5},{13,9},{2,14},{6,2},{... | collective-permute-start | bytes 36872 | tf_op jit(solution)/shard_map/ppermute | solution.py:176
  16.9 2.3 %copy-start = (bf16[2,4,2,192,768]{4,3,2,1,0:T(8,128)(2,1)S(1)}, bf16[2,4,2,192,768]{4,3,2,1,0:T(8,128)(2,1)}, u32[]{:S(2)}) copy-start(bf16[2,4,2,192,768]{4,3,2,1,0:T(8,128)(2,1)} %beam.1) | copy-start | bytes 14155780
  19.2 6.1 %copy-start.1 = (bf16[2,4,2,192,768]{4,3,2,1,0:T(8,128)(2,1)S(1)}, bf16[2,4,2,192,768]{4,3,2,1,0:T(8,128)(2,1)}, u32[]{:S(2)}) copy-start(bf16[2,4,2,192,768]{4,3,2,1,0:T(8,128)(2,1)} %beam.1) | copy-start | bytes 14155780
  20.4 4.0 %collective-permute-start.5 = (f32[4,4,768]{2,1,0:T(4,128)S(1)}, f32[4,4,768]{2,1,0:T(4,128)S(1)}, u32[]{:S(2)}, u32[]{:S(2)}) collective-permute-start(f32[4,4,768]{2,1,0:T(4,128)S(1)} %get-tuple-element.13.own_ref), channel_id=1, source_target_pairs={{3,0},{2,1},{1,2},{0,3},{7,4},{6,5},{5,6},{4,7},{11,8},{10,9},{9,1... | collective-permute-start | bytes 147464 | tf_op jit(solution)/shard_map/ppermute | solution.py:185
  20.4 4.9 %collective-permute-start.4 = (f32[4,4,768]{2,1,0:T(4,128)S(1)}, f32[4,4,768]{2,1,0:T(4,128)S(1)}, u32[]{:S(2)}, u32[]{:S(2)}) collective-permute-start(f32[4,4,768]{2,1,0:T(4,128)S(1)} %get-tuple-element.13.own_ref), channel_id=1, source_target_pairs={{2,0},{3,1},{0,2},{1,3},{6,4},{7,5},{4,6},{5,7},{10,8},{11,9},{8,1... | collective-permute-start | bytes 147464 | tf_op jit(solution)/shard_map/ppermute | solution.py:185
  21.9 3.4 %collective-permute-start.3 = (f32[4,4,768]{2,1,0:T(4,128)S(1)}, f32[4,4,768]{2,1,0:T(4,128)S(1)}, u32[]{:S(2)}, u32[]{:S(2)}) collective-permute-start(f32[4,4,768]{2,1,0:T(4,128)S(1)} %get-tuple-element.13.own_ref), channel_id=1, source_target_pairs={{1,0},{0,1},{3,2},{2,3},{5,4},{4,5},{7,6},{6,7},{9,8},{8,9},{11,10... | collective-permute-start | bytes 147464 | tf_op jit(solution)/shard_map/ppermute | solution.py:185

commit v2 on v1

v2 whole, which is shorter than its diff:
```python
import math

import jax
import jax.numpy as jnp
from jax import lax
from jax.experimental import pallas as pl
from jax.experimental.pallas import tpu as pltpu
from jax.sharding import PartitionSpec as P

TIME = 2048
BAND = 4
MIB = 1024 * 1024


def tables(order, time):
    step = (order * time) & (TIME - 1)
    quarter = (step + TIME // 8) >> 9
    x = (step - (quarter << 9)).astype(jnp.float32) * (2.0 * math.pi / TIME)
    y = x * x
    sine = x * (1.0 + y * (-1.0 / 6 + y * (1.0 / 120 + y * (-1.0 / 5040 + y * (1.0 / 362880)))))
    cosine = 1.0 + y * (
        -0.5 + y * (1.0 / 24 + y * (-1.0 / 720 + y * (1.0 / 40320 + y * (-1.0 / 3628800))))
    )
    factor = 1.0 / math.sqrt(TIME)
    odd = (quarter & 1) == 1
    cos_sign = jnp.where(((quarter + 1) & 2) == 2, -factor, factor)
    sin_sign = jnp.where((quarter & 2) == 2, -factor, factor)
    return jnp.where(odd, sine, cosine) * cos_sign, jnp.where(odd, cosine, sine) * sin_sign


def split(value):
    high = value.astype(jnp.bfloat16)
    return high, (value - high.astype(jnp.float32)).astype(jnp.bfloat16)


def dot_last(left, right):
    return lax.dot_general(left, right, (((1,), (1,)), ((), ())), preferred_element_type=jnp.float32)


def partner(me, step, size):
    return lax.rem(me + step, size)


def pin(array):
    return pltpu.with_memory_space_constraint(array, pltpu.HBM)


def transform(visibilities, m_orders, size):
    _, points, times = visibilities.shape
    total = m_orders.shape[0]
    per = total // size
    width = 384
    chunks = points // width

    def kernel(orders_ref, vis, *rest):
        out, held, orders, sems, order_sem = rest
        copies = [
            [
                pltpu.make_async_copy(
                    vis.at[c, pl.ds(n * width, width)], held.at[c, n], sems.at[c, n]
                )
                for c in range(2)
            ]
            for n in range(chunks)
        ]
        fetch = pltpu.make_async_copy(orders_ref, orders, order_sem)
        fetch.start()
        for pair in copies:
            for copy in pair:
                copy.start()
        fetch.wait()
        me = lax.axis_index("wide")
        row = lax.broadcasted_iota(jnp.int32, (total, times), 0)
        order = jnp.zeros((total, times), jnp.int32)
        for s in range(size):
            for i in range(per):
                order = jnp.where(row == s * per + i, orders[partner(me, s, size) * per + i], order)
        time = lax.broadcasted_iota(jnp.int32, (total, times), 1) + me * times
        cosine, sine = tables(order, time)
        lefts = []
        for c in range(2):
            table = jnp.concatenate([cosine, -sine] if c == 0 else [sine, cosine], 0)
            high, low = split(table)
            lefts.append((jnp.concatenate([high, low], 0), high))
        for n in range(chunks):
            acc = None
            for c in range(2):
                copies[n][c].wait()
                high, low = split(held[c, n])
                both = dot_last(lefts[c][0], high)
                term = both[: 2 * total] + both[2 * total :] + dot_last(lefts[c][1], low)
                acc = term if acc is None else acc + term
            out[:, pl.ds(n * width, width)] = acc

    return pl.pallas_call(
        kernel,
        out_shape=jax.ShapeDtypeStruct((2 * total, points), jnp.float32),
        in_specs=[pl.BlockSpec(memory_space=pltpu.HBM)] * 2,
        out_specs=pl.BlockSpec(memory_space=pltpu.VMEM),
        scratch_shapes=[
            pltpu.VMEM((2, chunks, width, times), jnp.float32),
            pltpu.SMEM((total,), jnp.int32),
            pltpu.SemaphoreType.DMA((2, chunks)),
            pltpu.SemaphoreType.DMA,
        ],
        compiler_params=pltpu.CompilerParams(vmem_limit_bytes=12 * MIB),
        cost_estimate=pl.CostEstimate(
            flops=4 * 10**9, bytes_accessed=8 * 10**6, transcendentals=0
        ),
        name="transform",
    )(pin(m_orders), pin(visibilities))


def cut(sums, size):
    rows, points = sums.shape
    total = rows // 2
    per = total // size

    def kernel(sums_ref, *outs):
        now = sums_ref[...]
        for s in range(size):
            for c in range(2):
                first = c * total + s * per
                outs[s][c * per : (c + 1) * per, :] = now[first : first + per]

    return pl.pallas_call(
        kernel,
        out_shape=[jax.ShapeDtypeStruct((2 * per, points), jnp.float32)] * size,
        in_specs=[pl.BlockSpec(memory_space=pltpu.VMEM)],
        out_specs=[pl.BlockSpec(memory_space=pltpu.VMEM)] * size,
        compiler_params=pltpu.CompilerParams(vmem_limit_bytes=4 * MIB),
        cost_estimate=pl.CostEstimate(flops=200 * 10**9, bytes_accessed=10**6, transcendentals=0),
        name="cut",
    )(sums)


def project(parts, beams):
    per, blocks, _, modes, degrees = beams.shape
    count = len(parts)

    def kernel(*refs):
        pieces, beam, total_out, proj_out = refs[:count], refs[count], refs[count + 1], refs[count + 2]
        row = lax.broadcasted_iota(jnp.int32, (2 * per, degrees), 0)
        total = pieces[0][...]
        for piece in pieces[1:]:
            total = total + piece[...]
        total_out[...] = total
        plain_all = total.astype(jnp.bfloat16)
        turned_all = jnp.concatenate([total[per:], -total[:per]], 0).astype(jnp.bfloat16)
        for f in range(blocks):
            plain = plain_all[:, f * modes : (f + 1) * modes]
            turned = turned_all[:, f * modes : (f + 1) * modes]
            acc = None
            for r in range(per):
                term = jnp.dot(plain, beam[r, f, 0], preferred_element_type=jnp.float32)
                term = term + jnp.dot(turned, beam[r, f, 1], preferred_element_type=jnp.float32)
                acc = term if acc is None else jnp.where(row % per == r, term, acc)
            proj_out[f] = acc

    return pl.pallas_call(
        kernel,
        out_shape=[
            jax.ShapeDtypeStruct((2 * per, blocks * modes), jnp.float32),
            jax.ShapeDtypeStruct((blocks, 2 * per, degrees), jnp.float32),
        ],
        in_specs=[pl.BlockSpec(memory_space=pltpu.VMEM)] * (count + 1),
        out_specs=[pl.BlockSpec(memory_space=pltpu.VMEM)] * 2,
        compiler_params=pltpu.CompilerParams(vmem_limit_bytes=12 * MIB),
        name="project",
    )(*parts, beams)


def arrange(total, beams):
    per, blocks, _, modes, degrees = beams.shape
    wide = per * modes

    def kernel(total_ref, beam, out, turned):
        total_now = total_ref[...]
        for f in range(blocks):
            block = total_now[:, f * modes : (f + 1) * modes]
            for r in range(per):
                for c in range(2):
                    out[r, f, c : c + 1, :] = block[c * per + r : c * per + r + 1]
            for c in range(2):
                both = jnp.concatenate([beam[r, f, c] for r in range(per)], 0)
                turned[c, :, f * wide : (f + 1) * wide] = both.T

    return pl.pallas_call(
        kernel,
        out_shape=[
            jax.ShapeDtypeStruct((per, blocks, 2, modes), jnp.float32),
            jax.ShapeDtypeStruct((2, degrees, blocks * wide), jnp.bfloat16),
        ],
        in_specs=[pl.BlockSpec(memory_space=pltpu.VMEM)] * 2,
        out_specs=[pl.BlockSpec(memory_space=pltpu.VMEM)] * 2,
        compiler_params=pltpu.CompilerParams(vmem_limit_bytes=16 * MIB),
        name="arrange",
    )(total, beams)


def couple(own, others, spectra, turned_beams, modes):
    blocks, rows, degrees = own.shape
    per = rows // 2
    wide = per * modes

    def kernel(own_ref, cross_ref, next_ref, pol_ref, spec, beam, out):
        summed = [own_ref[f] + pol_ref[f] for f in range(blocks)]
        summed += [next_ref[f] + cross_ref[f] for f in range(blocks)]
        plain, turned = [], []
        for f in range(blocks):
            mixed = None
            for d in range(BAND + 1):
                term = spec[f, d : d + 1, :] * summed[f + d]
                mixed = term if mixed is None else mixed + term
            plain.append(mixed)
            turned.append(jnp.concatenate([-mixed[per:], mixed[:per]], 0))
        plain = jnp.concatenate(plain, 0).astype(jnp.bfloat16)
        turned = jnp.concatenate(turned, 0).astype(jnp.bfloat16)
        acc = jnp.dot(plain, beam[0], preferred_element_type=jnp.float32)
        acc = acc + jnp.dot(turned, beam[1], preferred_element_type=jnp.float32)
        for f in range(blocks):
            for r in range(per):
                first = f * wide + r * modes
                piece = acc[f * rows : (f + 1) * rows, first : first + modes]
                for c in range(2):
                    out[r, f, c : c + 1, :] = piece[c * per + r : c * per + r + 1]

    return pl.pallas_call(
        kernel,
        out_shape=jax.ShapeDtypeStruct((per, blocks, 2, modes), jnp.float32),
        in_specs=[pl.BlockSpec(memory_space=pltpu.VMEM)] * 6,
        out_specs=pl.BlockSpec(memory_space=pltpu.VMEM),
        compiler_params=pltpu.CompilerParams(vmem_limit_bytes=12 * MIB),
        name="couple",
    )(own, *others, spectra, turned_beams)


def shards(visibilities, beams, spectra, m_orders):
    size = lax.axis_size("wide")
    freqs = lax.axis_size("freq")
    pols = lax.axis_size("pol")
    per, blocks, _, modes, _ = beams.shape
    times = visibilities.shape[1]
    sums = transform(
        visibilities.transpose(0, 2, 3, 1).reshape(2, blocks * modes, times), m_orders, size
    )
    parts = cut(sums, size)
    arrived = [parts[0]]
    for s in range(1, size):
        arrived.append(lax.ppermute(parts[s], "wide", [(i, (i + s) % size) for i in range(size)]))
    total, partial = project(arrived, beams)

    def fetch(freq_step, pol_step):
        pairs = [
            (((f + freq_step) % freqs) * pols + (p + pol_step) % pols, f * pols + p)
            for f in range(freqs)
            for p in range(pols)
        ]
        return lax.ppermute(partial, ("freq", "pol"), pairs)

    cross, next_one, pol = fetch(1, 1), fetch(1, 0), fetch(0, 1)
    others = [cross, next_one, pol]
    msdata, turned = arrange(total, beams)
    return msdata, couple(partial, others, spectra, turned, modes)


def solution(mesh):
    return jax.shard_map(
        shards,
        mesh=mesh,
        in_specs=(
            P(None, ("grp", "wide"), "freq", "pol"),
            P("wide", "freq", None, "pol", None),
            P("freq", None, None),
            P(),
        ),
        out_specs=(
            P(("grp", "wide"), "freq", None, "pol"),
            P(("grp", "wide"), "freq", None, "pol"),
        ),
        check_vma=False,
    )
```

time: 27.5 us -> 20 us (0.73)
  local copies, waits for them, and re-layouts: 4.9 us -> 0.03 us
  waiting for transfers between devices: 5.42 us -> 3.78 us
  Pallas kernels: 7.42 us -> 6.47 us
    unnamed x11 -> x5, local copies, waits for them, and re-layouts: 4.9 us -> 0.03 us
    ppermute x3, waiting for transfers between devices: 3.03 us -> 1.43 us  [fetch(): return lax.ppermute(partial, ('freq', 'pol'), pairs)]
    pallas_call x1, Pallas kernels: 1.95 us -> 1.44 us  [couple(): pl.pallas_call(kernel, out_shape=jax.ShapeDtypeStruct((per, blocks, 2, mo...]
    pallas_call x2 -> x4, Pallas kernels: 5.47 us -> 5.03 us  [the longest x1 2.76 us: transform(): pl.pallas_call(kernel, out_shape=jax.ShapeDtypeStruct((2 * total, points)...]
  transfers between devices with their start and end apart: 6 -> 6, of which waited for: 4 -> 4; matrix products, arithmetic and copies ran while one was open for 0% -> 0% of each run, Pallas kernels for 0% -> 8%
where the time goes in v2:
time: 20 us; the launch traced here: 19.9 us
  starting transfers between devices  8.93 us (45%)
  Pallas kernels  6.47 us (32%)
  waiting for transfers between devices  3.78 us (19%)
  between operations  0.68 us (3%)
    ppermute x3, starting transfers between devices, shards(): lax.ppermute(parts[s], 'wide', [(i, (i + s) % size) for i in range(size)])  7.01 us
    pallas_call x1, Pallas kernels, transform(): pl.pallas_call(kernel, out_shape=jax.ShapeDtypeStruct((2 * total, points)...  2.76 us
    ppermute x3, waiting for transfers between devices, shards(): lax.ppermute(parts[s], 'wide', [(i, (i + s) % size) for i in range(size)])  2.35 us
    ppermute x3, starting transfers between devices, fetch(): return lax.ppermute(partial, ('freq', 'pol'), pairs)  1.92 us
    pallas_call x1, Pallas kernels, arrange(): pl.pallas_call(kernel, out_shape=[jax.ShapeDtypeStruct((per, blocks, 2, m...  1.59 us
    pallas_call x1, Pallas kernels, couple(): pl.pallas_call(kernel, out_shape=jax.ShapeDtypeStruct((per, blocks, 2, mo...  1.44 us
    ppermute x3, waiting for transfers between devices, fetch(): return lax.ppermute(partial, ('freq', 'pol'), pairs)  1.43 us
    pallas_call x1, Pallas kernels, project(): pl.pallas_call(kernel, out_shape=[jax.ShapeDtypeStruct((2 * per, blocks *...  0.67 us
  transfers between devices with their start and end apart: 6, of which 4 were waited for; matrix products, arithmetic and copies ran while one was open for 0% of the time, Pallas kernels for 8%

profile of v2, /device:TPU:0, one launch (start us, length us, event | category | flops | bytes accessed | tf_op | source)
XLA Modules:
  0.0 19.9 jit_solution(2285302037508203591)
XLA Ops:
  0.6 2.8 %transform.1.sums_ref = f32[16,768]{1,0:T(8,128)S(1)} custom-call(s32[8]{0:T(128)} %orders_ref.1, f32[2,768,512]{2,1,0:T(8,128)} %bitcast.3), custom_call_target="tpu_custom_call" | custom-call | flops 4000000000 | bytes 8000000 | tf_op jit(solution)/shard_map/transform/pallas_call | solution.py:95
  3.4 0.0 copy-start
  3.4 0.0 copy-start.1
  3.4 3.1 %collective-permute-start = (f32[4,768]{1,0:T(4,128)S(1)}, f32[4,768]{1,0:T(4,128)S(1)}, u32[]{:S(2)}, u32[]{:S(2)}) collective-permute-start(f32[4,768]{1,0:T(4,128)S(1)} %get-tuple-element.11), channel_id=1, source_target_pairs={{0,4},{4,8},{8,12},{12,0},{1,5},{5,9},{9,13},{13,1},{2,6},{6,10},{... | collective-permute-start | bytes 36872 | tf_op jit(solution)/shard_map/ppermute | solution.py:250
  6.5 2.6 %collective-permute-start.1 = (f32[4,768]{1,0:T(4,128)S(1)}, f32[4,768]{1,0:T(4,128)S(1)}, u32[]{:S(2)}, u32[]{:S(2)}) collective-permute-start(f32[4,768]{1,0:T(4,128)S(1)} %get-tuple-element.12), channel_id=1, source_target_pairs={{0,8},{4,12},{8,0},{12,4},{1,9},{5,13},{9,1},{13,5},{2,10},{6,14},... | collective-permute-start | bytes 36872 | tf_op jit(solution)/shard_map/ppermute | solution.py:250
  9.1 1.3 %collective-permute-start.2 = (f32[4,768]{1,0:T(4,128)S(1)}, f32[4,768]{1,0:T(4,128)S(1)}, u32[]{:S(2)}, u32[]{:S(2)}) collective-permute-start(f32[4,768]{1,0:T(4,128)S(1)} %get-tuple-element.13), channel_id=1, source_target_pairs={{0,12},{4,0},{8,4},{12,8},{1,13},{5,1},{9,5},{13,9},{2,14},{6,2},{... | collective-permute-start | bytes 36872 | tf_op jit(solution)/shard_map/ppermute | solution.py:250
  10.5 0.0 collective-permute-done.refs_1_
  10.5 0.8 %collective-permute-done.1.refs_2_ = f32[4,768]{1,0:T(4,128)S(1)} collective-permute-done((f32[4,768]{1,0:T(4,128)S(1)}, f32[4,768]{1,0:T(4,128)S(1)}, u32[]{:S(2)}, u32[]{:S(2)}) %collective-permute-start.1) | collective-permute-done | bytes 12320 | tf_op jit(solution)/shard_map/ppermute | solution.py:250
  11.2 1.6 %collective-permute-done.2.refs_3_ = f32[4,768]{1,0:T(4,128)S(1)} collective-permute-done((f32[4,768]{1,0:T(4,128)S(1)}, f32[4,768]{1,0:T(4,128)S(1)}, u32[]{:S(2)}, u32[]{:S(2)}) %collective-permute-start.2) | collective-permute-done | bytes 12320 | tf_op jit(solution)/shard_map/ppermute | solution.py:250
  12.8 0.0 copy-done
  12.8 0.7 %project.1 = (f32[4,768]{1,0:T(4,128)S(1)}, f32[4,4,768]{2,1,0:T(4,128)S(1)}) custom-call(f32[4,768]{1,0:T(4,128)S(1)} %get-tuple-element.10.refs_0_, f32[4,768]{1,0:T(4,128)S(1)} %collective-permute-done.refs_1_, f32[4,768]{1,0:T(4,128)S(1)} %collective-permute-done.1.refs_2_, f32[4,768]{1,0:T(4,128)S(1)} %collective-permute-done.2.refs_3_, ...), custom_call_target="tpu_custom_call" | custom-call | tf_op jit(solution)/shard_map/project/pallas_call | solution.py:160
  13.5 0.1 collective-permute-start.3
  13.6 1.6 %collective-permute-start.4 = (f32[4,4,768]{2,1,0:T(4,128)S(1)}, f32[4,4,768]{2,1,0:T(4,128)S(1)}, u32[]{:S(2)}, u32[]{:S(2)}) collective-permute-start(f32[4,4,768]{2,1,0:T(4,128)S(1)} %get-tuple-element.16.own_ref), channel_id=1, source_target_pairs={{2,0},{3,1},{0,2},{1,3},{6,4},{7,5},{4,6},{5,7},{10,8},{11,9},{8,1... | collective-permute-start | bytes 147464 | tf_op jit(solution)/shard_map/ppermute | solution.py:259
  15.1 0.3 %collective-permute-start.5 = (f32[4,4,768]{2,1,0:T(4,128)S(1)}, f32[4,4,768]{2,1,0:T(4,128)S(1)}, u32[]{:S(2)}, u32[]{:S(2)}) collective-permute-start(f32[4,4,768]{2,1,0:T(4,128)S(1)} %get-tuple-element.16.own_ref), channel_id=1, source_target_pairs={{1,0},{0,1},{3,2},{2,3},{5,4},{4,5},{7,6},{6,7},{9,8},{8,9},{11,10... | collective-permute-start | bytes 147464 | tf_op jit(solution)/shard_map/ppermute | solution.py:259
  15.4 0.0 copy-done.1
  15.4 1.6 %arrange.1 = (f32[2,4,2,192]{3,2,1,0:T(2,128)}, bf16[2,768,1536]{2,1,0:T(8,128)(2,1)S(1)}) custom-call(f32[4,768]{1,0:T(4,128)S(1)} %get-tuple-element.14.total_ref, bf16[2,4,2,192,768]{4,3,2,1,0:T(8,128)(2,1)S(1)} %copy-done), custom_call_target="tpu_custom_call" | custom-call | tf_op jit(solution)/shard_map/arrange/pallas_call | solution.py:188
  17.0 0.5 %collective-permute-done.3.cross_ref = f32[4,4,768]{2,1,0:T(4,128)S(1)} collective-permute-done((f32[4,4,768]{2,1,0:T(4,128)S(1)}, f32[4,4,768]{2,1,0:T(4,128)S(1)}, u32[]{:S(2)}, u32[]{:S(2)}) %collective-permute-start.3) | collective-permute-done | bytes 49184 | tf_op jit(solution)/shard_map/ppermute | solution.py:259
  17.5 0.9 %collective-permute-done.4.next_ref = f32[4,4,768]{2,1,0:T(4,128)S(1)} collective-permute-done((f32[4,4,768]{2,1,0:T(4,128)S(1)}, f32[4,4,768]{2,1,0:T(4,128)S(1)}, u32[]{:S(2)}, u32[]{:S(2)}) %collective-permute-start.4) | collective-permute-done | bytes 49184 | tf_op jit(solution)/shard_map/ppermute | solution.py:259
  18.5 0.0 collective-permute-done.5.pol_ref
  18.5 1.4 %couple.1 = f32[2,4,2,192]{3,2,1,0:T(2,128)} custom-call(f32[4,4,768]{2,1,0:T(4,128)S(1)} %get-tuple-element.16.own_ref, f32[4,4,768]{2,1,0:T(4,128)S(1)} %collective-permute-done.3.cross_ref, f32[4,4,768]{2,1,0:T(4,128)S(1)} %collective-permute-done.4.next_ref, f32[4,4,768]{2,1,0:T(4,128)S(1)} %collective-permute-done.5.pol_ref, ...), custom_call_target="tpu_custom_call" | custom-call | tf_op jit(solution)/shard_map/couple/pallas_call | solution.py:228
  (2 shorter events, 0.0 us)
Async XLA Ops:
  3.4 9.4 %copy-start = (bf16[2,4,2,192,768]{4,3,2,1,0:T(8,128)(2,1)S(1)}, bf16[2,4,2,192,768]{4,3,2,1,0:T(8,128)(2,1)}, u32[]{:S(2)}) copy-start(bf16[2,4,2,192,768]{4,3,2,1,0:T(8,128)(2,1)} %beam.1) | copy-start | bytes 14155780
  3.4 12.0 %copy-start.1 = (f32[4,5,768]{2,0,1:T(4,128)S(1)}, f32[4,5,768]{2,0,1:T(4,128)}, u32[]{:S(2)}) copy-start(f32[4,5,768]{2,0,1:T(4,128)} %param.6) | copy-start | bytes 184324
  3.4 7.0 %collective-permute-start = (f32[4,768]{1,0:T(4,128)S(1)}, f32[4,768]{1,0:T(4,128)S(1)}, u32[]{:S(2)}, u32[]{:S(2)}) collective-permute-start(f32[4,768]{1,0:T(4,128)S(1)} %get-tuple-element.11), channel_id=1, source_target_pairs={{0,4},{4,8},{8,12},{12,0},{1,5},{5,9},{9,13},{13,1},{2,6},{6,10},{... | collective-permute-start | bytes 36872 | tf_op jit(solution)/shard_map/ppermute | solution.py:250
  6.5 4.7 %collective-permute-start.1 = (f32[4,768]{1,0:T(4,128)S(1)}, f32[4,768]{1,0:T(4,128)S(1)}, u32[]{:S(2)}, u32[]{:S(2)}) collective-permute-start(f32[4,768]{1,0:T(4,128)S(1)} %get-tuple-element.12), channel_id=1, source_target_pairs={{0,8},{4,12},{8,0},{12,4},{1,9},{5,13},{9,1},{13,5},{2,10},{6,14},... | collective-permute-start | bytes 36872 | tf_op jit(solution)/shard_map/ppermute | solution.py:250
  9.1 3.7 %collective-permute-start.2 = (f32[4,768]{1,0:T(4,128)S(1)}, f32[4,768]{1,0:T(4,128)S(1)}, u32[]{:S(2)}, u32[]{:S(2)}) collective-permute-start(f32[4,768]{1,0:T(4,128)S(1)} %get-tuple-element.13), channel_id=1, source_target_pairs={{0,12},{4,0},{8,4},{12,8},{1,13},{5,1},{9,5},{13,9},{2,14},{6,2},{... | collective-permute-start | bytes 36872 | tf_op jit(solution)/shard_map/ppermute | solution.py:250
  13.5 4.1 %collective-permute-start.3 = (f32[4,4,768]{2,1,0:T(4,128)S(1)}, f32[4,4,768]{2,1,0:T(4,128)S(1)}, u32[]{:S(2)}, u32[]{:S(2)}) collective-permute-start(f32[4,4,768]{2,1,0:T(4,128)S(1)} %get-tuple-element.16.own_ref), channel_id=1, source_target_pairs={{3,0},{2,1},{1,2},{0,3},{7,4},{6,5},{5,6},{4,7},{11,8},{10,9},{9,1... | collective-permute-start | bytes 147464 | tf_op jit(solution)/shard_map/ppermute | solution.py:259
  13.6 4.9 %collective-permute-start.4 = (f32[4,4,768]{2,1,0:T(4,128)S(1)}, f32[4,4,768]{2,1,0:T(4,128)S(1)}, u32[]{:S(2)}, u32[]{:S(2)}) collective-permute-start(f32[4,4,768]{2,1,0:T(4,128)S(1)} %get-tuple-element.16.own_ref), channel_id=1, source_target_pairs={{2,0},{3,1},{0,2},{1,3},{6,4},{7,5},{4,6},{5,7},{10,8},{11,9},{8,1... | collective-permute-start | bytes 147464 | tf_op jit(solution)/shard_map/ppermute | solution.py:259
  15.1 3.3 %collective-permute-start.5 = (f32[4,4,768]{2,1,0:T(4,128)S(1)}, f32[4,4,768]{2,1,0:T(4,128)S(1)}, u32[]{:S(2)}, u32[]{:S(2)}) collective-permute-start(f32[4,4,768]{2,1,0:T(4,128)S(1)} %get-tuple-element.16.own_ref), channel_id=1, source_target_pairs={{1,0},{0,1},{3,2},{2,3},{5,4},{4,5},{7,6},{6,7},{9,8},{8,9},{11,10... | collective-permute-start | bytes 147464 | tf_op jit(solution)/shard_map/ppermute | solution.py:259

commit v3 on v2

--- a/solution.py
+++ b/solution.py
@@ -10,6 +10,7 @@
 TIME = 2048
 BAND = 4
 MIB = 1024 * 1024
+PLAN = ((1, 3, 2, 0), (2, 1, 0, 3), (3, 0, 2, 1), (0, 2, 1, 3), (0, 1, 3, 2))
 
 
 def tables(order, time):
@@ -37,8 +38,12 @@
     return lax.dot_general(left, right, (((1,), (1,)), ((), ())), preferred_element_type=jnp.float32)
 
 
-def partner(me, step, size):
-    return lax.rem(me + step, size)
+def pairs_of(step, pols):
+    return [
+        (w * pols + p, to * pols + (p if to != w else (p + 1) % pols))
+        for w, to in enumerate(step)
+        for p in range(pols)
+    ]
 
 
 def pin(array):
@@ -72,29 +77,32 @@
         me = lax.axis_index("wide")
         row = lax.broadcasted_iota(jnp.int32, (total, times), 0)
         order = jnp.zeros((total, times), jnp.int32)
-        for s in range(size):
-            for i in range(per):
-                order = jnp.where(row == s * per + i, orders[partner(me, s, size) * per + i], order)
+        for i in range(total):
+            order = jnp.where(row == i, orders[i], order)
         time = lax.broadcasted_iota(jnp.int32, (total, times), 1) + me * times
         cosine, sine = tables(order, time)
         lefts = []
         for c in range(2):
             table = jnp.concatenate([cosine, -sine] if c == 0 else [sine, cosine], 0)
             high, low = split(table)
-            lefts.append((jnp.concatenate([high, low], 0), high))
+            lefts.append(jnp.concatenate([high, low], 0))
         for n in range(chunks):
+            for copy in copies[n]:
+                copy.wait()
             acc = None
             for c in range(2):
-                copies[n][c].wait()
                 high, low = split(held[c, n])
-                both = dot_last(lefts[c][0], high)
-                term = both[: 2 * total] + both[2 * total :] + dot_last(lefts[c][1], low)
+                both = dot_last(lefts[c], jnp.concatenate([high, low], 0))
+                term = both[: 2 * total, :width] + both[2 * total :, :width] + both[: 2 * total, width:]
                 acc = term if acc is None else acc + term
-            out[:, pl.ds(n * width, width)] = acc
-
-    return pl.pallas_call(
-        kernel,
-        out_shape=jax.ShapeDtypeStruct((2 * total, points), jnp.float32),
+            for s in range(size):
+                for c in range(2):
+                    first = c * total + s * per
+                    out[s, c * per : (c + 1) * per, pl.ds(n * width, width)] = acc[first : first + per]
+
+    return pl.pallas_call(
+        kernel,
+        out_shape=jax.ShapeDtypeStruct((size, 2 * per, points), jnp.float32),
         in_specs=[pl.BlockSpec(memory_space=pltpu.HBM)] * 2,
         out_specs=pl.BlockSpec(memory_space=pltpu.VMEM),
         scratch_shapes=[
@@ -111,23 +119,26 @@
     )(pin(m_orders), pin(visibilities))
 
 
-def cut(sums, size):
-    rows, points = sums.shape
-    total = rows // 2
-    per = total // size
+def cut(sums, plan):
+    size, rows, points = sums.shape
 
     def kernel(sums_ref, *outs):
-        now = sums_ref[...]
-        for s in range(size):
-            for c in range(2):
-                first = c * total + s * per
-                outs[s][c * per : (c + 1) * per, :] = now[first : first + per]
-
-    return pl.pallas_call(
-        kernel,
-        out_shape=[jax.ShapeDtypeStruct((2 * per, points), jnp.float32)] * size,
+        me = lax.axis_index("wide")
+        outs[0][...] = sums_ref[me]
+        for out, step in zip(outs[1:], plan):
+            to = jnp.int32(step[0])
+            for w in range(1, size):
+                to = jnp.where(me == w, step[w], to)
+            if any(step[w] == w for w in range(size)):
+                out[...] = jnp.where(to == me, 0.0, sums_ref[to])
+            else:
+                out[...] = sums_ref[to]
+
+    return pl.pallas_call(
+        kernel,
+        out_shape=[jax.ShapeDtypeStruct((rows, points), jnp.float32)] * (len(plan) + 1),
         in_specs=[pl.BlockSpec(memory_space=pltpu.VMEM)],
-        out_specs=[pl.BlockSpec(memory_space=pltpu.VMEM)] * size,
+        out_specs=[pl.BlockSpec(memory_space=pltpu.VMEM)] * (len(plan) + 1),
         compiler_params=pltpu.CompilerParams(vmem_limit_bytes=4 * MIB),
         cost_estimate=pl.CostEstimate(flops=200 * 10**9, bytes_accessed=10**6, transcendentals=0),
         name="cut",
@@ -198,14 +209,13 @@
     )(total, beams)
 
 
-def couple(own, others, spectra, turned_beams, modes):
+def couple(own, following, spectra, turned_beams, modes):
     blocks, rows, degrees = own.shape
     per = rows // 2
     wide = per * modes
 
-    def kernel(own_ref, cross_ref, next_ref, pol_ref, spec, beam, out):
-        summed = [own_ref[f] + pol_ref[f] for f in range(blocks)]
-        summed += [next_ref[f] + cross_ref[f] for f in range(blocks)]
+    def kernel(own_ref, next_ref, spec, beam, out):
+        summed = [own_ref[f] for f in range(blocks)] + [next_ref[f] for f in range(blocks)]
         plain, turned = [], []
         for f in range(blocks):
             mixed = None
@@ -228,11 +238,11 @@
     return pl.pallas_call(
         kernel,
         out_shape=jax.ShapeDtypeStruct((per, blocks, 2, modes), jnp.float32),
-        in_specs=[pl.BlockSpec(memory_space=pltpu.VMEM)] * 6,
+        in_specs=[pl.BlockSpec(memory_space=pltpu.VMEM)] * 4,
         out_specs=pl.BlockSpec(memory_space=pltpu.VMEM),
         compiler_params=pltpu.CompilerParams(vmem_limit_bytes=12 * MIB),
         name="couple",
-    )(own, *others, spectra, turned_beams)
+    )(own, following, spectra, turned_beams)
 
 
 def shards(visibilities, beams, spectra, m_orders):
@@ -244,24 +254,23 @@
     sums = transform(
         visibilities.transpose(0, 2, 3, 1).reshape(2, blocks * modes, times), m_orders, size
     )
-    parts = cut(sums, size)
-    arrived = [parts[0]]
-    for s in range(1, size):
-        arrived.append(lax.ppermute(parts[s], "wide", [(i, (i + s) % size) for i in range(size)]))
+    plan = PLAN if size == 4 else [[(w + s) % size for w in range(size)] for s in range(1, size)]
+    own, *parts = cut(sums, plan)
+    arrived = [own] + [
+        lax.ppermute(part, ("wide", "pol"), pairs_of(step, pols)) for part, step in zip(parts, plan)
+    ]
     total, partial = project(arrived, beams)
 
-    def fetch(freq_step, pol_step):
-        pairs = [
-            (((f + freq_step) % freqs) * pols + (p + pol_step) % pols, f * pols + p)
-            for f in range(freqs)
-            for p in range(pols)
-        ]
-        return lax.ppermute(partial, ("freq", "pol"), pairs)
-
-    cross, next_one, pol = fetch(1, 1), fetch(1, 0), fetch(0, 1)
-    others = [cross, next_one, pol]
+    other = lax.ppermute(partial, "pol", [(p, (p + 1) % pols) for p in range(pols)])
+    projected = partial + other
+    pairs = [
+        (((f + 1) % freqs) * pols + (p + 1) % pols, f * pols + p)
+        for f in range(freqs)
+        for p in range(pols)
+    ]
+    following = lax.ppermute(projected, ("freq", "pol"), pairs)
     msdata, turned = arrange(total, beams)
-    return msdata, couple(partial, others, spectra, turned, modes)
+    return msdata, couple(projected, following, spectra, turned, modes)
 
 
 def solution(mesh):

time: 20 us -> 18.5 us (0.925)
  starting transfers between devices: 8.93 us -> 7.14 us
  waiting for transfers between devices: 3.78 us -> 4.16 us
    ppermute x6 -> x7, starting transfers between devices: 8.93 us -> 7.14 us  [the longest x5 5.75 us: shards(): lax.ppermute(part, ('wide', 'pol'), pairs_of(step, pols))]
    ppermute x6 -> x7, waiting for transfers between devices: 3.78 us -> 4.16 us  [the longest x5 2.11 us: shards(): lax.ppermute(part, ('wide', 'pol'), pairs_of(step, pols))]
  transfers between devices with their start and end apart: 6 -> 7, of which waited for: 4 -> 5; matrix products, arithmetic and copies ran while one was open for 0% -> 0% of each run, Pallas kernels for 8% -> 9%
where the time goes in v3:
time: 18.5 us; the launch traced here: 18.3 us
  starting transfers between devices  7.14 us (39%)
  Pallas kernels  6.29 us (34%)
  waiting for transfers between devices  4.16 us (22%)
  between operations  0.69 us (4%)
    ppermute x5, starting transfers between devices, shards(): lax.ppermute(part, ('wide', 'pol'), pairs_of(step, pols))  5.75 us
    pallas_call x1, Pallas kernels, transform(): pl.pallas_call(kernel, out_shape=jax.ShapeDtypeStruct((size, 2 * per, poi...  2.57 us
    ppermute x5, waiting for transfers between devices, shards(): lax.ppermute(part, ('wide', 'pol'), pairs_of(step, pols))  2.11 us
    pallas_call x1, Pallas kernels, arrange(): pl.pallas_call(kernel, out_shape=[jax.ShapeDtypeStruct((per, blocks, 2, m...  1.59 us
    pallas_call x1, Pallas kernels, couple(): pl.pallas_call(kernel, out_shape=jax.ShapeDtypeStruct((per, blocks, 2, mo...  1.43 us
    ppermute x1, starting transfers between devices, shards(): following = lax.ppermute(projected, ('freq', 'pol'), pairs)  1.32 us
    ppermute x1, waiting for transfers between devices, shards(): lax.ppermute(partial, 'pol', [(p, (p + 1) % pols) for p in range(pols)])  1.22 us
    ppermute x1, waiting for transfers between devices, shards(): following = lax.ppermute(projected, ('freq', 'pol'), pairs)  0.83 us
  transfers between devices with their start and end apart: 7, of which 5 were waited for; matrix products, arithmetic and copies ran while one was open for 0% of the time, Pallas kernels for 9%

profile of v3, /device:TPU:0, one launch (start us, length us, event | category | flops | bytes accessed | tf_op | source)
XLA Modules:
  0.0 18.3 jit_solution(12119078880310027274)
XLA Ops:
  0.6 2.6 %transform.1.sums_ref = f32[4,4,768]{2,1,0:T(4,128)S(1)} custom-call(s32[8]{0:T(128)} %orders_ref.1, f32[2,768,512]{2,1,0:T(8,128)} %bitcast.3), custom_call_target="tpu_custom_call" | custom-call | flops 4000000000 | bytes 8000000 | tf_op jit(solution)/shard_map/transform/pallas_call | solution.py:103
  3.2 0.0 copy-start
  3.3 0.0 copy-start.1
  3.3 3.1 %collective-permute-start = (f32[4,768]{1,0:T(4,128)S(1)}, f32[4,768]{1,0:T(4,128)S(1)}, u32[]{:S(2)}, u32[]{:S(2)}) collective-permute-start(f32[4,768]{1,0:T(4,128)S(1)} %get-tuple-element.13), channel_id=1, source_target_pairs={{0,4},{1,5},{4,12},{5,13},{8,9},{9,8},{12,0},{13,1},{2,6},{3,7},{6... | collective-permute-start | bytes 36872 | tf_op jit(solution)/shard_map/ppermute | solution.py:260
  6.3 1.1 %collective-permute-start.1 = (f32[4,768]{1,0:T(4,128)S(1)}, f32[4,768]{1,0:T(4,128)S(1)}, u32[]{:S(2)}, u32[]{:S(2)}) collective-permute-start(f32[4,768]{1,0:T(4,128)S(1)} %get-tuple-element.14), channel_id=1, source_target_pairs={{0,8},{1,9},{4,5},{5,4},{8,0},{9,1},{12,13},{13,12},{2,10},{3,11},... | collective-permute-start | bytes 36872 | tf_op jit(solution)/shard_map/ppermute | solution.py:260
  7.4 1.1 %collective-permute-start.2 = (f32[4,768]{1,0:T(4,128)S(1)}, f32[4,768]{1,0:T(4,128)S(1)}, u32[]{:S(2)}, u32[]{:S(2)}) collective-permute-start(f32[4,768]{1,0:T(4,128)S(1)} %get-tuple-element.15), channel_id=1, source_target_pairs={{0,12},{1,13},{4,0},{5,1},{8,9},{9,8},{12,4},{13,5},{2,14},{3,15},... | collective-permute-start | bytes 36872 | tf_op jit(solution)/shard_map/ppermute | solution.py:260
  8.5 0.2 collective-permute-start.3
  8.7 0.3 %collective-permute-start.4 = (f32[4,768]{1,0:T(4,128)S(1)}, f32[4,768]{1,0:T(4,128)S(1)}, u32[]{:S(2)}, u32[]{:S(2)}) collective-permute-start(f32[4,768]{1,0:T(4,128)S(1)} %get-tuple-element.17), channel_id=1, source_target_pairs={{0,1},{1,0},{4,5},{5,4},{8,12},{9,13},{12,8},{13,9},{2,3},{3,2},{6... | collective-permute-start | bytes 36872 | tf_op jit(solution)/shard_map/ppermute | solution.py:260
  9.0 1.0 %collective-permute-done.refs_1_ = f32[4,768]{1,0:T(4,128)S(1)} collective-permute-done((f32[4,768]{1,0:T(4,128)S(1)}, f32[4,768]{1,0:T(4,128)S(1)}, u32[]{:S(2)}, u32[]{:S(2)}) %collective-permute-start) | collective-permute-done | bytes 12320 | tf_op jit(solution)/shard_map/ppermute | solution.py:260
  10.0 0.9 %collective-permute-done.1.refs_2_ = f32[4,768]{1,0:T(4,128)S(1)} collective-permute-done((f32[4,768]{1,0:T(4,128)S(1)}, f32[4,768]{1,0:T(4,128)S(1)}, u32[]{:S(2)}, u32[]{:S(2)}) %collective-permute-start.1) | collective-permute-done | bytes 12320 | tf_op jit(solution)/shard_map/ppermute | solution.py:260
  10.9 0.2 %collective-permute-done.2.refs_3_ = f32[4,768]{1,0:T(4,128)S(1)} collective-permute-done((f32[4,768]{1,0:T(4,128)S(1)}, f32[4,768]{1,0:T(4,128)S(1)}, u32[]{:S(2)}, u32[]{:S(2)}) %collective-permute-start.2) | collective-permute-done | bytes 12320 | tf_op jit(solution)/shard_map/ppermute | solution.py:260
  11.1 0.0 collective-permute-done.3.refs_4_
  11.1 0.0 collective-permute-done.4.refs_5_
  11.1 0.0 copy-done
  11.1 0.7 %project.1 = (f32[4,768]{1,0:T(4,128)S(1)}, f32[4,4,768]{2,1,0:T(4,128)S(1)}) custom-call(f32[4,768]{1,0:T(4,128)S(1)} %get-tuple-element.12.refs_0_, f32[4,768]{1,0:T(4,128)S(1)} %collective-permute-done.refs_1_, f32[4,768]{1,0:T(4,128)S(1)} %collective-permute-done.1.refs_2_, f32[4,768]{1,0:T(4,128)S(1)} %collective-permute-done.2.refs_3_, ...), custom_call_target="tpu_custom_call" | custom-call | tf_op jit(solution)/shard_map/project/pallas_call | solution.py:171
  11.8 0.1 collective-permute-start.5
  11.9 1.2 %collective-permute-done.5 = f32[4,4,768]{2,1,0:T(4,128)S(1)} collective-permute-done((f32[4,4,768]{2,1,0:T(4,128)S(1)}, f32[4,4,768]{2,1,0:T(4,128)S(1)}, u32[]{:S(2)}, u32[]{:S(2)}) %collective-permute-start.5) | collective-permute-done | bytes 49184 | tf_op jit(solution)/shard_map/ppermute | solution.py:264
  13.1 1.3 %collective-permute-start.6 = (f32[4,4,768]{2,1,0:T(4,128)S(1)}, f32[4,4,768]{2,1,0:T(4,128)S(1)}, u32[]{:S(2)}, u32[]{:S(2)}) collective-permute-start(f32[4,4,768]{2,1,0:T(4,128)S(1)} %add.3.own_ref), channel_id=1, source_target_pairs={{3,0},{2,1},{1,2},{0,3},{7,4},{6,5},{5,6},{4,7},{11,8},{10,9},{9,1... | collective-permute-start | bytes 147464 | tf_op jit(solution)/shard_map/ppermute | solution.py:271
  14.5 0.0 copy-done.1
  14.5 1.6 %arrange.1 = (f32[2,4,2,192]{3,2,1,0:T(2,128)}, bf16[2,768,1536]{2,1,0:T(8,128)(2,1)S(1)}) custom-call(f32[4,768]{1,0:T(4,128)S(1)} %get-tuple-element.18.total_ref, bf16[2,4,2,192,768]{4,3,2,1,0:T(8,128)(2,1)S(1)} %copy-done), custom_call_target="tpu_custom_call" | custom-call | tf_op jit(solution)/shard_map/arrange/pallas_call | solution.py:199
  16.1 0.8 %collective-permute-done.6.next_ref = f32[4,4,768]{2,1,0:T(4,128)S(1)} collective-permute-done((f32[4,4,768]{2,1,0:T(4,128)S(1)}, f32[4,4,768]{2,1,0:T(4,128)S(1)}, u32[]{:S(2)}, u32[]{:S(2)}) %collective-permute-start.6) | collective-permute-done | bytes 49184 | tf_op jit(solution)/shard_map/ppermute | solution.py:271
  16.9 1.4 %couple.1 = f32[2,4,2,192]{3,2,1,0:T(2,128)} custom-call(f32[4,4,768]{2,1,0:T(4,128)S(1)} %add.3.own_ref, f32[4,4,768]{2,1,0:T(4,128)S(1)} %collective-permute-done.6.next_ref, f32[4,5,768]{2,1,0:T(8,128)S(1)} %copy.6.spec, bf16[2,768,1536]{2,1,0:T(8,128)(2,1)S(1)} %get-tuple-element.21.beam), custom_call_target="tpu_custom_call" | custom-call | tf_op jit(solution)/shard_map/couple/pallas_call | solution.py:238
  (3 shorter events, 0.1 us)
Async XLA Ops:
  3.2 7.9 %copy-start = (bf16[2,4,2,192,768]{4,3,2,1,0:T(8,128)(2,1)S(1)}, bf16[2,4,2,192,768]{4,3,2,1,0:T(8,128)(2,1)}, u32[]{:S(2)}) copy-start(bf16[2,4,2,192,768]{4,3,2,1,0:T(8,128)(2,1)} %beam.1) | copy-start | bytes 14155780
  3.3 11.2 %copy-start.1 = (f32[4,5,768]{2,0,1:T(4,128)S(1)}, f32[4,5,768]{2,0,1:T(4,128)}, u32[]{:S(2)}) copy-start(f32[4,5,768]{2,0,1:T(4,128)} %param.6) | copy-start | bytes 184324
  3.3 6.8 %collective-permute-start = (f32[4,768]{1,0:T(4,128)S(1)}, f32[4,768]{1,0:T(4,128)S(1)}, u32[]{:S(2)}, u32[]{:S(2)}) collective-permute-start(f32[4,768]{1,0:T(4,128)S(1)} %get-tuple-element.13), channel_id=1, source_target_pairs={{0,4},{1,5},{4,12},{5,13},{8,9},{9,8},{12,0},{13,1},{2,6},{3,7},{6... | collective-permute-start | bytes 36872 | tf_op jit(solution)/shard_map/ppermute | solution.py:260
  6.3 4.6 %collective-permute-start.1 = (f32[4,768]{1,0:T(4,128)S(1)}, f32[4,768]{1,0:T(4,128)S(1)}, u32[]{:S(2)}, u32[]{:S(2)}) collective-permute-start(f32[4,768]{1,0:T(4,128)S(1)} %get-tuple-element.14), channel_id=1, source_target_pairs={{0,8},{1,9},{4,5},{5,4},{8,0},{9,1},{12,13},{13,12},{2,10},{3,11},... | collective-permute-start | bytes 36872 | tf_op jit(solution)/shard_map/ppermute | solution.py:260
  7.4 3.7 %collective-permute-start.2 = (f32[4,768]{1,0:T(4,128)S(1)}, f32[4,768]{1,0:T(4,128)S(1)}, u32[]{:S(2)}, u32[]{:S(2)}) collective-permute-start(f32[4,768]{1,0:T(4,128)S(1)} %get-tuple-element.15), channel_id=1, source_target_pairs={{0,12},{1,13},{4,0},{5,1},{8,9},{9,8},{12,4},{13,5},{2,14},{3,15},... | collective-permute-start | bytes 36872 | tf_op jit(solution)/shard_map/ppermute | solution.py:260
  8.5 2.6 %collective-permute-start.3 = (f32[4,768]{1,0:T(4,128)S(1)}, f32[4,768]{1,0:T(4,128)S(1)}, u32[]{:S(2)}, u32[]{:S(2)}) collective-permute-start(f32[4,768]{1,0:T(4,128)S(1)} %get-tuple-element.16), channel_id=1, source_target_pairs={{0,1},{1,0},{4,8},{5,9},{8,4},{9,5},{12,13},{13,12},{2,3},{3,2},{6... | collective-permute-start | bytes 36872 | tf_op jit(solution)/shard_map/ppermute | solution.py:260
  8.7 2.5 %collective-permute-start.4 = (f32[4,768]{1,0:T(4,128)S(1)}, f32[4,768]{1,0:T(4,128)S(1)}, u32[]{:S(2)}, u32[]{:S(2)}) collective-permute-start(f32[4,768]{1,0:T(4,128)S(1)} %get-tuple-element.17), channel_id=1, source_target_pairs={{0,1},{1,0},{4,5},{5,4},{8,12},{9,13},{12,8},{13,9},{2,3},{3,2},{6... | collective-permute-start | bytes 36872 | tf_op jit(solution)/shard_map/ppermute | solution.py:260
  11.8 1.3 %collective-permute-start.5 = (f32[4,4,768]{2,1,0:T(4,128)S(1)}, f32[4,4,768]{2,1,0:T(4,128)S(1)}, u32[]{:S(2)}, u32[]{:S(2)}) collective-permute-start(f32[4,4,768]{2,1,0:T(4,128)S(1)} %get-tuple-element.20), channel_id=1, source_target_pairs={{0,1},{1,0},{2,3},{3,2},{4,5},{5,4},{6,7},{7,6},{8,9},{9,8},{10,11... | collective-permute-start | bytes 147464 | tf_op jit(solution)/shard_map/ppermute | solution.py:264
  13.1 3.8 %collective-permute-start.6 = (f32[4,4,768]{2,1,0:T(4,128)S(1)}, f32[4,4,768]{2,1,0:T(4,128)S(1)}, u32[]{:S(2)}, u32[]{:S(2)}) collective-permute-start(f32[4,4,768]{2,1,0:T(4,128)S(1)} %add.3.own_ref), channel_id=1, source_target_pairs={{3,0},{2,1},{1,2},{0,3},{7,4},{6,5},{5,6},{4,7},{11,8},{10,9},{9,1... | collective-permute-start | bytes 147464 | tf_op jit(solution)/shard_map/ppermute | solution.py:271

commit v4 on v3

--- a/solution.py
+++ b/solution.py
@@ -54,7 +54,7 @@
     _, points, times = visibilities.shape
     total = m_orders.shape[0]
     per = total // size
-    width = 384
+    width = 256
     chunks = points // width
 
     def kernel(orders_ref, vis, *rest):
@@ -89,12 +89,15 @@
         for n in range(chunks):
             for copy in copies[n]:
                 copy.wait()
-            acc = None
+            acc, small = None, None
             for c in range(2):
                 high, low = split(held[c, n])
-                both = dot_last(lefts[c], jnp.concatenate([high, low], 0))
-                term = both[: 2 * total, :width] + both[2 * total :, :width] + both[: 2 * total, width:]
+                rest = dot_last(low, lefts[c][: 2 * total])
+                small = rest if small is None else small + rest
+                both = dot_last(lefts[c], high)
+                term = both[: 2 * total] + both[2 * total :]
                 acc = term if acc is None else acc + term
+            acc = acc + small.T
             for s in range(size):
                 for c in range(2):
                     first = c * total + s * per
@@ -209,13 +212,14 @@
     )(total, beams)
 
 
-def couple(own, following, spectra, turned_beams, modes):
+def couple(own, others, spectra, turned_beams, modes):
     blocks, rows, degrees = own.shape
     per = rows // 2
     wide = per * modes
 
-    def kernel(own_ref, next_ref, spec, beam, out):
-        summed = [own_ref[f] for f in range(blocks)] + [next_ref[f] for f in range(blocks)]
+    def kernel(own_ref, cross_ref, next_ref, pol_ref, spec, beam, out):
+        summed = [own_ref[f] + pol_ref[f] for f in range(blocks)]
+        summed += [next_ref[f] + cross_ref[f] for f in range(blocks)]
         plain, turned = [], []
         for f in range(blocks):
             mixed = None
@@ -238,11 +242,11 @@
     return pl.pallas_call(
         kernel,
         out_shape=jax.ShapeDtypeStruct((per, blocks, 2, modes), jnp.float32),
-        in_specs=[pl.BlockSpec(memory_space=pltpu.VMEM)] * 4,
+        in_specs=[pl.BlockSpec(memory_space=pltpu.VMEM)] * 6,
         out_specs=pl.BlockSpec(memory_space=pltpu.VMEM),
         compiler_params=pltpu.CompilerParams(vmem_limit_bytes=12 * MIB),
         name="couple",
-    )(own, following, spectra, turned_beams)
+    )(own, *others, spectra, turned_beams)
 
 
 def shards(visibilities, beams, spectra, m_orders):
@@ -261,16 +265,18 @@
     ]
     total, partial = project(arrived, beams)
 
-    other = lax.ppermute(partial, "pol", [(p, (p + 1) % pols) for p in range(pols)])
-    projected = partial + other
-    pairs = [
-        (((f + 1) % freqs) * pols + (p + 1) % pols, f * pols + p)
-        for f in range(freqs)
-        for p in range(pols)
-    ]
-    following = lax.ppermute(projected, ("freq", "pol"), pairs)
+    def fetch(freq_step, pol_step):
+        pairs = [
+            (((f + freq_step) % freqs) * pols + (p + pol_step) % pols, f * pols + p)
+            for f in range(freqs)
+            for p in range(pols)
+        ]
+        return lax.ppermute(partial, ("freq", "pol"), pairs)
+
+    cross, following, pol = fetch(1, 1), fetch(1, 0), fetch(0, 1)
+    others = [cross, following, pol]
     msdata, turned = arrange(total, beams)
-    return msdata, couple(projected, following, spectra, turned, modes)
+    return msdata, couple(partial, others, spectra, turned, modes)
 
 
 def solution(mesh):

time: 18.5 us -> 18.3 us (0.989)
  waiting for transfers between devices: 4.16 us -> 3.55 us
  starting transfers between devices: 7.14 us -> 7.67 us
    ppermute x2 -> x3, waiting for transfers between devices: 2.04 us -> 1.43 us  [fetch(): return lax.ppermute(partial, ('freq', 'pol'), pairs)]
    ppermute x2 -> x3, starting transfers between devices: 1.39 us -> 1.93 us  [fetch(): return lax.ppermute(partial, ('freq', 'pol'), pairs)]
  transfers between devices with their start and end apart: 7 -> 8, of which waited for: 5 -> 5; matrix products, arithmetic and copies ran while one was open for 0% -> 0% of each run, Pallas kernels for 9% -> 9%
where the time goes in v4:
time: 18.3 us; the launch traced here: 18.1 us
  starting transfers between devices  7.67 us (42%)
  Pallas kernels  6.2 us (34%)
  waiting for transfers between devices  3.55 us (19%)
  between operations  0.68 us (4%)
    ppermute x5, starting transfers between devices, shards(): lax.ppermute(part, ('wide', 'pol'), pairs_of(step, pols))  5.75 us
    pallas_call x1, Pallas kernels, transform(): pl.pallas_call(kernel, out_shape=jax.ShapeDtypeStruct((size, 2 * per, poi...  2.47 us
    ppermute x5, waiting for transfers between devices, shards(): lax.ppermute(part, ('wide', 'pol'), pairs_of(step, pols))  2.11 us
    ppermute x3, starting transfers between devices, fetch(): return lax.ppermute(partial, ('freq', 'pol'), pairs)  1.93 us
    pallas_call x1, Pallas kernels, arrange(): pl.pallas_call(kernel, out_shape=[jax.ShapeDtypeStruct((per, blocks, 2, m...  1.59 us
    pallas_call x1, Pallas kernels, couple(): pl.pallas_call(kernel, out_shape=jax.ShapeDtypeStruct((per, blocks, 2, mo...  1.44 us
    ppermute x3, waiting for transfers between devices, fetch(): return lax.ppermute(partial, ('freq', 'pol'), pairs)  1.43 us
    pallas_call x1, Pallas kernels, project(): pl.pallas_call(kernel, out_shape=[jax.ShapeDtypeStruct((2 * per, blocks *...  0.67 us
  transfers between devices with their start and end apart: 8, of which 5 were waited for; matrix products, arithmetic and copies ran while one was open for 0% of the time, Pallas kernels for 9%

profile of v4, /device:TPU:0, one launch (start us, length us, event | category | flops | bytes accessed | tf_op | source)
XLA Modules:
  0.0 18.1 jit_solution(6309755740255959893)
XLA Ops:
  0.6 2.5 %transform.1.sums_ref = f32[4,4,768]{2,1,0:T(4,128)S(1)} custom-call(s32[8]{0:T(128)} %orders_ref.1, f32[2,768,512]{2,1,0:T(8,128)} %bitcast.3), custom_call_target="tpu_custom_call" | custom-call | flops 4000000000 | bytes 8000000 | tf_op jit(solution)/shard_map/transform/pallas_call | solution.py:106
  3.1 0.0 copy-start
  3.2 0.0 copy-start.1
  3.2 3.1 %collective-permute-start = (f32[4,768]{1,0:T(4,128)S(1)}, f32[4,768]{1,0:T(4,128)S(1)}, u32[]{:S(2)}, u32[]{:S(2)}) collective-permute-start(f32[4,768]{1,0:T(4,128)S(1)} %get-tuple-element.13), channel_id=1, source_target_pairs={{0,4},{1,5},{4,12},{5,13},{8,9},{9,8},{12,0},{13,1},{2,6},{3,7},{6... | collective-permute-start | bytes 36872 | tf_op jit(solution)/shard_map/ppermute | solution.py:264
  6.2 1.1 %collective-permute-start.1 = (f32[4,768]{1,0:T(4,128)S(1)}, f32[4,768]{1,0:T(4,128)S(1)}, u32[]{:S(2)}, u32[]{:S(2)}) collective-permute-start(f32[4,768]{1,0:T(4,128)S(1)} %get-tuple-element.14), channel_id=1, source_target_pairs={{0,8},{1,9},{4,5},{5,4},{8,0},{9,1},{12,13},{13,12},{2,10},{3,11},... | collective-permute-start | bytes 36872 | tf_op jit(solution)/shard_map/ppermute | solution.py:264
  7.3 1.1 %collective-permute-start.2 = (f32[4,768]{1,0:T(4,128)S(1)}, f32[4,768]{1,0:T(4,128)S(1)}, u32[]{:S(2)}, u32[]{:S(2)}) collective-permute-start(f32[4,768]{1,0:T(4,128)S(1)} %get-tuple-element.15), channel_id=1, source_target_pairs={{0,12},{1,13},{4,0},{5,1},{8,9},{9,8},{12,4},{13,5},{2,14},{3,15},... | collective-permute-start | bytes 36872 | tf_op jit(solution)/shard_map/ppermute | solution.py:264
  8.4 0.2 collective-permute-start.3
  8.6 0.3 %collective-permute-start.4 = (f32[4,768]{1,0:T(4,128)S(1)}, f32[4,768]{1,0:T(4,128)S(1)}, u32[]{:S(2)}, u32[]{:S(2)}) collective-permute-start(f32[4,768]{1,0:T(4,128)S(1)} %get-tuple-element.17), channel_id=1, source_target_pairs={{0,1},{1,0},{4,5},{5,4},{8,12},{9,13},{12,8},{13,9},{2,3},{3,2},{6... | collective-permute-start | bytes 36872 | tf_op jit(solution)/shard_map/ppermute | solution.py:264
  8.9 1.0 %collective-permute-done.refs_1_ = f32[4,768]{1,0:T(4,128)S(1)} collective-permute-done((f32[4,768]{1,0:T(4,128)S(1)}, f32[4,768]{1,0:T(4,128)S(1)}, u32[]{:S(2)}, u32[]{:S(2)}) %collective-permute-start) | collective-permute-done | bytes 12320 | tf_op jit(solution)/shard_map/ppermute | solution.py:264
  9.9 0.9 %collective-permute-done.1.refs_2_ = f32[4,768]{1,0:T(4,128)S(1)} collective-permute-done((f32[4,768]{1,0:T(4,128)S(1)}, f32[4,768]{1,0:T(4,128)S(1)}, u32[]{:S(2)}, u32[]{:S(2)}) %collective-permute-start.1) | collective-permute-done | bytes 12320 | tf_op jit(solution)/shard_map/ppermute | solution.py:264
  10.8 0.2 %collective-permute-done.2.refs_3_ = f32[4,768]{1,0:T(4,128)S(1)} collective-permute-done((f32[4,768]{1,0:T(4,128)S(1)}, f32[4,768]{1,0:T(4,128)S(1)}, u32[]{:S(2)}, u32[]{:S(2)}) %collective-permute-start.2) | collective-permute-done | bytes 12320 | tf_op jit(solution)/shard_map/ppermute | solution.py:264
  11.0 0.0 collective-permute-done.3.refs_4_
  11.0 0.0 collective-permute-done.4.refs_5_
  11.0 0.0 copy-done
  11.0 0.7 %project.1 = (f32[4,768]{1,0:T(4,128)S(1)}, f32[4,4,768]{2,1,0:T(4,128)S(1)}) custom-call(f32[4,768]{1,0:T(4,128)S(1)} %get-tuple-element.12.refs_0_, f32[4,768]{1,0:T(4,128)S(1)} %collective-permute-done.refs_1_, f32[4,768]{1,0:T(4,128)S(1)} %collective-permute-done.1.refs_2_, f32[4,768]{1,0:T(4,128)S(1)} %collective-permute-done.2.refs_3_, ...), custom_call_target="tpu_custom_call" | custom-call | tf_op jit(solution)/shard_map/project/pallas_call | solution.py:174
  11.7 0.4 %collective-permute-start.5 = (f32[4,4,768]{2,1,0:T(4,128)S(1)}, f32[4,4,768]{2,1,0:T(4,128)S(1)}, u32[]{:S(2)}, u32[]{:S(2)}) collective-permute-start(f32[4,4,768]{2,1,0:T(4,128)S(1)} %get-tuple-element.20.own_ref), channel_id=1, source_target_pairs={{3,0},{2,1},{1,2},{0,3},{7,4},{6,5},{5,6},{4,7},{11,8},{10,9},{9,1... | collective-permute-start | bytes 147464 | tf_op jit(solution)/shard_map/ppermute | solution.py:274
  12.1 1.2 %collective-permute-start.6 = (f32[4,4,768]{2,1,0:T(4,128)S(1)}, f32[4,4,768]{2,1,0:T(4,128)S(1)}, u32[]{:S(2)}, u32[]{:S(2)}) collective-permute-start(f32[4,4,768]{2,1,0:T(4,128)S(1)} %get-tuple-element.20.own_ref), channel_id=1, source_target_pairs={{2,0},{3,1},{0,2},{1,3},{6,4},{7,5},{4,6},{5,7},{10,8},{11,9},{8,1... | collective-permute-start | bytes 147464 | tf_op jit(solution)/shard_map/ppermute | solution.py:274
  13.4 0.3 %collective-permute-start.7 = (f32[4,4,768]{2,1,0:T(4,128)S(1)}, f32[4,4,768]{2,1,0:T(4,128)S(1)}, u32[]{:S(2)}, u32[]{:S(2)}) collective-permute-start(f32[4,4,768]{2,1,0:T(4,128)S(1)} %get-tuple-element.20.own_ref), channel_id=1, source_target_pairs={{1,0},{0,1},{3,2},{2,3},{5,4},{4,5},{7,6},{6,7},{9,8},{8,9},{11,10... | collective-permute-start | bytes 147464 | tf_op jit(solution)/shard_map/ppermute | solution.py:274
  13.6 0.0 copy-done.1
  13.7 1.6 %arrange.1 = (f32[2,4,2,192]{3,2,1,0:T(2,128)}, bf16[2,768,1536]{2,1,0:T(8,128)(2,1)S(1)}) custom-call(f32[4,768]{1,0:T(4,128)S(1)} %get-tuple-element.18.total_ref, bf16[2,4,2,192,768]{4,3,2,1,0:T(8,128)(2,1)S(1)} %copy-done), custom_call_target="tpu_custom_call" | custom-call | tf_op jit(solution)/shard_map/arrange/pallas_call | solution.py:202
  15.3 0.5 %collective-permute-done.5.cross_ref = f32[4,4,768]{2,1,0:T(4,128)S(1)} collective-permute-done((f32[4,4,768]{2,1,0:T(4,128)S(1)}, f32[4,4,768]{2,1,0:T(4,128)S(1)}, u32[]{:S(2)}, u32[]{:S(2)}) %collective-permute-start.5) | collective-permute-done | bytes 49184 | tf_op jit(solution)/shard_map/ppermute | solution.py:274
  15.8 0.9 %collective-permute-done.6.next_ref = f32[4,4,768]{2,1,0:T(4,128)S(1)} collective-permute-done((f32[4,4,768]{2,1,0:T(4,128)S(1)}, f32[4,4,768]{2,1,0:T(4,128)S(1)}, u32[]{:S(2)}, u32[]{:S(2)}) %collective-permute-start.6) | collective-permute-done | bytes 49184 | tf_op jit(solution)/shard_map/ppermute | solution.py:274
  16.7 0.0 collective-permute-done.7.pol_ref
  16.7 1.4 %couple.1 = f32[2,4,2,192]{3,2,1,0:T(2,128)} custom-call(f32[4,4,768]{2,1,0:T(4,128)S(1)} %get-tuple-element.20.own_ref, f32[4,4,768]{2,1,0:T(4,128)S(1)} %collective-permute-done.5.cross_ref, f32[4,4,768]{2,1,0:T(4,128)S(1)} %collective-permute-done.6.next_ref, f32[4,4,768]{2,1,0:T(4,128)S(1)} %collective-permute-done.7.pol_ref, ...), custom_call_target="tpu_custom_call" | custom-call | tf_op jit(solution)/shard_map/couple/pallas_call | solution.py:242
  (2 shorter events, 0.1 us)
Async XLA Ops:
  3.1 7.9 %copy-start = (bf16[2,4,2,192,768]{4,3,2,1,0:T(8,128)(2,1)S(1)}, bf16[2,4,2,192,768]{4,3,2,1,0:T(8,128)(2,1)}, u32[]{:S(2)}) copy-start(bf16[2,4,2,192,768]{4,3,2,1,0:T(8,128)(2,1)} %beam.1) | copy-start | bytes 14155780
  3.2 10.5 %copy-start.1 = (f32[4,5,768]{2,0,1:T(4,128)S(1)}, f32[4,5,768]{2,0,1:T(4,128)}, u32[]{:S(2)}) copy-start(f32[4,5,768]{2,0,1:T(4,128)} %param.6) | copy-start | bytes 184324
  3.2 6.8 %collective-permute-start = (f32[4,768]{1,0:T(4,128)S(1)}, f32[4,768]{1,0:T(4,128)S(1)}, u32[]{:S(2)}, u32[]{:S(2)}) collective-permute-start(f32[4,768]{1,0:T(4,128)S(1)} %get-tuple-element.13), channel_id=1, source_target_pairs={{0,4},{1,5},{4,12},{5,13},{8,9},{9,8},{12,0},{13,1},{2,6},{3,7},{6... | collective-permute-start | bytes 36872 | tf_op jit(solution)/shard_map/ppermute | solution.py:264
  6.2 4.6 %collective-permute-start.1 = (f32[4,768]{1,0:T(4,128)S(1)}, f32[4,768]{1,0:T(4,128)S(1)}, u32[]{:S(2)}, u32[]{:S(2)}) collective-permute-start(f32[4,768]{1,0:T(4,128)S(1)} %get-tuple-element.14), channel_id=1, source_target_pairs={{0,8},{1,9},{4,5},{5,4},{8,0},{9,1},{12,13},{13,12},{2,10},{3,11},... | collective-permute-start | bytes 36872 | tf_op jit(solution)/shard_map/ppermute | solution.py:264
  7.3 3.7 %collective-permute-start.2 = (f32[4,768]{1,0:T(4,128)S(1)}, f32[4,768]{1,0:T(4,128)S(1)}, u32[]{:S(2)}, u32[]{:S(2)}) collective-permute-start(f32[4,768]{1,0:T(4,128)S(1)} %get-tuple-element.15), channel_id=1, source_target_pairs={{0,12},{1,13},{4,0},{5,1},{8,9},{9,8},{12,4},{13,5},{2,14},{3,15},... | collective-permute-start | bytes 36872 | tf_op jit(solution)/shard_map/ppermute | solution.py:264
  8.4 2.6 %collective-permute-start.3 = (f32[4,768]{1,0:T(4,128)S(1)}, f32[4,768]{1,0:T(4,128)S(1)}, u32[]{:S(2)}, u32[]{:S(2)}) collective-permute-start(f32[4,768]{1,0:T(4,128)S(1)} %get-tuple-element.16), channel_id=1, source_target_pairs={{0,1},{1,0},{4,8},{5,9},{8,4},{9,5},{12,13},{13,12},{2,3},{3,2},{6... | collective-permute-start | bytes 36872 | tf_op jit(solution)/shard_map/ppermute | solution.py:264
  8.6 2.5 %collective-permute-start.4 = (f32[4,768]{1,0:T(4,128)S(1)}, f32[4,768]{1,0:T(4,128)S(1)}, u32[]{:S(2)}, u32[]{:S(2)}) collective-permute-start(f32[4,768]{1,0:T(4,128)S(1)} %get-tuple-element.17), channel_id=1, source_target_pairs={{0,1},{1,0},{4,5},{5,4},{8,12},{9,13},{12,8},{13,9},{2,3},{3,2},{6... | collective-permute-start | bytes 36872 | tf_op jit(solution)/shard_map/ppermute | solution.py:264
  11.7 4.1 %collective-permute-start.5 = (f32[4,4,768]{2,1,0:T(4,128)S(1)}, f32[4,4,768]{2,1,0:T(4,128)S(1)}, u32[]{:S(2)}, u32[]{:S(2)}) collective-permute-start(f32[4,4,768]{2,1,0:T(4,128)S(1)} %get-tuple-element.20.own_ref), channel_id=1, source_target_pairs={{3,0},{2,1},{1,2},{0,3},{7,4},{6,5},{5,6},{4,7},{11,8},{10,9},{9,1... | collective-permute-start | bytes 147464 | tf_op jit(solution)/shard_map/ppermute | solution.py:274
  12.1 4.6 %collective-permute-start.6 = (f32[4,4,768]{2,1,0:T(4,128)S(1)}, f32[4,4,768]{2,1,0:T(4,128)S(1)}, u32[]{:S(2)}, u32[]{:S(2)}) collective-permute-start(f32[4,4,768]{2,1,0:T(4,128)S(1)} %get-tuple-element.20.own_ref), channel_id=1, source_target_pairs={{2,0},{3,1},{0,2},{1,3},{6,4},{7,5},{4,6},{5,7},{10,8},{11,9},{8,1... | collective-permute-start | bytes 147464 | tf_op jit(solution)/shard_map/ppermute | solution.py:274
  13.4 3.3 %collective-permute-start.7 = (f32[4,4,768]{2,1,0:T(4,128)S(1)}, f32[4,4,768]{2,1,0:T(4,128)S(1)}, u32[]{:S(2)}, u32[]{:S(2)}) collective-permute-start(f32[4,4,768]{2,1,0:T(4,128)S(1)} %get-tuple-element.20.own_ref), channel_id=1, source_target_pairs={{1,0},{0,1},{3,2},{2,3},{5,4},{4,5},{7,6},{6,7},{9,8},{8,9},{11,10... | collective-permute-start | bytes 147464 | tf_op jit(solution)/shard_map/ppermute | solution.py:274

commit v5 on v4

--- a/solution.py
+++ b/solution.py
@@ -86,6 +86,7 @@
             table = jnp.concatenate([cosine, -sine] if c == 0 else [sine, cosine], 0)
             high, low = split(table)
             lefts.append(jnp.concatenate([high, low], 0))
+        sums = []
         for n in range(chunks):
             for copy in copies[n]:
                 copy.wait()
@@ -97,7 +98,9 @@
                 both = dot_last(lefts[c], high)
                 term = both[: 2 * total] + both[2 * total :]
                 acc = term if acc is None else acc + term
-            acc = acc + small.T
+            sums.append((acc, small))
+        for n in range(chunks):
+            acc = sums[n][0] + sums[n][1].T
             for s in range(size):
                 for c in range(2):
                     first = c * total + s * per

time: 18.3 us -> 18.2 us (level)
  no operation moved by 1% of the time
where the time goes in v5:
time: 18.2 us; the launch traced here: 18.1 us
  starting transfers between devices  7.67 us (42%)
  Pallas kernels  6.17 us (34%)
  waiting for transfers between devices  3.54 us (19%)
  between operations  0.68 us (4%)
    ppermute x5, starting transfers between devices, shards(): lax.ppermute(part, ('wide', 'pol'), pairs_of(step, pols))  5.74 us
    pallas_call x1, Pallas kernels, transform(): pl.pallas_call(kernel, out_shape=jax.ShapeDtypeStruct((size, 2 * per, poi...  2.44 us
    ppermute x5, waiting for transfers between devices, shards(): lax.ppermute(part, ('wide', 'pol'), pairs_of(step, pols))  2.11 us
    ppermute x3, starting transfers between devices, fetch(): return lax.ppermute(partial, ('freq', 'pol'), pairs)  1.93 us
    pallas_call x1, Pallas kernels, arrange(): pl.pallas_call(kernel, out_shape=[jax.ShapeDtypeStruct((per, blocks, 2, m...  1.59 us
    pallas_call x1, Pallas kernels, couple(): pl.pallas_call(kernel, out_shape=jax.ShapeDtypeStruct((per, blocks, 2, mo...  1.44 us
    ppermute x3, waiting for transfers between devices, fetch(): return lax.ppermute(partial, ('freq', 'pol'), pairs)  1.43 us
    pallas_call x1, Pallas kernels, project(): pl.pallas_call(kernel, out_shape=[jax.ShapeDtypeStruct((2 * per, blocks *...  0.67 us
  transfers between devices with their start and end apart: 8, of which 5 were waited for; matrix products, arithmetic and copies ran while one was open for 0% of the time, Pallas kernels for 9%

profile of v5, /device:TPU:0, one launch (start us, length us, event | category | flops | bytes accessed | tf_op | source)
XLA Modules:
  0.0 18.1 jit_solution(5318973356106425097)
XLA Ops:
  0.6 2.4 %transform.1.sums_ref = f32[4,4,768]{2,1,0:T(4,128)S(1)} custom-call(s32[8]{0:T(128)} %orders_ref.1, f32[2,768,512]{2,1,0:T(8,128)} %bitcast.3), custom_call_target="tpu_custom_call" | custom-call | flops 4000000000 | bytes 8000000 | tf_op jit(solution)/shard_map/transform/pallas_call | solution.py:109
  3.1 0.0 copy-start
  3.1 0.0 copy-start.1
  3.1 3.1 %collective-permute-start = (f32[4,768]{1,0:T(4,128)S(1)}, f32[4,768]{1,0:T(4,128)S(1)}, u32[]{:S(2)}, u32[]{:S(2)}) collective-permute-start(f32[4,768]{1,0:T(4,128)S(1)} %get-tuple-element.13), channel_id=1, source_target_pairs={{0,4},{1,5},{4,12},{5,13},{8,9},{9,8},{12,0},{13,1},{2,6},{3,7},{6... | collective-permute-start | bytes 36872 | tf_op jit(solution)/shard_map/ppermute | solution.py:267
  6.2 1.1 %collective-permute-start.1 = (f32[4,768]{1,0:T(4,128)S(1)}, f32[4,768]{1,0:T(4,128)S(1)}, u32[]{:S(2)}, u32[]{:S(2)}) collective-permute-start(f32[4,768]{1,0:T(4,128)S(1)} %get-tuple-element.14), channel_id=1, source_target_pairs={{0,8},{1,9},{4,5},{5,4},{8,0},{9,1},{12,13},{13,12},{2,10},{3,11},... | collective-permute-start | bytes 36872 | tf_op jit(solution)/shard_map/ppermute | solution.py:267
  7.3 1.1 %collective-permute-start.2 = (f32[4,768]{1,0:T(4,128)S(1)}, f32[4,768]{1,0:T(4,128)S(1)}, u32[]{:S(2)}, u32[]{:S(2)}) collective-permute-start(f32[4,768]{1,0:T(4,128)S(1)} %get-tuple-element.15), channel_id=1, source_target_pairs={{0,12},{1,13},{4,0},{5,1},{8,9},{9,8},{12,4},{13,5},{2,14},{3,15},... | collective-permute-start | bytes 36872 | tf_op jit(solution)/shard_map/ppermute | solution.py:267
  8.4 0.2 collective-permute-start.3
  8.5 0.3 %collective-permute-start.4 = (f32[4,768]{1,0:T(4,128)S(1)}, f32[4,768]{1,0:T(4,128)S(1)}, u32[]{:S(2)}, u32[]{:S(2)}) collective-permute-start(f32[4,768]{1,0:T(4,128)S(1)} %get-tuple-element.17), channel_id=1, source_target_pairs={{0,1},{1,0},{4,5},{5,4},{8,12},{9,13},{12,8},{13,9},{2,3},{3,2},{6... | collective-permute-start | bytes 36872 | tf_op jit(solution)/shard_map/ppermute | solution.py:267
  8.9 1.0 %collective-permute-done.refs_1_ = f32[4,768]{1,0:T(4,128)S(1)} collective-permute-done((f32[4,768]{1,0:T(4,128)S(1)}, f32[4,768]{1,0:T(4,128)S(1)}, u32[]{:S(2)}, u32[]{:S(2)}) %collective-permute-start) | collective-permute-done | bytes 12320 | tf_op jit(solution)/shard_map/ppermute | solution.py:267
  9.9 0.9 %collective-permute-done.1.refs_2_ = f32[4,768]{1,0:T(4,128)S(1)} collective-permute-done((f32[4,768]{1,0:T(4,128)S(1)}, f32[4,768]{1,0:T(4,128)S(1)}, u32[]{:S(2)}, u32[]{:S(2)}) %collective-permute-start.1) | collective-permute-done | bytes 12320 | tf_op jit(solution)/shard_map/ppermute | solution.py:267
  10.8 0.2 %collective-permute-done.2.refs_3_ = f32[4,768]{1,0:T(4,128)S(1)} collective-permute-done((f32[4,768]{1,0:T(4,128)S(1)}, f32[4,768]{1,0:T(4,128)S(1)}, u32[]{:S(2)}, u32[]{:S(2)}) %collective-permute-start.2) | collective-permute-done | bytes 12320 | tf_op jit(solution)/shard_map/ppermute | solution.py:267
  11.0 0.0 collective-permute-done.3.refs_4_
  11.0 0.0 collective-permute-done.4.refs_5_
  11.0 0.0 copy-done
  11.0 0.7 %project.1 = (f32[4,768]{1,0:T(4,128)S(1)}, f32[4,4,768]{2,1,0:T(4,128)S(1)}) custom-call(f32[4,768]{1,0:T(4,128)S(1)} %get-tuple-element.12.refs_0_, f32[4,768]{1,0:T(4,128)S(1)} %collective-permute-done.refs_1_, f32[4,768]{1,0:T(4,128)S(1)} %collective-permute-done.1.refs_2_, f32[4,768]{1,0:T(4,128)S(1)} %collective-permute-done.2.refs_3_, ...), custom_call_target="tpu_custom_call" | custom-call | tf_op jit(solution)/shard_map/project/pallas_call | solution.py:177
  11.7 0.4 %collective-permute-start.5 = (f32[4,4,768]{2,1,0:T(4,128)S(1)}, f32[4,4,768]{2,1,0:T(4,128)S(1)}, u32[]{:S(2)}, u32[]{:S(2)}) collective-permute-start(f32[4,4,768]{2,1,0:T(4,128)S(1)} %get-tuple-element.20.own_ref), channel_id=1, source_target_pairs={{3,0},{2,1},{1,2},{0,3},{7,4},{6,5},{5,6},{4,7},{11,8},{10,9},{9,1... | collective-permute-start | bytes 147464 | tf_op jit(solution)/shard_map/ppermute | solution.py:277
  12.1 1.2 %collective-permute-start.6 = (f32[4,4,768]{2,1,0:T(4,128)S(1)}, f32[4,4,768]{2,1,0:T(4,128)S(1)}, u32[]{:S(2)}, u32[]{:S(2)}) collective-permute-start(f32[4,4,768]{2,1,0:T(4,128)S(1)} %get-tuple-element.20.own_ref), channel_id=1, source_target_pairs={{2,0},{3,1},{0,2},{1,3},{6,4},{7,5},{4,6},{5,7},{10,8},{11,9},{8,1... | collective-permute-start | bytes 147464 | tf_op jit(solution)/shard_map/ppermute | solution.py:277
  13.3 0.3 %collective-permute-start.7 = (f32[4,4,768]{2,1,0:T(4,128)S(1)}, f32[4,4,768]{2,1,0:T(4,128)S(1)}, u32[]{:S(2)}, u32[]{:S(2)}) collective-permute-start(f32[4,4,768]{2,1,0:T(4,128)S(1)} %get-tuple-element.20.own_ref), channel_id=1, source_target_pairs={{1,0},{0,1},{3,2},{2,3},{5,4},{4,5},{7,6},{6,7},{9,8},{8,9},{11,10... | collective-permute-start | bytes 147464 | tf_op jit(solution)/shard_map/ppermute | solution.py:277
  13.6 0.0 copy-done.1
  13.6 1.6 %arrange.1 = (f32[2,4,2,192]{3,2,1,0:T(2,128)}, bf16[2,768,1536]{2,1,0:T(8,128)(2,1)S(1)}) custom-call(f32[4,768]{1,0:T(4,128)S(1)} %get-tuple-element.18.total_ref, bf16[2,4,2,192,768]{4,3,2,1,0:T(8,128)(2,1)S(1)} %copy-done), custom_call_target="tpu_custom_call" | custom-call | tf_op jit(solution)/shard_map/arrange/pallas_call | solution.py:205
  15.2 0.5 %collective-permute-done.5.cross_ref = f32[4,4,768]{2,1,0:T(4,128)S(1)} collective-permute-done((f32[4,4,768]{2,1,0:T(4,128)S(1)}, f32[4,4,768]{2,1,0:T(4,128)S(1)}, u32[]{:S(2)}, u32[]{:S(2)}) %collective-permute-start.5) | collective-permute-done | bytes 49184 | tf_op jit(solution)/shard_map/ppermute | solution.py:277
  15.7 0.9 %collective-permute-done.6.next_ref = f32[4,4,768]{2,1,0:T(4,128)S(1)} collective-permute-done((f32[4,4,768]{2,1,0:T(4,128)S(1)}, f32[4,4,768]{2,1,0:T(4,128)S(1)}, u32[]{:S(2)}, u32[]{:S(2)}) %collective-permute-start.6) | collective-permute-done | bytes 49184 | tf_op jit(solution)/shard_map/ppermute | solution.py:277
  16.7 0.0 collective-permute-done.7.pol_ref
  16.7 1.4 %couple.1 = f32[2,4,2,192]{3,2,1,0:T(2,128)} custom-call(f32[4,4,768]{2,1,0:T(4,128)S(1)} %get-tuple-element.20.own_ref, f32[4,4,768]{2,1,0:T(4,128)S(1)} %collective-permute-done.5.cross_ref, f32[4,4,768]{2,1,0:T(4,128)S(1)} %collective-permute-done.6.next_ref, f32[4,4,768]{2,1,0:T(4,128)S(1)} %collective-permute-done.7.pol_ref, ...), custom_call_target="tpu_custom_call" | custom-call | tf_op jit(solution)/shard_map/couple/pallas_call | solution.py:245
  (2 shorter events, 0.1 us)
Async XLA Ops:
  3.1 7.9 %copy-start = (bf16[2,4,2,192,768]{4,3,2,1,0:T(8,128)(2,1)S(1)}, bf16[2,4,2,192,768]{4,3,2,1,0:T(8,128)(2,1)}, u32[]{:S(2)}) copy-start(bf16[2,4,2,192,768]{4,3,2,1,0:T(8,128)(2,1)} %beam.1) | copy-start | bytes 14155780
  3.1 10.5 %copy-start.1 = (f32[4,5,768]{2,0,1:T(4,128)S(1)}, f32[4,5,768]{2,0,1:T(4,128)}, u32[]{:S(2)}) copy-start(f32[4,5,768]{2,0,1:T(4,128)} %param.6) | copy-start | bytes 184324
  3.1 6.8 %collective-permute-start = (f32[4,768]{1,0:T(4,128)S(1)}, f32[4,768]{1,0:T(4,128)S(1)}, u32[]{:S(2)}, u32[]{:S(2)}) collective-permute-start(f32[4,768]{1,0:T(4,128)S(1)} %get-tuple-element.13), channel_id=1, source_target_pairs={{0,4},{1,5},{4,12},{5,13},{8,9},{9,8},{12,0},{13,1},{2,6},{3,7},{6... | collective-permute-start | bytes 36872 | tf_op jit(solution)/shard_map/ppermute | solution.py:267
  6.2 4.6 %collective-permute-start.1 = (f32[4,768]{1,0:T(4,128)S(1)}, f32[4,768]{1,0:T(4,128)S(1)}, u32[]{:S(2)}, u32[]{:S(2)}) collective-permute-start(f32[4,768]{1,0:T(4,128)S(1)} %get-tuple-element.14), channel_id=1, source_target_pairs={{0,8},{1,9},{4,5},{5,4},{8,0},{9,1},{12,13},{13,12},{2,10},{3,11},... | collective-permute-start | bytes 36872 | tf_op jit(solution)/shard_map/ppermute | solution.py:267
  7.3 3.7 %collective-permute-start.2 = (f32[4,768]{1,0:T(4,128)S(1)}, f32[4,768]{1,0:T(4,128)S(1)}, u32[]{:S(2)}, u32[]{:S(2)}) collective-permute-start(f32[4,768]{1,0:T(4,128)S(1)} %get-tuple-element.15), channel_id=1, source_target_pairs={{0,12},{1,13},{4,0},{5,1},{8,9},{9,8},{12,4},{13,5},{2,14},{3,15},... | collective-permute-start | bytes 36872 | tf_op jit(solution)/shard_map/ppermute | solution.py:267
  8.4 2.6 %collective-permute-start.3 = (f32[4,768]{1,0:T(4,128)S(1)}, f32[4,768]{1,0:T(4,128)S(1)}, u32[]{:S(2)}, u32[]{:S(2)}) collective-permute-start(f32[4,768]{1,0:T(4,128)S(1)} %get-tuple-element.16), channel_id=1, source_target_pairs={{0,1},{1,0},{4,8},{5,9},{8,4},{9,5},{12,13},{13,12},{2,3},{3,2},{6... | collective-permute-start | bytes 36872 | tf_op jit(solution)/shard_map/ppermute | solution.py:267
  8.5 2.5 %collective-permute-start.4 = (f32[4,768]{1,0:T(4,128)S(1)}, f32[4,768]{1,0:T(4,128)S(1)}, u32[]{:S(2)}, u32[]{:S(2)}) collective-permute-start(f32[4,768]{1,0:T(4,128)S(1)} %get-tuple-element.17), channel_id=1, source_target_pairs={{0,1},{1,0},{4,5},{5,4},{8,12},{9,13},{12,8},{13,9},{2,3},{3,2},{6... | collective-permute-start | bytes 36872 | tf_op jit(solution)/shard_map/ppermute | solution.py:267
  11.7 4.1 %collective-permute-start.5 = (f32[4,4,768]{2,1,0:T(4,128)S(1)}, f32[4,4,768]{2,1,0:T(4,128)S(1)}, u32[]{:S(2)}, u32[]{:S(2)}) collective-permute-start(f32[4,4,768]{2,1,0:T(4,128)S(1)} %get-tuple-element.20.own_ref), channel_id=1, source_target_pairs={{3,0},{2,1},{1,2},{0,3},{7,4},{6,5},{5,6},{4,7},{11,8},{10,9},{9,1... | collective-permute-start | bytes 147464 | tf_op jit(solution)/shard_map/ppermute | solution.py:277
  12.1 4.6 %collective-permute-start.6 = (f32[4,4,768]{2,1,0:T(4,128)S(1)}, f32[4,4,768]{2,1,0:T(4,128)S(1)}, u32[]{:S(2)}, u32[]{:S(2)}) collective-permute-start(f32[4,4,768]{2,1,0:T(4,128)S(1)} %get-tuple-element.20.own_ref), channel_id=1, source_target_pairs={{2,0},{3,1},{0,2},{1,3},{6,4},{7,5},{4,6},{5,7},{10,8},{11,9},{8,1... | collective-permute-start | bytes 147464 | tf_op jit(solution)/shard_map/ppermute | solution.py:277
  13.3 3.3 %collective-permute-start.7 = (f32[4,4,768]{2,1,0:T(4,128)S(1)}, f32[4,4,768]{2,1,0:T(4,128)S(1)}, u32[]{:S(2)}, u32[]{:S(2)}) collective-permute-start(f32[4,4,768]{2,1,0:T(4,128)S(1)} %get-tuple-element.20.own_ref), channel_id=1, source_target_pairs={{1,0},{0,1},{3,2},{2,3},{5,4},{4,5},{7,6},{6,7},{9,8},{8,9},{11,10... | collective-permute-start | bytes 147464 | tf_op jit(solution)/shard_map/ppermute | solution.py:277

commit v6 on v5

--- a/solution.py
+++ b/solution.py
@@ -187,32 +187,44 @@
     )(*parts, beams)
 
 
-def arrange(total, beams):
-    per, blocks, _, modes, degrees = beams.shape
-    wide = per * modes
-
-    def kernel(total_ref, beam, out, turned):
+def arrange(total, per, blocks, modes):
+    def kernel(total_ref, out):
         total_now = total_ref[...]
         for f in range(blocks):
             block = total_now[:, f * modes : (f + 1) * modes]
             for r in range(per):
                 for c in range(2):
                     out[r, f, c : c + 1, :] = block[c * per + r : c * per + r + 1]
+
+    return pl.pallas_call(
+        kernel,
+        out_shape=jax.ShapeDtypeStruct((per, blocks, 2, modes), jnp.float32),
+        in_specs=[pl.BlockSpec(memory_space=pltpu.VMEM)],
+        out_specs=pl.BlockSpec(memory_space=pltpu.VMEM),
+        compiler_params=pltpu.CompilerParams(vmem_limit_bytes=4 * MIB),
+        name="arrange",
+    )(total)
+
+
+def turn(beams):
+    per, blocks, _, modes, degrees = beams.shape
+    wide = per * modes
+
+    def kernel(beam, turned):
+        for f in range(blocks):
             for c in range(2):
                 both = jnp.concatenate([beam[r, f, c] for r in range(per)], 0)
                 turned[c, :, f * wide : (f + 1) * wide] = both.T
 
     return pl.pallas_call(
         kernel,
-        out_shape=[
-            jax.ShapeDtypeStruct((per, blocks, 2, modes), jnp.float32),
-            jax.ShapeDtypeStruct((2, degrees, blocks * wide), jnp.bfloat16),
-        ],
-        in_specs=[pl.BlockSpec(memory_space=pltpu.VMEM)] * 2,
-        out_specs=[pl.BlockSpec(memory_space=pltpu.VMEM)] * 2,
+        out_shape=jax.ShapeDtypeStruct((2, degrees, blocks * wide), jnp.bfloat16),
+        in_specs=[pl.BlockSpec(memory_space=pltpu.VMEM)],
+        out_specs=pl.BlockSpec(memory_space=pltpu.VMEM),
         compiler_params=pltpu.CompilerParams(vmem_limit_bytes=16 * MIB),
-        name="arrange",
-    )(total, beams)
+        cost_estimate=pl.CostEstimate(flops=10**9, bytes_accessed=10**7, transcendentals=0),
+        name="turn",
+    )(beams)
 
 
 def couple(own, others, spectra, turned_beams, modes):
@@ -278,7 +290,7 @@
 
     cross, following, pol = fetch(1, 1), fetch(1, 0), fetch(0, 1)
     others = [cross, following, pol]
-    msdata, turned = arrange(total, beams)
+    msdata, turned = arrange(total, per, blocks, modes), turn(beams)
     return msdata, couple(partial, others, spectra, turned, modes)
 
 

time: 18.2 us -> 18.2 us (level)
  waiting for transfers between devices: 3.54 us -> 3.18 us
  Pallas kernels: 6.17 us -> 6.52 us
    pallas_call x1 -> x2, Pallas kernels: 1.59 us -> 1.95 us  [the longest x1 1.26 us: turn(): pl.pallas_call(kernel, out_shape=jax.ShapeDtypeStruct((2, degrees, blocks...]
    ppermute x3, waiting for transfers between devices: 1.43 us -> 1.1 us  [fetch(): return lax.ppermute(partial, ('freq', 'pol'), pairs)]
  transfers between devices with their start and end apart: 8 -> 8, of which waited for: 5 -> 5; matrix products, arithmetic and copies ran while one was open for 0% -> 0% of each run, Pallas kernels for 9% -> 11%
where the time goes in v6:
time: 18.2 us; the launch traced here: 18.1 us
  starting transfers between devices  7.67 us (42%)
  Pallas kernels  6.52 us (36%)
  waiting for transfers between devices  3.18 us (17%)
  between operations  0.68 us (4%)
    ppermute x5, starting transfers between devices, shards(): lax.ppermute(part, ('wide', 'pol'), pairs_of(step, pols))  5.74 us
    pallas_call x1, Pallas kernels, transform(): pl.pallas_call(kernel, out_shape=jax.ShapeDtypeStruct((size, 2 * per, poi...  2.44 us
    ppermute x5, waiting for transfers between devices, shards(): lax.ppermute(part, ('wide', 'pol'), pairs_of(step, pols))  2.09 us
    ppermute x3, starting transfers between devices, fetch(): return lax.ppermute(partial, ('freq', 'pol'), pairs)  1.93 us
    pallas_call x1, Pallas kernels, couple(): pl.pallas_call(kernel, out_shape=jax.ShapeDtypeStruct((per, blocks, 2, mo...  1.43 us
    pallas_call x1, Pallas kernels, turn(): pl.pallas_call(kernel, out_shape=jax.ShapeDtypeStruct((2, degrees, blocks...  1.26 us
    ppermute x3, waiting for transfers between devices, fetch(): return lax.ppermute(partial, ('freq', 'pol'), pairs)  1.1 us
    pallas_call x1, Pallas kernels, arrange(): pl.pallas_call(kernel, out_shape=jax.ShapeDtypeStruct((per, blocks, 2, mo...  0.68 us
  transfers between devices with their start and end apart: 8, of which 5 were waited for; matrix products, arithmetic and copies ran while one was open for 0% of the time, Pallas kernels for 11%

profile of v6, /device:TPU:0, one launch (start us, length us, event | category | flops | bytes accessed | tf_op | source)
XLA Modules:
  0.0 18.1 jit_solution(13449373300088465261)
XLA Ops:
  0.6 2.4 %transform.1.sums_ref = f32[4,4,768]{2,1,0:T(4,128)S(1)} custom-call(s32[8]{0:T(128)} %orders_ref.1, f32[2,768,512]{2,1,0:T(8,128)} %bitcast.3), custom_call_target="tpu_custom_call" | custom-call | flops 4000000000 | bytes 8000000 | tf_op jit(solution)/shard_map/transform/pallas_call | solution.py:109
  3.1 0.0 copy-start.1
  3.1 0.0 copy-start
  3.1 3.1 %collective-permute-start = (f32[4,768]{1,0:T(4,128)S(1)}, f32[4,768]{1,0:T(4,128)S(1)}, u32[]{:S(2)}, u32[]{:S(2)}) collective-permute-start(f32[4,768]{1,0:T(4,128)S(1)} %get-tuple-element.11), channel_id=1, source_target_pairs={{0,4},{1,5},{4,12},{5,13},{8,9},{9,8},{12,0},{13,1},{2,6},{3,7},{6... | collective-permute-start | bytes 36872 | tf_op jit(solution)/shard_map/ppermute | solution.py:279
  6.2 1.1 %collective-permute-start.1 = (f32[4,768]{1,0:T(4,128)S(1)}, f32[4,768]{1,0:T(4,128)S(1)}, u32[]{:S(2)}, u32[]{:S(2)}) collective-permute-start(f32[4,768]{1,0:T(4,128)S(1)} %get-tuple-element.12), channel_id=1, source_target_pairs={{0,8},{1,9},{4,5},{5,4},{8,0},{9,1},{12,13},{13,12},{2,10},{3,11},... | collective-permute-start | bytes 36872 | tf_op jit(solution)/shard_map/ppermute | solution.py:279
  7.3 1.1 %collective-permute-start.2 = (f32[4,768]{1,0:T(4,128)S(1)}, f32[4,768]{1,0:T(4,128)S(1)}, u32[]{:S(2)}, u32[]{:S(2)}) collective-permute-start(f32[4,768]{1,0:T(4,128)S(1)} %get-tuple-element.13), channel_id=1, source_target_pairs={{0,12},{1,13},{4,0},{5,1},{8,9},{9,8},{12,4},{13,5},{2,14},{3,15},... | collective-permute-start | bytes 36872 | tf_op jit(solution)/shard_map/ppermute | solution.py:279
  8.4 0.2 collective-permute-start.3
  8.5 0.3 %collective-permute-start.4 = (f32[4,768]{1,0:T(4,128)S(1)}, f32[4,768]{1,0:T(4,128)S(1)}, u32[]{:S(2)}, u32[]{:S(2)}) collective-permute-start(f32[4,768]{1,0:T(4,128)S(1)} %get-tuple-element.15), channel_id=1, source_target_pairs={{0,1},{1,0},{4,5},{5,4},{8,12},{9,13},{12,8},{13,9},{2,3},{3,2},{6... | collective-permute-start | bytes 36872 | tf_op jit(solution)/shard_map/ppermute | solution.py:279
  8.9 0.0 copy-done.1
  8.9 1.0 %collective-permute-done.refs_1_ = f32[4,768]{1,0:T(4,128)S(1)} collective-permute-done((f32[4,768]{1,0:T(4,128)S(1)}, f32[4,768]{1,0:T(4,128)S(1)}, u32[]{:S(2)}, u32[]{:S(2)}) %collective-permute-start) | collective-permute-done | bytes 12320 | tf_op jit(solution)/shard_map/ppermute | solution.py:279
  9.9 0.9 %collective-permute-done.1.refs_2_ = f32[4,768]{1,0:T(4,128)S(1)} collective-permute-done((f32[4,768]{1,0:T(4,128)S(1)}, f32[4,768]{1,0:T(4,128)S(1)}, u32[]{:S(2)}, u32[]{:S(2)}) %collective-permute-start.1) | collective-permute-done | bytes 12320 | tf_op jit(solution)/shard_map/ppermute | solution.py:279
  10.8 0.2 %collective-permute-done.2.refs_3_ = f32[4,768]{1,0:T(4,128)S(1)} collective-permute-done((f32[4,768]{1,0:T(4,128)S(1)}, f32[4,768]{1,0:T(4,128)S(1)}, u32[]{:S(2)}, u32[]{:S(2)}) %collective-permute-start.2) | collective-permute-done | bytes 12320 | tf_op jit(solution)/shard_map/ppermute | solution.py:279
  11.0 0.0 collective-permute-done.3.refs_4_
  11.0 0.0 collective-permute-done.4.refs_5_
  11.0 0.0 copy-done
  11.0 0.7 %project.1 = (f32[4,768]{1,0:T(4,128)S(1)}, f32[4,4,768]{2,1,0:T(4,128)S(1)}) custom-call(f32[4,768]{1,0:T(4,128)S(1)} %get-tuple-element.10.refs_0_, f32[4,768]{1,0:T(4,128)S(1)} %collective-permute-done.refs_1_, f32[4,768]{1,0:T(4,128)S(1)} %collective-permute-done.1.refs_2_, f32[4,768]{1,0:T(4,128)S(1)} %collective-permute-done.2.refs_3_, ...), custom_call_target="tpu_custom_call" | custom-call | tf_op jit(solution)/shard_map/project/pallas_call | solution.py:177
  11.7 0.4 %collective-permute-start.5 = (f32[4,4,768]{2,1,0:T(4,128)S(1)}, f32[4,4,768]{2,1,0:T(4,128)S(1)}, u32[]{:S(2)}, u32[]{:S(2)}) collective-permute-start(f32[4,4,768]{2,1,0:T(4,128)S(1)} %get-tuple-element.17.own_ref), channel_id=1, source_target_pairs={{3,0},{2,1},{1,2},{0,3},{7,4},{6,5},{5,6},{4,7},{11,8},{10,9},{9,1... | collective-permute-start | bytes 147464 | tf_op jit(solution)/shard_map/ppermute | solution.py:289
  12.1 1.2 %collective-permute-start.6 = (f32[4,4,768]{2,1,0:T(4,128)S(1)}, f32[4,4,768]{2,1,0:T(4,128)S(1)}, u32[]{:S(2)}, u32[]{:S(2)}) collective-permute-start(f32[4,4,768]{2,1,0:T(4,128)S(1)} %get-tuple-element.17.own_ref), channel_id=1, source_target_pairs={{2,0},{3,1},{0,2},{1,3},{6,4},{7,5},{4,6},{5,7},{10,8},{11,9},{8,1... | collective-permute-start | bytes 147464 | tf_op jit(solution)/shard_map/ppermute | solution.py:289
  13.3 0.3 %collective-permute-start.7 = (f32[4,4,768]{2,1,0:T(4,128)S(1)}, f32[4,4,768]{2,1,0:T(4,128)S(1)}, u32[]{:S(2)}, u32[]{:S(2)}) collective-permute-start(f32[4,4,768]{2,1,0:T(4,128)S(1)} %get-tuple-element.17.own_ref), channel_id=1, source_target_pairs={{1,0},{0,1},{3,2},{2,3},{5,4},{4,5},{7,6},{6,7},{9,8},{8,9},{11,10... | collective-permute-start | bytes 147464 | tf_op jit(solution)/shard_map/ppermute | solution.py:289
  13.6 1.3 %turn.1.beam = bf16[2,768,1536]{2,1,0:T(8,128)(2,1)S(1)} custom-call(bf16[2,4,2,192,768]{4,3,2,1,0:T(8,128)(2,1)S(1)} %copy-done), custom_call_target="tpu_custom_call" | custom-call | flops 1000000000 | bytes 10000000 | tf_op jit(solution)/shard_map/turn/pallas_call | solution.py:219
  14.9 0.7 %arrange.1 = f32[2,4,2,192]{3,2,1,0:T(2,128)} custom-call(f32[4,768]{1,0:T(4,128)S(1)} %get-tuple-element.16.total_ref), custom_call_target="tpu_custom_call" | custom-call | tf_op jit(solution)/shard_map/arrange/pallas_call | solution.py:199
  15.6 0.2 collective-permute-done.5.cross_ref
  15.7 0.9 %collective-permute-done.6.next_ref = f32[4,4,768]{2,1,0:T(4,128)S(1)} collective-permute-done((f32[4,4,768]{2,1,0:T(4,128)S(1)}, f32[4,4,768]{2,1,0:T(4,128)S(1)}, u32[]{:S(2)}, u32[]{:S(2)}) %collective-permute-start.6) | collective-permute-done | bytes 49184 | tf_op jit(solution)/shard_map/ppermute | solution.py:289
  16.7 0.0 collective-permute-done.7.pol_ref
  16.7 1.4 %couple.1 = f32[2,4,2,192]{3,2,1,0:T(2,128)} custom-call(f32[4,4,768]{2,1,0:T(4,128)S(1)} %get-tuple-element.17.own_ref, f32[4,4,768]{2,1,0:T(4,128)S(1)} %collective-permute-done.5.cross_ref, f32[4,4,768]{2,1,0:T(4,128)S(1)} %collective-permute-done.6.next_ref, f32[4,4,768]{2,1,0:T(4,128)S(1)} %collective-permute-done.7.pol_ref, ...), custom_call_target="tpu_custom_call" | custom-call | tf_op jit(solution)/shard_map/couple/pallas_call | solution.py:257
  (2 shorter events, 0.1 us)
Async XLA Ops:
  3.1 5.8 %copy-start.1 = (f32[4,5,768]{2,0,1:T(4,128)S(1)}, f32[4,5,768]{2,0,1:T(4,128)}, u32[]{:S(2)}) copy-start(f32[4,5,768]{2,0,1:T(4,128)} %param.6) | copy-start | bytes 184324
  3.1 7.9 %copy-start = (bf16[2,4,2,192,768]{4,3,2,1,0:T(8,128)(2,1)S(1)}, bf16[2,4,2,192,768]{4,3,2,1,0:T(8,128)(2,1)}, u32[]{:S(2)}) copy-start(bf16[2,4,2,192,768]{4,3,2,1,0:T(8,128)(2,1)} %beam.1) | copy-start | bytes 14155780
  3.1 6.8 %collective-permute-start = (f32[4,768]{1,0:T(4,128)S(1)}, f32[4,768]{1,0:T(4,128)S(1)}, u32[]{:S(2)}, u32[]{:S(2)}) collective-permute-start(f32[4,768]{1,0:T(4,128)S(1)} %get-tuple-element.11), channel_id=1, source_target_pairs={{0,4},{1,5},{4,12},{5,13},{8,9},{9,8},{12,0},{13,1},{2,6},{3,7},{6... | collective-permute-start | bytes 36872 | tf_op jit(solution)/shard_map/ppermute | solution.py:279
  6.2 4.6 %collective-permute-start.1 = (f32[4,768]{1,0:T(4,128)S(1)}, f32[4,768]{1,0:T(4,128)S(1)}, u32[]{:S(2)}, u32[]{:S(2)}) collective-permute-start(f32[4,768]{1,0:T(4,128)S(1)} %get-tuple-element.12), channel_id=1, source_target_pairs={{0,8},{1,9},{4,5},{5,4},{8,0},{9,1},{12,13},{13,12},{2,10},{3,11},... | collective-permute-start | bytes 36872 | tf_op jit(solution)/shard_map/ppermute | solution.py:279
  7.3 3.7 %collective-permute-start.2 = (f32[4,768]{1,0:T(4,128)S(1)}, f32[4,768]{1,0:T(4,128)S(1)}, u32[]{:S(2)}, u32[]{:S(2)}) collective-permute-start(f32[4,768]{1,0:T(4,128)S(1)} %get-tuple-element.13), channel_id=1, source_target_pairs={{0,12},{1,13},{4,0},{5,1},{8,9},{9,8},{12,4},{13,5},{2,14},{3,15},... | collective-permute-start | bytes 36872 | tf_op jit(solution)/shard_map/ppermute | solution.py:279
  8.4 2.6 %collective-permute-start.3 = (f32[4,768]{1,0:T(4,128)S(1)}, f32[4,768]{1,0:T(4,128)S(1)}, u32[]{:S(2)}, u32[]{:S(2)}) collective-permute-start(f32[4,768]{1,0:T(4,128)S(1)} %get-tuple-element.14), channel_id=1, source_target_pairs={{0,1},{1,0},{4,8},{5,9},{8,4},{9,5},{12,13},{13,12},{2,3},{3,2},{6... | collective-permute-start | bytes 36872 | tf_op jit(solution)/shard_map/ppermute | solution.py:279
  8.5 2.5 %collective-permute-start.4 = (f32[4,768]{1,0:T(4,128)S(1)}, f32[4,768]{1,0:T(4,128)S(1)}, u32[]{:S(2)}, u32[]{:S(2)}) collective-permute-start(f32[4,768]{1,0:T(4,128)S(1)} %get-tuple-element.15), channel_id=1, source_target_pairs={{0,1},{1,0},{4,5},{5,4},{8,12},{9,13},{12,8},{13,9},{2,3},{3,2},{6... | collective-permute-start | bytes 36872 | tf_op jit(solution)/shard_map/ppermute | solution.py:279
  11.7 4.1 %collective-permute-start.5 = (f32[4,4,768]{2,1,0:T(4,128)S(1)}, f32[4,4,768]{2,1,0:T(4,128)S(1)}, u32[]{:S(2)}, u32[]{:S(2)}) collective-permute-start(f32[4,4,768]{2,1,0:T(4,128)S(1)} %get-tuple-element.17.own_ref), channel_id=1, source_target_pairs={{3,0},{2,1},{1,2},{0,3},{7,4},{6,5},{5,6},{4,7},{11,8},{10,9},{9,1... | collective-permute-start | bytes 147464 | tf_op jit(solution)/shard_map/ppermute | solution.py:289
  12.1 4.6 %collective-permute-start.6 = (f32[4,4,768]{2,1,0:T(4,128)S(1)}, f32[4,4,768]{2,1,0:T(4,128)S(1)}, u32[]{:S(2)}, u32[]{:S(2)}) collective-permute-start(f32[4,4,768]{2,1,0:T(4,128)S(1)} %get-tuple-element.17.own_ref), channel_id=1, source_target_pairs={{2,0},{3,1},{0,2},{1,3},{6,4},{7,5},{4,6},{5,7},{10,8},{11,9},{8,1... | collective-permute-start | bytes 147464 | tf_op jit(solution)/shard_map/ppermute | solution.py:289
  13.3 3.3 %collective-permute-start.7 = (f32[4,4,768]{2,1,0:T(4,128)S(1)}, f32[4,4,768]{2,1,0:T(4,128)S(1)}, u32[]{:S(2)}, u32[]{:S(2)}) collective-permute-start(f32[4,4,768]{2,1,0:T(4,128)S(1)} %get-tuple-element.17.own_ref), channel_id=1, source_target_pairs={{1,0},{0,1},{3,2},{2,3},{5,4},{4,5},{7,6},{6,7},{9,8},{8,9},{11,10... | collective-permute-start | bytes 147464 | tf_op jit(solution)/shard_map/ppermute | solution.py:289

commit v7 on v6

--- a/solution.py
+++ b/solution.py
@@ -60,19 +60,15 @@
     def kernel(orders_ref, vis, *rest):
         out, held, orders, sems, order_sem = rest
         copies = [
-            [
-                pltpu.make_async_copy(
-                    vis.at[c, pl.ds(n * width, width)], held.at[c, n], sems.at[c, n]
-                )
-                for c in range(2)
-            ]
+            pltpu.make_async_copy(
+                vis.at[:, pl.ds(n * width, width)], held.at[:, n], sems.at[n]
+            )
             for n in range(chunks)
         ]
         fetch = pltpu.make_async_copy(orders_ref, orders, order_sem)
         fetch.start()
-        for pair in copies:
-            for copy in pair:
-                copy.start()
+        for copy in copies:
+            copy.start()
         fetch.wait()
         me = lax.axis_index("wide")
         row = lax.broadcasted_iota(jnp.int32, (total, times), 0)
@@ -88,8 +84,7 @@
             lefts.append(jnp.concatenate([high, low], 0))
         sums = []
         for n in range(chunks):
-            for copy in copies[n]:
-                copy.wait()
+            copies[n].wait()
             acc, small = None, None
             for c in range(2):
                 high, low = split(held[c, n])
@@ -114,7 +109,7 @@
         scratch_shapes=[
             pltpu.VMEM((2, chunks, width, times), jnp.float32),
             pltpu.SMEM((total,), jnp.int32),
-            pltpu.SemaphoreType.DMA((2, chunks)),
+            pltpu.SemaphoreType.DMA((chunks,)),
             pltpu.SemaphoreType.DMA,
         ],
         compiler_params=pltpu.CompilerParams(vmem_limit_bytes=12 * MIB),

time: 18.2 us -> 18.2 us (level)
  no operation moved by 1% of the time
where the time goes in v7:
time: 18.2 us; the launch traced here: 18.1 us
  starting transfers between devices  7.67 us (42%)
  Pallas kernels  6.51 us (36%)
  waiting for transfers between devices  3.18 us (17%)
  between operations  0.68 us (4%)
    ppermute x5, starting transfers between devices, shards(): lax.ppermute(part, ('wide', 'pol'), pairs_of(step, pols))  5.74 us
    pallas_call x1, Pallas kernels, transform(): pl.pallas_call(kernel, out_shape=jax.ShapeDtypeStruct((size, 2 * per, poi...  2.44 us
    ppermute x5, waiting for transfers between devices, shards(): lax.ppermute(part, ('wide', 'pol'), pairs_of(step, pols))  2.09 us
    ppermute x3, starting transfers between devices, fetch(): return lax.ppermute(partial, ('freq', 'pol'), pairs)  1.93 us
    pallas_call x1, Pallas kernels, couple(): pl.pallas_call(kernel, out_shape=jax.ShapeDtypeStruct((per, blocks, 2, mo...  1.43 us
    pallas_call x1, Pallas kernels, turn(): pl.pallas_call(kernel, out_shape=jax.ShapeDtypeStruct((2, degrees, blocks...  1.26 us
    ppermute x3, waiting for transfers between devices, fetch(): return lax.ppermute(partial, ('freq', 'pol'), pairs)  1.1 us
    pallas_call x1, Pallas kernels, arrange(): pl.pallas_call(kernel, out_shape=jax.ShapeDtypeStruct((per, blocks, 2, mo...  0.68 us
  transfers between devices with their start and end apart: 8, of which 5 were waited for; matrix products, arithmetic and copies ran while one was open for 0% of the time, Pallas kernels for 11%

profile of v7, /device:TPU:0, one launch (start us, length us, event | category | flops | bytes accessed | tf_op | source)
XLA Modules:
  0.0 18.1 jit_solution(7199189502614116229)
XLA Ops:
  0.6 2.4 %transform.1.sums_ref = f32[4,4,768]{2,1,0:T(4,128)S(1)} custom-call(s32[8]{0:T(128)} %orders_ref.1, f32[2,768,512]{2,1,0:T(8,128)} %bitcast.3), custom_call_target="tpu_custom_call" | custom-call | flops 4000000000 | bytes 8000000 | tf_op jit(solution)/shard_map/transform/pallas_call | solution.py:104
  3.1 0.0 copy-start.1
  3.1 0.0 copy-start
  3.1 3.1 %collective-permute-start = (f32[4,768]{1,0:T(4,128)S(1)}, f32[4,768]{1,0:T(4,128)S(1)}, u32[]{:S(2)}, u32[]{:S(2)}) collective-permute-start(f32[4,768]{1,0:T(4,128)S(1)} %get-tuple-element.11), channel_id=1, source_target_pairs={{0,4},{1,5},{4,12},{5,13},{8,9},{9,8},{12,0},{13,1},{2,6},{3,7},{6... | collective-permute-start | bytes 36872 | tf_op jit(solution)/shard_map/ppermute | solution.py:274
  6.2 1.1 %collective-permute-start.1 = (f32[4,768]{1,0:T(4,128)S(1)}, f32[4,768]{1,0:T(4,128)S(1)}, u32[]{:S(2)}, u32[]{:S(2)}) collective-permute-start(f32[4,768]{1,0:T(4,128)S(1)} %get-tuple-element.12), channel_id=1, source_target_pairs={{0,8},{1,9},{4,5},{5,4},{8,0},{9,1},{12,13},{13,12},{2,10},{3,11},... | collective-permute-start | bytes 36872 | tf_op jit(solution)/shard_map/ppermute | solution.py:274
  7.3 1.1 %collective-permute-start.2 = (f32[4,768]{1,0:T(4,128)S(1)}, f32[4,768]{1,0:T(4,128)S(1)}, u32[]{:S(2)}, u32[]{:S(2)}) collective-permute-start(f32[4,768]{1,0:T(4,128)S(1)} %get-tuple-element.13), channel_id=1, source_target_pairs={{0,12},{1,13},{4,0},{5,1},{8,9},{9,8},{12,4},{13,5},{2,14},{3,15},... | collective-permute-start | bytes 36872 | tf_op jit(solution)/shard_map/ppermute | solution.py:274
  8.4 0.2 collective-permute-start.3
  8.5 0.3 %collective-permute-start.4 = (f32[4,768]{1,0:T(4,128)S(1)}, f32[4,768]{1,0:T(4,128)S(1)}, u32[]{:S(2)}, u32[]{:S(2)}) collective-permute-start(f32[4,768]{1,0:T(4,128)S(1)} %get-tuple-element.15), channel_id=1, source_target_pairs={{0,1},{1,0},{4,5},{5,4},{8,12},{9,13},{12,8},{13,9},{2,3},{3,2},{6... | collective-permute-start | bytes 36872 | tf_op jit(solution)/shard_map/ppermute | solution.py:274
  8.9 0.0 copy-done.1
  8.9 1.0 %collective-permute-done.refs_1_ = f32[4,768]{1,0:T(4,128)S(1)} collective-permute-done((f32[4,768]{1,0:T(4,128)S(1)}, f32[4,768]{1,0:T(4,128)S(1)}, u32[]{:S(2)}, u32[]{:S(2)}) %collective-permute-start) | collective-permute-done | bytes 12320 | tf_op jit(solution)/shard_map/ppermute | solution.py:274
  9.9 0.9 %collective-permute-done.1.refs_2_ = f32[4,768]{1,0:T(4,128)S(1)} collective-permute-done((f32[4,768]{1,0:T(4,128)S(1)}, f32[4,768]{1,0:T(4,128)S(1)}, u32[]{:S(2)}, u32[]{:S(2)}) %collective-permute-start.1) | collective-permute-done | bytes 12320 | tf_op jit(solution)/shard_map/ppermute | solution.py:274
  10.8 0.2 %collective-permute-done.2.refs_3_ = f32[4,768]{1,0:T(4,128)S(1)} collective-permute-done((f32[4,768]{1,0:T(4,128)S(1)}, f32[4,768]{1,0:T(4,128)S(1)}, u32[]{:S(2)}, u32[]{:S(2)}) %collective-permute-start.2) | collective-permute-done | bytes 12320 | tf_op jit(solution)/shard_map/ppermute | solution.py:274
  11.0 0.0 collective-permute-done.3.refs_4_
  11.0 0.0 collective-permute-done.4.refs_5_
  11.0 0.0 copy-done
  11.0 0.7 %project.1 = (f32[4,768]{1,0:T(4,128)S(1)}, f32[4,4,768]{2,1,0:T(4,128)S(1)}) custom-call(f32[4,768]{1,0:T(4,128)S(1)} %get-tuple-element.10.refs_0_, f32[4,768]{1,0:T(4,128)S(1)} %collective-permute-done.refs_1_, f32[4,768]{1,0:T(4,128)S(1)} %collective-permute-done.1.refs_2_, f32[4,768]{1,0:T(4,128)S(1)} %collective-permute-done.2.refs_3_, ...), custom_call_target="tpu_custom_call" | custom-call | tf_op jit(solution)/shard_map/project/pallas_call | solution.py:172
  11.7 0.4 %collective-permute-start.5 = (f32[4,4,768]{2,1,0:T(4,128)S(1)}, f32[4,4,768]{2,1,0:T(4,128)S(1)}, u32[]{:S(2)}, u32[]{:S(2)}) collective-permute-start(f32[4,4,768]{2,1,0:T(4,128)S(1)} %get-tuple-element.17.own_ref), channel_id=1, source_target_pairs={{3,0},{2,1},{1,2},{0,3},{7,4},{6,5},{5,6},{4,7},{11,8},{10,9},{9,1... | collective-permute-start | bytes 147464 | tf_op jit(solution)/shard_map/ppermute | solution.py:284
  12.1 1.2 %collective-permute-start.6 = (f32[4,4,768]{2,1,0:T(4,128)S(1)}, f32[4,4,768]{2,1,0:T(4,128)S(1)}, u32[]{:S(2)}, u32[]{:S(2)}) collective-permute-start(f32[4,4,768]{2,1,0:T(4,128)S(1)} %get-tuple-element.17.own_ref), channel_id=1, source_target_pairs={{2,0},{3,1},{0,2},{1,3},{6,4},{7,5},{4,6},{5,7},{10,8},{11,9},{8,1... | collective-permute-start | bytes 147464 | tf_op jit(solution)/shard_map/ppermute | solution.py:284
  13.3 0.3 %collective-permute-start.7 = (f32[4,4,768]{2,1,0:T(4,128)S(1)}, f32[4,4,768]{2,1,0:T(4,128)S(1)}, u32[]{:S(2)}, u32[]{:S(2)}) collective-permute-start(f32[4,4,768]{2,1,0:T(4,128)S(1)} %get-tuple-element.17.own_ref), channel_id=1, source_target_pairs={{1,0},{0,1},{3,2},{2,3},{5,4},{4,5},{7,6},{6,7},{9,8},{8,9},{11,10... | collective-permute-start | bytes 147464 | tf_op jit(solution)/shard_map/ppermute | solution.py:284
  13.6 1.3 %turn.1.beam = bf16[2,768,1536]{2,1,0:T(8,128)(2,1)S(1)} custom-call(bf16[2,4,2,192,768]{4,3,2,1,0:T(8,128)(2,1)S(1)} %copy-done), custom_call_target="tpu_custom_call" | custom-call | flops 1000000000 | bytes 10000000 | tf_op jit(solution)/shard_map/turn/pallas_call | solution.py:214
  14.9 0.7 %arrange.1 = f32[2,4,2,192]{3,2,1,0:T(2,128)} custom-call(f32[4,768]{1,0:T(4,128)S(1)} %get-tuple-element.16.total_ref), custom_call_target="tpu_custom_call" | custom-call | tf_op jit(solution)/shard_map/arrange/pallas_call | solution.py:194
  15.6 0.2 collective-permute-done.5.cross_ref
  15.7 0.9 %collective-permute-done.6.next_ref = f32[4,4,768]{2,1,0:T(4,128)S(1)} collective-permute-done((f32[4,4,768]{2,1,0:T(4,128)S(1)}, f32[4,4,768]{2,1,0:T(4,128)S(1)}, u32[]{:S(2)}, u32[]{:S(2)}) %collective-permute-start.6) | collective-permute-done | bytes 49184 | tf_op jit(solution)/shard_map/ppermute | solution.py:284
  16.7 0.0 collective-permute-done.7.pol_ref
  16.7 1.4 %couple.1 = f32[2,4,2,192]{3,2,1,0:T(2,128)} custom-call(f32[4,4,768]{2,1,0:T(4,128)S(1)} %get-tuple-element.17.own_ref, f32[4,4,768]{2,1,0:T(4,128)S(1)} %collective-permute-done.5.cross_ref, f32[4,4,768]{2,1,0:T(4,128)S(1)} %collective-permute-done.6.next_ref, f32[4,4,768]{2,1,0:T(4,128)S(1)} %collective-permute-done.7.pol_ref, ...), custom_call_target="tpu_custom_call" | custom-call | tf_op jit(solution)/shard_map/couple/pallas_call | solution.py:252
  (2 shorter events, 0.1 us)
Async XLA Ops:
  3.1 5.8 %copy-start.1 = (f32[4,5,768]{2,0,1:T(4,128)S(1)}, f32[4,5,768]{2,0,1:T(4,128)}, u32[]{:S(2)}) copy-start(f32[4,5,768]{2,0,1:T(4,128)} %param.6) | copy-start | bytes 184324
  3.1 7.9 %copy-start = (bf16[2,4,2,192,768]{4,3,2,1,0:T(8,128)(2,1)S(1)}, bf16[2,4,2,192,768]{4,3,2,1,0:T(8,128)(2,1)}, u32[]{:S(2)}) copy-start(bf16[2,4,2,192,768]{4,3,2,1,0:T(8,128)(2,1)} %beam.1) | copy-start | bytes 14155780
  3.1 6.8 %collective-permute-start = (f32[4,768]{1,0:T(4,128)S(1)}, f32[4,768]{1,0:T(4,128)S(1)}, u32[]{:S(2)}, u32[]{:S(2)}) collective-permute-start(f32[4,768]{1,0:T(4,128)S(1)} %get-tuple-element.11), channel_id=1, source_target_pairs={{0,4},{1,5},{4,12},{5,13},{8,9},{9,8},{12,0},{13,1},{2,6},{3,7},{6... | collective-permute-start | bytes 36872 | tf_op jit(solution)/shard_map/ppermute | solution.py:274
  6.2 4.6 %collective-permute-start.1 = (f32[4,768]{1,0:T(4,128)S(1)}, f32[4,768]{1,0:T(4,128)S(1)}, u32[]{:S(2)}, u32[]{:S(2)}) collective-permute-start(f32[4,768]{1,0:T(4,128)S(1)} %get-tuple-element.12), channel_id=1, source_target_pairs={{0,8},{1,9},{4,5},{5,4},{8,0},{9,1},{12,13},{13,12},{2,10},{3,11},... | collective-permute-start | bytes 36872 | tf_op jit(solution)/shard_map/ppermute | solution.py:274
  7.3 3.7 %collective-permute-start.2 = (f32[4,768]{1,0:T(4,128)S(1)}, f32[4,768]{1,0:T(4,128)S(1)}, u32[]{:S(2)}, u32[]{:S(2)}) collective-permute-start(f32[4,768]{1,0:T(4,128)S(1)} %get-tuple-element.13), channel_id=1, source_target_pairs={{0,12},{1,13},{4,0},{5,1},{8,9},{9,8},{12,4},{13,5},{2,14},{3,15},... | collective-permute-start | bytes 36872 | tf_op jit(solution)/shard_map/ppermute | solution.py:274
  8.4 2.6 %collective-permute-start.3 = (f32[4,768]{1,0:T(4,128)S(1)}, f32[4,768]{1,0:T(4,128)S(1)}, u32[]{:S(2)}, u32[]{:S(2)}) collective-permute-start(f32[4,768]{1,0:T(4,128)S(1)} %get-tuple-element.14), channel_id=1, source_target_pairs={{0,1},{1,0},{4,8},{5,9},{8,4},{9,5},{12,13},{13,12},{2,3},{3,2},{6... | collective-permute-start | bytes 36872 | tf_op jit(solution)/shard_map/ppermute | solution.py:274
  8.5 2.5 %collective-permute-start.4 = (f32[4,768]{1,0:T(4,128)S(1)}, f32[4,768]{1,0:T(4,128)S(1)}, u32[]{:S(2)}, u32[]{:S(2)}) collective-permute-start(f32[4,768]{1,0:T(4,128)S(1)} %get-tuple-element.15), channel_id=1, source_target_pairs={{0,1},{1,0},{4,5},{5,4},{8,12},{9,13},{12,8},{13,9},{2,3},{3,2},{6... | collective-permute-start | bytes 36872 | tf_op jit(solution)/shard_map/ppermute | solution.py:274
  11.7 4.1 %collective-permute-start.5 = (f32[4,4,768]{2,1,0:T(4,128)S(1)}, f32[4,4,768]{2,1,0:T(4,128)S(1)}, u32[]{:S(2)}, u32[]{:S(2)}) collective-permute-start(f32[4,4,768]{2,1,0:T(4,128)S(1)} %get-tuple-element.17.own_ref), channel_id=1, source_target_pairs={{3,0},{2,1},{1,2},{0,3},{7,4},{6,5},{5,6},{4,7},{11,8},{10,9},{9,1... | collective-permute-start | bytes 147464 | tf_op jit(solution)/shard_map/ppermute | solution.py:284
  12.1 4.6 %collective-permute-start.6 = (f32[4,4,768]{2,1,0:T(4,128)S(1)}, f32[4,4,768]{2,1,0:T(4,128)S(1)}, u32[]{:S(2)}, u32[]{:S(2)}) collective-permute-start(f32[4,4,768]{2,1,0:T(4,128)S(1)} %get-tuple-element.17.own_ref), channel_id=1, source_target_pairs={{2,0},{3,1},{0,2},{1,3},{6,4},{7,5},{4,6},{5,7},{10,8},{11,9},{8,1... | collective-permute-start | bytes 147464 | tf_op jit(solution)/shard_map/ppermute | solution.py:284
  13.3 3.3 %collective-permute-start.7 = (f32[4,4,768]{2,1,0:T(4,128)S(1)}, f32[4,4,768]{2,1,0:T(4,128)S(1)}, u32[]{:S(2)}, u32[]{:S(2)}) collective-permute-start(f32[4,4,768]{2,1,0:T(4,128)S(1)} %get-tuple-element.17.own_ref), channel_id=1, source_target_pairs={{1,0},{0,1},{3,2},{2,3},{5,4},{4,5},{7,6},{6,7},{9,8},{8,9},{11,10... | collective-permute-start | bytes 147464 | tf_op jit(solution)/shard_map/ppermute | solution.py:284

commit v8 on v6

--- a/solution.py
+++ b/solution.py
@@ -69,8 +69,10 @@
             for n in range(chunks)
         ]
         fetch = pltpu.make_async_copy(orders_ref, orders, order_sem)
+        for copy in copies[0]:
+            copy.start()
         fetch.start()
-        for pair in copies:
+        for pair in copies[1:]:
             for copy in pair:
                 copy.start()
         fetch.wait()

time: 18.2 us -> 18.2 us (level)
  no operation moved by 1% of the time
where the time goes in v8:
time: 18.2 us; the launch traced here: 18.1 us
  starting transfers between devices  7.67 us (42%)
  Pallas kernels  6.52 us (36%)
  waiting for transfers between devices  3.18 us (17%)
  between operations  0.68 us (4%)
    ppermute x5, starting transfers between devices, shards(): lax.ppermute(part, ('wide', 'pol'), pairs_of(step, pols))  5.74 us
    pallas_call x1, Pallas kernels, transform(): pl.pallas_call(kernel, out_shape=jax.ShapeDtypeStruct((size, 2 * per, poi...  2.44 us
    ppermute x5, waiting for transfers between devices, shards(): lax.ppermute(part, ('wide', 'pol'), pairs_of(step, pols))  2.09 us
    ppermute x3, starting transfers between devices, fetch(): return lax.ppermute(partial, ('freq', 'pol'), pairs)  1.93 us
    pallas_call x1, Pallas kernels, couple(): pl.pallas_call(kernel, out_shape=jax.ShapeDtypeStruct((per, blocks, 2, mo...  1.43 us
    pallas_call x1, Pallas kernels, turn(): pl.pallas_call(kernel, out_shape=jax.ShapeDtypeStruct((2, degrees, blocks...  1.26 us
    ppermute x3, waiting for transfers between devices, fetch(): return lax.ppermute(partial, ('freq', 'pol'), pairs)  1.1 us
    pallas_call x1, Pallas kernels, arrange(): pl.pallas_call(kernel, out_shape=jax.ShapeDtypeStruct((per, blocks, 2, mo...  0.68 us
  transfers between devices with their start and end apart: 8, of which 5 were waited for; matrix products, arithmetic and copies ran while one was open for 0% of the time, Pallas kernels for 11%

profile of v8, /device:TPU:0, one launch (start us, length us, event | category | flops | bytes accessed | tf_op | source)
XLA Modules:
  0.0 18.1 jit_solution(13449373300088465261)
XLA Ops:
  0.6 2.4 %transform.1.sums_ref = f32[4,4,768]{2,1,0:T(4,128)S(1)} custom-call(s32[8]{0:T(128)} %orders_ref.1, f32[2,768,512]{2,1,0:T(8,128)} %bitcast.3), custom_call_target="tpu_custom_call" | custom-call | flops 4000000000 | bytes 8000000 | tf_op jit(solution)/shard_map/transform/pallas_call | solution.py:111
  3.1 0.0 copy-start.1
  3.1 0.0 copy-start
  3.1 3.1 %collective-permute-start = (f32[4,768]{1,0:T(4,128)S(1)}, f32[4,768]{1,0:T(4,128)S(1)}, u32[]{:S(2)}, u32[]{:S(2)}) collective-permute-start(f32[4,768]{1,0:T(4,128)S(1)} %get-tuple-element.11), channel_id=1, source_target_pairs={{0,4},{1,5},{4,12},{5,13},{8,9},{9,8},{12,0},{13,1},{2,6},{3,7},{6... | collective-permute-start | bytes 36872 | tf_op jit(solution)/shard_map/ppermute | solution.py:281
  6.2 1.1 %collective-permute-start.1 = (f32[4,768]{1,0:T(4,128)S(1)}, f32[4,768]{1,0:T(4,128)S(1)}, u32[]{:S(2)}, u32[]{:S(2)}) collective-permute-start(f32[4,768]{1,0:T(4,128)S(1)} %get-tuple-element.12), channel_id=1, source_target_pairs={{0,8},{1,9},{4,5},{5,4},{8,0},{9,1},{12,13},{13,12},{2,10},{3,11},... | collective-permute-start | bytes 36872 | tf_op jit(solution)/shard_map/ppermute | solution.py:281
  7.3 1.1 %collective-permute-start.2 = (f32[4,768]{1,0:T(4,128)S(1)}, f32[4,768]{1,0:T(4,128)S(1)}, u32[]{:S(2)}, u32[]{:S(2)}) collective-permute-start(f32[4,768]{1,0:T(4,128)S(1)} %get-tuple-element.13), channel_id=1, source_target_pairs={{0,12},{1,13},{4,0},{5,1},{8,9},{9,8},{12,4},{13,5},{2,14},{3,15},... | collective-permute-start | bytes 36872 | tf_op jit(solution)/shard_map/ppermute | solution.py:281
  8.4 0.2 collective-permute-start.3
  8.5 0.3 %collective-permute-start.4 = (f32[4,768]{1,0:T(4,128)S(1)}, f32[4,768]{1,0:T(4,128)S(1)}, u32[]{:S(2)}, u32[]{:S(2)}) collective-permute-start(f32[4,768]{1,0:T(4,128)S(1)} %get-tuple-element.15), channel_id=1, source_target_pairs={{0,1},{1,0},{4,5},{5,4},{8,12},{9,13},{12,8},{13,9},{2,3},{3,2},{6... | collective-permute-start | bytes 36872 | tf_op jit(solution)/shard_map/ppermute | solution.py:281
  8.9 0.0 copy-done.1
  8.9 1.0 %collective-permute-done.refs_1_ = f32[4,768]{1,0:T(4,128)S(1)} collective-permute-done((f32[4,768]{1,0:T(4,128)S(1)}, f32[4,768]{1,0:T(4,128)S(1)}, u32[]{:S(2)}, u32[]{:S(2)}) %collective-permute-start) | collective-permute-done | bytes 12320 | tf_op jit(solution)/shard_map/ppermute | solution.py:281
  9.9 0.9 %collective-permute-done.1.refs_2_ = f32[4,768]{1,0:T(4,128)S(1)} collective-permute-done((f32[4,768]{1,0:T(4,128)S(1)}, f32[4,768]{1,0:T(4,128)S(1)}, u32[]{:S(2)}, u32[]{:S(2)}) %collective-permute-start.1) | collective-permute-done | bytes 12320 | tf_op jit(solution)/shard_map/ppermute | solution.py:281
  10.8 0.2 %collective-permute-done.2.refs_3_ = f32[4,768]{1,0:T(4,128)S(1)} collective-permute-done((f32[4,768]{1,0:T(4,128)S(1)}, f32[4,768]{1,0:T(4,128)S(1)}, u32[]{:S(2)}, u32[]{:S(2)}) %collective-permute-start.2) | collective-permute-done | bytes 12320 | tf_op jit(solution)/shard_map/ppermute | solution.py:281
  11.0 0.0 collective-permute-done.3.refs_4_
  11.0 0.0 collective-permute-done.4.refs_5_
  11.0 0.0 copy-done
  11.0 0.7 %project.1 = (f32[4,768]{1,0:T(4,128)S(1)}, f32[4,4,768]{2,1,0:T(4,128)S(1)}) custom-call(f32[4,768]{1,0:T(4,128)S(1)} %get-tuple-element.10.refs_0_, f32[4,768]{1,0:T(4,128)S(1)} %collective-permute-done.refs_1_, f32[4,768]{1,0:T(4,128)S(1)} %collective-permute-done.1.refs_2_, f32[4,768]{1,0:T(4,128)S(1)} %collective-permute-done.2.refs_3_, ...), custom_call_target="tpu_custom_call" | custom-call | tf_op jit(solution)/shard_map/project/pallas_call | solution.py:179
  11.7 0.4 %collective-permute-start.5 = (f32[4,4,768]{2,1,0:T(4,128)S(1)}, f32[4,4,768]{2,1,0:T(4,128)S(1)}, u32[]{:S(2)}, u32[]{:S(2)}) collective-permute-start(f32[4,4,768]{2,1,0:T(4,128)S(1)} %get-tuple-element.17.own_ref), channel_id=1, source_target_pairs={{3,0},{2,1},{1,2},{0,3},{7,4},{6,5},{5,6},{4,7},{11,8},{10,9},{9,1... | collective-permute-start | bytes 147464 | tf_op jit(solution)/shard_map/ppermute | solution.py:291
  12.1 1.2 %collective-permute-start.6 = (f32[4,4,768]{2,1,0:T(4,128)S(1)}, f32[4,4,768]{2,1,0:T(4,128)S(1)}, u32[]{:S(2)}, u32[]{:S(2)}) collective-permute-start(f32[4,4,768]{2,1,0:T(4,128)S(1)} %get-tuple-element.17.own_ref), channel_id=1, source_target_pairs={{2,0},{3,1},{0,2},{1,3},{6,4},{7,5},{4,6},{5,7},{10,8},{11,9},{8,1... | collective-permute-start | bytes 147464 | tf_op jit(solution)/shard_map/ppermute | solution.py:291
  13.3 0.3 %collective-permute-start.7 = (f32[4,4,768]{2,1,0:T(4,128)S(1)}, f32[4,4,768]{2,1,0:T(4,128)S(1)}, u32[]{:S(2)}, u32[]{:S(2)}) collective-permute-start(f32[4,4,768]{2,1,0:T(4,128)S(1)} %get-tuple-element.17.own_ref), channel_id=1, source_target_pairs={{1,0},{0,1},{3,2},{2,3},{5,4},{4,5},{7,6},{6,7},{9,8},{8,9},{11,10... | collective-permute-start | bytes 147464 | tf_op jit(solution)/shard_map/ppermute | solution.py:291
  13.6 1.3 %turn.1.beam = bf16[2,768,1536]{2,1,0:T(8,128)(2,1)S(1)} custom-call(bf16[2,4,2,192,768]{4,3,2,1,0:T(8,128)(2,1)S(1)} %copy-done), custom_call_target="tpu_custom_call" | custom-call | flops 1000000000 | bytes 10000000 | tf_op jit(solution)/shard_map/turn/pallas_call | solution.py:221
  14.9 0.7 %arrange.1 = f32[2,4,2,192]{3,2,1,0:T(2,128)} custom-call(f32[4,768]{1,0:T(4,128)S(1)} %get-tuple-element.16.total_ref), custom_call_target="tpu_custom_call" | custom-call | tf_op jit(solution)/shard_map/arrange/pallas_call | solution.py:201
  15.6 0.2 collective-permute-done.5.cross_ref
  15.7 0.9 %collective-permute-done.6.next_ref = f32[4,4,768]{2,1,0:T(4,128)S(1)} collective-permute-done((f32[4,4,768]{2,1,0:T(4,128)S(1)}, f32[4,4,768]{2,1,0:T(4,128)S(1)}, u32[]{:S(2)}, u32[]{:S(2)}) %collective-permute-start.6) | collective-permute-done | bytes 49184 | tf_op jit(solution)/shard_map/ppermute | solution.py:291
  16.7 0.0 collective-permute-done.7.pol_ref
  16.7 1.4 %couple.1 = f32[2,4,2,192]{3,2,1,0:T(2,128)} custom-call(f32[4,4,768]{2,1,0:T(4,128)S(1)} %get-tuple-element.17.own_ref, f32[4,4,768]{2,1,0:T(4,128)S(1)} %collective-permute-done.5.cross_ref, f32[4,4,768]{2,1,0:T(4,128)S(1)} %collective-permute-done.6.next_ref, f32[4,4,768]{2,1,0:T(4,128)S(1)} %collective-permute-done.7.pol_ref, ...), custom_call_target="tpu_custom_call" | custom-call | tf_op jit(solution)/shard_map/couple/pallas_call | solution.py:259
  (2 shorter events, 0.1 us)
Async XLA Ops:
  3.1 5.8 %copy-start.1 = (f32[4,5,768]{2,0,1:T(4,128)S(1)}, f32[4,5,768]{2,0,1:T(4,128)}, u32[]{:S(2)}) copy-start(f32[4,5,768]{2,0,1:T(4,128)} %param.6) | copy-start | bytes 184324
  3.1 7.9 %copy-start = (bf16[2,4,2,192,768]{4,3,2,1,0:T(8,128)(2,1)S(1)}, bf16[2,4,2,192,768]{4,3,2,1,0:T(8,128)(2,1)}, u32[]{:S(2)}) copy-start(bf16[2,4,2,192,768]{4,3,2,1,0:T(8,128)(2,1)} %beam.1) | copy-start | bytes 14155780
  3.1 6.8 %collective-permute-start = (f32[4,768]{1,0:T(4,128)S(1)}, f32[4,768]{1,0:T(4,128)S(1)}, u32[]{:S(2)}, u32[]{:S(2)}) collective-permute-start(f32[4,768]{1,0:T(4,128)S(1)} %get-tuple-element.11), channel_id=1, source_target_pairs={{0,4},{1,5},{4,12},{5,13},{8,9},{9,8},{12,0},{13,1},{2,6},{3,7},{6... | collective-permute-start | bytes 36872 | tf_op jit(solution)/shard_map/ppermute | solution.py:281
  6.2 4.6 %collective-permute-start.1 = (f32[4,768]{1,0:T(4,128)S(1)}, f32[4,768]{1,0:T(4,128)S(1)}, u32[]{:S(2)}, u32[]{:S(2)}) collective-permute-start(f32[4,768]{1,0:T(4,128)S(1)} %get-tuple-element.12), channel_id=1, source_target_pairs={{0,8},{1,9},{4,5},{5,4},{8,0},{9,1},{12,13},{13,12},{2,10},{3,11},... | collective-permute-start | bytes 36872 | tf_op jit(solution)/shard_map/ppermute | solution.py:281
  7.3 3.7 %collective-permute-start.2 = (f32[4,768]{1,0:T(4,128)S(1)}, f32[4,768]{1,0:T(4,128)S(1)}, u32[]{:S(2)}, u32[]{:S(2)}) collective-permute-start(f32[4,768]{1,0:T(4,128)S(1)} %get-tuple-element.13), channel_id=1, source_target_pairs={{0,12},{1,13},{4,0},{5,1},{8,9},{9,8},{12,4},{13,5},{2,14},{3,15},... | collective-permute-start | bytes 36872 | tf_op jit(solution)/shard_map/ppermute | solution.py:281
  8.4 2.6 %collective-permute-start.3 = (f32[4,768]{1,0:T(4,128)S(1)}, f32[4,768]{1,0:T(4,128)S(1)}, u32[]{:S(2)}, u32[]{:S(2)}) collective-permute-start(f32[4,768]{1,0:T(4,128)S(1)} %get-tuple-element.14), channel_id=1, source_target_pairs={{0,1},{1,0},{4,8},{5,9},{8,4},{9,5},{12,13},{13,12},{2,3},{3,2},{6... | collective-permute-start | bytes 36872 | tf_op jit(solution)/shard_map/ppermute | solution.py:281
  8.5 2.5 %collective-permute-start.4 = (f32[4,768]{1,0:T(4,128)S(1)}, f32[4,768]{1,0:T(4,128)S(1)}, u32[]{:S(2)}, u32[]{:S(2)}) collective-permute-start(f32[4,768]{1,0:T(4,128)S(1)} %get-tuple-element.15), channel_id=1, source_target_pairs={{0,1},{1,0},{4,5},{5,4},{8,12},{9,13},{12,8},{13,9},{2,3},{3,2},{6... | collective-permute-start | bytes 36872 | tf_op jit(solution)/shard_map/ppermute | solution.py:281
  11.7 4.1 %collective-permute-start.5 = (f32[4,4,768]{2,1,0:T(4,128)S(1)}, f32[4,4,768]{2,1,0:T(4,128)S(1)}, u32[]{:S(2)}, u32[]{:S(2)}) collective-permute-start(f32[4,4,768]{2,1,0:T(4,128)S(1)} %get-tuple-element.17.own_ref), channel_id=1, source_target_pairs={{3,0},{2,1},{1,2},{0,3},{7,4},{6,5},{5,6},{4,7},{11,8},{10,9},{9,1... | collective-permute-start | bytes 147464 | tf_op jit(solution)/shard_map/ppermute | solution.py:291
  12.1 4.6 %collective-permute-start.6 = (f32[4,4,768]{2,1,0:T(4,128)S(1)}, f32[4,4,768]{2,1,0:T(4,128)S(1)}, u32[]{:S(2)}, u32[]{:S(2)}) collective-permute-start(f32[4,4,768]{2,1,0:T(4,128)S(1)} %get-tuple-element.17.own_ref), channel_id=1, source_target_pairs={{2,0},{3,1},{0,2},{1,3},{6,4},{7,5},{4,6},{5,7},{10,8},{11,9},{8,1... | collective-permute-start | bytes 147464 | tf_op jit(solution)/shard_map/ppermute | solution.py:291
  13.3 3.3 %collective-permute-start.7 = (f32[4,4,768]{2,1,0:T(4,128)S(1)}, f32[4,4,768]{2,1,0:T(4,128)S(1)}, u32[]{:S(2)}, u32[]{:S(2)}) collective-permute-start(f32[4,4,768]{2,1,0:T(4,128)S(1)} %get-tuple-element.17.own_ref), channel_id=1, source_target_pairs={{1,0},{0,1},{3,2},{2,3},{5,4},{4,5},{7,6},{6,7},{9,8},{8,9},{11,10... | collective-permute-start | bytes 147464 | tf_op jit(solution)/shard_map/ppermute | solution.py:291

commit v9 on v6

--- a/solution.py
+++ b/solution.py
@@ -99,12 +99,12 @@
                 term = both[: 2 * total] + both[2 * total :]
                 acc = term if acc is None else acc + term
             sums.append((acc, small))
-        for n in range(chunks):
-            acc = sums[n][0] + sums[n][1].T
-            for s in range(size):
-                for c in range(2):
-                    first = c * total + s * per
-                    out[s, c * per : (c + 1) * per, pl.ds(n * width, width)] = acc[first : first + per]
+            for m in [n - 1] * (n > 0) + [n] * (n == chunks - 1):
+                acc = sums[m][0] + sums[m][1].T
+                for s in range(size):
+                    for c in range(2):
+                        first = c * total + s * per
+                        out[s, c * per : (c + 1) * per, pl.ds(m * width, width)] = acc[first : first + per]
 
     return pl.pallas_call(
         kernel,

time: 18.2 us -> 18.2 us (level)
  no operation moved by 1% of the time
where the time goes in v9:
time: 18.2 us; the launch traced here: 18.1 us
  starting transfers between devices  7.67 us (42%)
  Pallas kernels  6.52 us (36%)
  waiting for transfers between devices  3.18 us (17%)
  between operations  0.68 us (4%)
    ppermute x5, starting transfers between devices, shards(): lax.ppermute(part, ('wide', 'pol'), pairs_of(step, pols))  5.74 us
    pallas_call x1, Pallas kernels, transform(): pl.pallas_call(kernel, out_shape=jax.ShapeDtypeStruct((size, 2 * per, poi...  2.44 us
    ppermute x5, waiting for transfers between devices, shards(): lax.ppermute(part, ('wide', 'pol'), pairs_of(step, pols))  2.09 us
    ppermute x3, starting transfers between devices, fetch(): return lax.ppermute(partial, ('freq', 'pol'), pairs)  1.93 us
    pallas_call x1, Pallas kernels, couple(): pl.pallas_call(kernel, out_shape=jax.ShapeDtypeStruct((per, blocks, 2, mo...  1.43 us
    pallas_call x1, Pallas kernels, turn(): pl.pallas_call(kernel, out_shape=jax.ShapeDtypeStruct((2, degrees, blocks...  1.26 us
    ppermute x3, waiting for transfers between devices, fetch(): return lax.ppermute(partial, ('freq', 'pol'), pairs)  1.1 us
    pallas_call x1, Pallas kernels, arrange(): pl.pallas_call(kernel, out_shape=jax.ShapeDtypeStruct((per, blocks, 2, mo...  0.68 us
  transfers between devices with their start and end apart: 8, of which 5 were waited for; matrix products, arithmetic and copies ran while one was open for 0% of the time, Pallas kernels for 11%

profile of v9, /device:TPU:0, one launch (start us, length us, event | category | flops | bytes accessed | tf_op | source)
XLA Modules:
  0.0 18.1 jit_solution(8236035402793747928)
XLA Ops:
  0.6 2.4 %transform.1.sums_ref = f32[4,4,768]{2,1,0:T(4,128)S(1)} custom-call(s32[8]{0:T(128)} %orders_ref.1, f32[2,768,512]{2,1,0:T(8,128)} %bitcast.3), custom_call_target="tpu_custom_call" | custom-call | flops 4000000000 | bytes 8000000 | tf_op jit(solution)/shard_map/transform/pallas_call | solution.py:109
  3.1 0.0 copy-start.1
  3.1 0.0 copy-start
  3.1 3.1 %collective-permute-start = (f32[4,768]{1,0:T(4,128)S(1)}, f32[4,768]{1,0:T(4,128)S(1)}, u32[]{:S(2)}, u32[]{:S(2)}) collective-permute-start(f32[4,768]{1,0:T(4,128)S(1)} %get-tuple-element.11), channel_id=1, source_target_pairs={{0,4},{1,5},{4,12},{5,13},{8,9},{9,8},{12,0},{13,1},{2,6},{3,7},{6... | collective-permute-start | bytes 36872 | tf_op jit(solution)/shard_map/ppermute | solution.py:279
  6.2 1.1 %collective-permute-start.1 = (f32[4,768]{1,0:T(4,128)S(1)}, f32[4,768]{1,0:T(4,128)S(1)}, u32[]{:S(2)}, u32[]{:S(2)}) collective-permute-start(f32[4,768]{1,0:T(4,128)S(1)} %get-tuple-element.12), channel_id=1, source_target_pairs={{0,8},{1,9},{4,5},{5,4},{8,0},{9,1},{12,13},{13,12},{2,10},{3,11},... | collective-permute-start | bytes 36872 | tf_op jit(solution)/shard_map/ppermute | solution.py:279
  7.3 1.1 %collective-permute-start.2 = (f32[4,768]{1,0:T(4,128)S(1)}, f32[4,768]{1,0:T(4,128)S(1)}, u32[]{:S(2)}, u32[]{:S(2)}) collective-permute-start(f32[4,768]{1,0:T(4,128)S(1)} %get-tuple-element.13), channel_id=1, source_target_pairs={{0,12},{1,13},{4,0},{5,1},{8,9},{9,8},{12,4},{13,5},{2,14},{3,15},... | collective-permute-start | bytes 36872 | tf_op jit(solution)/shard_map/ppermute | solution.py:279
  8.4 0.2 collective-permute-start.3
  8.5 0.3 %collective-permute-start.4 = (f32[4,768]{1,0:T(4,128)S(1)}, f32[4,768]{1,0:T(4,128)S(1)}, u32[]{:S(2)}, u32[]{:S(2)}) collective-permute-start(f32[4,768]{1,0:T(4,128)S(1)} %get-tuple-element.15), channel_id=1, source_target_pairs={{0,1},{1,0},{4,5},{5,4},{8,12},{9,13},{12,8},{13,9},{2,3},{3,2},{6... | collective-permute-start | bytes 36872 | tf_op jit(solution)/shard_map/ppermute | solution.py:279
  8.9 0.0 copy-done.1
  8.9 1.0 %collective-permute-done.refs_1_ = f32[4,768]{1,0:T(4,128)S(1)} collective-permute-done((f32[4,768]{1,0:T(4,128)S(1)}, f32[4,768]{1,0:T(4,128)S(1)}, u32[]{:S(2)}, u32[]{:S(2)}) %collective-permute-start) | collective-permute-done | bytes 12320 | tf_op jit(solution)/shard_map/ppermute | solution.py:279
  9.9 0.9 %collective-permute-done.1.refs_2_ = f32[4,768]{1,0:T(4,128)S(1)} collective-permute-done((f32[4,768]{1,0:T(4,128)S(1)}, f32[4,768]{1,0:T(4,128)S(1)}, u32[]{:S(2)}, u32[]{:S(2)}) %collective-permute-start.1) | collective-permute-done | bytes 12320 | tf_op jit(solution)/shard_map/ppermute | solution.py:279
  10.8 0.2 %collective-permute-done.2.refs_3_ = f32[4,768]{1,0:T(4,128)S(1)} collective-permute-done((f32[4,768]{1,0:T(4,128)S(1)}, f32[4,768]{1,0:T(4,128)S(1)}, u32[]{:S(2)}, u32[]{:S(2)}) %collective-permute-start.2) | collective-permute-done | bytes 12320 | tf_op jit(solution)/shard_map/ppermute | solution.py:279
  11.0 0.0 collective-permute-done.3.refs_4_
  11.0 0.0 collective-permute-done.4.refs_5_
  11.0 0.0 copy-done
  11.0 0.7 %project.1 = (f32[4,768]{1,0:T(4,128)S(1)}, f32[4,4,768]{2,1,0:T(4,128)S(1)}) custom-call(f32[4,768]{1,0:T(4,128)S(1)} %get-tuple-element.10.refs_0_, f32[4,768]{1,0:T(4,128)S(1)} %collective-permute-done.refs_1_, f32[4,768]{1,0:T(4,128)S(1)} %collective-permute-done.1.refs_2_, f32[4,768]{1,0:T(4,128)S(1)} %collective-permute-done.2.refs_3_, ...), custom_call_target="tpu_custom_call" | custom-call | tf_op jit(solution)/shard_map/project/pallas_call | solution.py:177
  11.7 0.4 %collective-permute-start.5 = (f32[4,4,768]{2,1,0:T(4,128)S(1)}, f32[4,4,768]{2,1,0:T(4,128)S(1)}, u32[]{:S(2)}, u32[]{:S(2)}) collective-permute-start(f32[4,4,768]{2,1,0:T(4,128)S(1)} %get-tuple-element.17.own_ref), channel_id=1, source_target_pairs={{3,0},{2,1},{1,2},{0,3},{7,4},{6,5},{5,6},{4,7},{11,8},{10,9},{9,1... | collective-permute-start | bytes 147464 | tf_op jit(solution)/shard_map/ppermute | solution.py:289
  12.1 1.2 %collective-permute-start.6 = (f32[4,4,768]{2,1,0:T(4,128)S(1)}, f32[4,4,768]{2,1,0:T(4,128)S(1)}, u32[]{:S(2)}, u32[]{:S(2)}) collective-permute-start(f32[4,4,768]{2,1,0:T(4,128)S(1)} %get-tuple-element.17.own_ref), channel_id=1, source_target_pairs={{2,0},{3,1},{0,2},{1,3},{6,4},{7,5},{4,6},{5,7},{10,8},{11,9},{8,1... | collective-permute-start | bytes 147464 | tf_op jit(solution)/shard_map/ppermute | solution.py:289
  13.3 0.3 %collective-permute-start.7 = (f32[4,4,768]{2,1,0:T(4,128)S(1)}, f32[4,4,768]{2,1,0:T(4,128)S(1)}, u32[]{:S(2)}, u32[]{:S(2)}) collective-permute-start(f32[4,4,768]{2,1,0:T(4,128)S(1)} %get-tuple-element.17.own_ref), channel_id=1, source_target_pairs={{1,0},{0,1},{3,2},{2,3},{5,4},{4,5},{7,6},{6,7},{9,8},{8,9},{11,10... | collective-permute-start | bytes 147464 | tf_op jit(solution)/shard_map/ppermute | solution.py:289
  13.6 1.3 %turn.1.beam = bf16[2,768,1536]{2,1,0:T(8,128)(2,1)S(1)} custom-call(bf16[2,4,2,192,768]{4,3,2,1,0:T(8,128)(2,1)S(1)} %copy-done), custom_call_target="tpu_custom_call" | custom-call | flops 1000000000 | bytes 10000000 | tf_op jit(solution)/shard_map/turn/pallas_call | solution.py:219
  14.9 0.7 %arrange.1 = f32[2,4,2,192]{3,2,1,0:T(2,128)} custom-call(f32[4,768]{1,0:T(4,128)S(1)} %get-tuple-element.16.total_ref), custom_call_target="tpu_custom_call" | custom-call | tf_op jit(solution)/shard_map/arrange/pallas_call | solution.py:199
  15.6 0.2 collective-permute-done.5.cross_ref
  15.7 0.9 %collective-permute-done.6.next_ref = f32[4,4,768]{2,1,0:T(4,128)S(1)} collective-permute-done((f32[4,4,768]{2,1,0:T(4,128)S(1)}, f32[4,4,768]{2,1,0:T(4,128)S(1)}, u32[]{:S(2)}, u32[]{:S(2)}) %collective-permute-start.6) | collective-permute-done | bytes 49184 | tf_op jit(solution)/shard_map/ppermute | solution.py:289
  16.7 0.0 collective-permute-done.7.pol_ref
  16.7 1.4 %couple.1 = f32[2,4,2,192]{3,2,1,0:T(2,128)} custom-call(f32[4,4,768]{2,1,0:T(4,128)S(1)} %get-tuple-element.17.own_ref, f32[4,4,768]{2,1,0:T(4,128)S(1)} %collective-permute-done.5.cross_ref, f32[4,4,768]{2,1,0:T(4,128)S(1)} %collective-permute-done.6.next_ref, f32[4,4,768]{2,1,0:T(4,128)S(1)} %collective-permute-done.7.pol_ref, ...), custom_call_target="tpu_custom_call" | custom-call | tf_op jit(solution)/shard_map/couple/pallas_call | solution.py:257
  (2 shorter events, 0.1 us)
Async XLA Ops:
  3.1 5.8 %copy-start.1 = (f32[4,5,768]{2,0,1:T(4,128)S(1)}, f32[4,5,768]{2,0,1:T(4,128)}, u32[]{:S(2)}) copy-start(f32[4,5,768]{2,0,1:T(4,128)} %param.6) | copy-start | bytes 184324
  3.1 7.9 %copy-start = (bf16[2,4,2,192,768]{4,3,2,1,0:T(8,128)(2,1)S(1)}, bf16[2,4,2,192,768]{4,3,2,1,0:T(8,128)(2,1)}, u32[]{:S(2)}) copy-start(bf16[2,4,2,192,768]{4,3,2,1,0:T(8,128)(2,1)} %beam.1) | copy-start | bytes 14155780
  3.1 6.8 %collective-permute-start = (f32[4,768]{1,0:T(4,128)S(1)}, f32[4,768]{1,0:T(4,128)S(1)}, u32[]{:S(2)}, u32[]{:S(2)}) collective-permute-start(f32[4,768]{1,0:T(4,128)S(1)} %get-tuple-element.11), channel_id=1, source_target_pairs={{0,4},{1,5},{4,12},{5,13},{8,9},{9,8},{12,0},{13,1},{2,6},{3,7},{6... | collective-permute-start | bytes 36872 | tf_op jit(solution)/shard_map/ppermute | solution.py:279
  6.2 4.6 %collective-permute-start.1 = (f32[4,768]{1,0:T(4,128)S(1)}, f32[4,768]{1,0:T(4,128)S(1)}, u32[]{:S(2)}, u32[]{:S(2)}) collective-permute-start(f32[4,768]{1,0:T(4,128)S(1)} %get-tuple-element.12), channel_id=1, source_target_pairs={{0,8},{1,9},{4,5},{5,4},{8,0},{9,1},{12,13},{13,12},{2,10},{3,11},... | collective-permute-start | bytes 36872 | tf_op jit(solution)/shard_map/ppermute | solution.py:279
  7.3 3.7 %collective-permute-start.2 = (f32[4,768]{1,0:T(4,128)S(1)}, f32[4,768]{1,0:T(4,128)S(1)}, u32[]{:S(2)}, u32[]{:S(2)}) collective-permute-start(f32[4,768]{1,0:T(4,128)S(1)} %get-tuple-element.13), channel_id=1, source_target_pairs={{0,12},{1,13},{4,0},{5,1},{8,9},{9,8},{12,4},{13,5},{2,14},{3,15},... | collective-permute-start | bytes 36872 | tf_op jit(solution)/shard_map/ppermute | solution.py:279
  8.4 2.6 %collective-permute-start.3 = (f32[4,768]{1,0:T(4,128)S(1)}, f32[4,768]{1,0:T(4,128)S(1)}, u32[]{:S(2)}, u32[]{:S(2)}) collective-permute-start(f32[4,768]{1,0:T(4,128)S(1)} %get-tuple-element.14), channel_id=1, source_target_pairs={{0,1},{1,0},{4,8},{5,9},{8,4},{9,5},{12,13},{13,12},{2,3},{3,2},{6... | collective-permute-start | bytes 36872 | tf_op jit(solution)/shard_map/ppermute | solution.py:279
  8.5 2.5 %collective-permute-start.4 = (f32[4,768]{1,0:T(4,128)S(1)}, f32[4,768]{1,0:T(4,128)S(1)}, u32[]{:S(2)}, u32[]{:S(2)}) collective-permute-start(f32[4,768]{1,0:T(4,128)S(1)} %get-tuple-element.15), channel_id=1, source_target_pairs={{0,1},{1,0},{4,5},{5,4},{8,12},{9,13},{12,8},{13,9},{2,3},{3,2},{6... | collective-permute-start | bytes 36872 | tf_op jit(solution)/shard_map/ppermute | solution.py:279
  11.7 4.1 %collective-permute-start.5 = (f32[4,4,768]{2,1,0:T(4,128)S(1)}, f32[4,4,768]{2,1,0:T(4,128)S(1)}, u32[]{:S(2)}, u32[]{:S(2)}) collective-permute-start(f32[4,4,768]{2,1,0:T(4,128)S(1)} %get-tuple-element.17.own_ref), channel_id=1, source_target_pairs={{3,0},{2,1},{1,2},{0,3},{7,4},{6,5},{5,6},{4,7},{11,8},{10,9},{9,1... | collective-permute-start | bytes 147464 | tf_op jit(solution)/shard_map/ppermute | solution.py:289
  12.1 4.6 %collective-permute-start.6 = (f32[4,4,768]{2,1,0:T(4,128)S(1)}, f32[4,4,768]{2,1,0:T(4,128)S(1)}, u32[]{:S(2)}, u32[]{:S(2)}) collective-permute-start(f32[4,4,768]{2,1,0:T(4,128)S(1)} %get-tuple-element.17.own_ref), channel_id=1, source_target_pairs={{2,0},{3,1},{0,2},{1,3},{6,4},{7,5},{4,6},{5,7},{10,8},{11,9},{8,1... | collective-permute-start | bytes 147464 | tf_op jit(solution)/shard_map/ppermute | solution.py:289
  13.3 3.3 %collective-permute-start.7 = (f32[4,4,768]{2,1,0:T(4,128)S(1)}, f32[4,4,768]{2,1,0:T(4,128)S(1)}, u32[]{:S(2)}, u32[]{:S(2)}) collective-permute-start(f32[4,4,768]{2,1,0:T(4,128)S(1)} %get-tuple-element.17.own_ref), channel_id=1, source_target_pairs={{1,0},{0,1},{3,2},{2,3},{5,4},{4,5},{7,6},{6,7},{9,8},{8,9},{11,10... | collective-permute-start | bytes 147464 | tf_op jit(solution)/shard_map/ppermute | solution.py:289
